TPU v7x, 32 devices: a whole 2x2x4 slice. The times are simulated.
32 devices in a mesh: tile: 4 (over y, x), blk: 8 (over z, core).
Axes of the slice: x: 2, y: 2, z: 4, core: 2. Of those that a mesh axis runs over, the one named last changes fastest.
Arguments:
- tiles: bfloat16 [1536, 8, 8, 2048], P(('blk', 'tile')), may hold values from -10 to 10
- w_reduce: bfloat16 [2048, 512], replicated, may hold values from -0.125 to 0.125
- w_spatial: bfloat16 [9, 512, 512], replicated, may hold values from -0.09375 to 0.09375
- w_expand: bfloat16 [512, 2048], replicated, may hold values from -0.25 to 0.25
- w_embed: bfloat16 [2048, 1536], replicated, may hold values from -0.125 to 0.125
- w_query: bfloat16 [1536, 1536], P(None, 'tile'), may hold values from -8 to 8
- w_key: bfloat16 [1536, 1536], P(None, 'tile'), may hold values from -200 to 200
- w_value: bfloat16 [1536, 1536], P(None, 'tile'), may hold values from -0.15625 to 0.15625
- w_out: bfloat16 [1536, 1536], P('tile'), may hold values from -0.15625 to 0.15625
- slide_tiles: int32 [4], replicated, may hold values from 1 to 1152, 1536 in all
Outputs:
- mixed: bfloat16 [1536, 1536], P(('blk', 'tile'))
Inputs may be any that keep to these rules, and one draw needn't show every extreme that they name: `slide_tiles`: the counts sum to 1536 and the largest is exactly 1152.
All inputs are finite; a program needn't handle non-finite values.
Results may differ from a plain program's by a relative error of at most 0.017.
Values may be sent and summed in bfloat16 or wider, within the bound.
No kernel may reach another device: no remote copies, remote signals or barrier semaphores. Data moves between devices by JAX's collectives and lax.ppermute only.
A program may use at most 256 MiB of HBM per device.

v0:
```python
import math

import jax
import jax.numpy as jnp
from jax import lax
from jax.sharding import PartitionSpec as P

C = 2048
MID = 512
SIDE = 8
HD = 96


def encode(block, w_reduce, w_spatial, w_expand, w_embed):
    count = block.shape[0]
    flat = block.reshape(count * SIDE * SIDE, C)
    reduced = jax.nn.relu(jnp.dot(flat, w_reduce, preferred_element_type=jnp.float32)).astype(
        jnp.bfloat16
    )
    reduced = reduced.reshape(count, SIDE, SIDE, MID)
    padded = jnp.pad(reduced, ((0, 0), (1, 1), (1, 1), (0, 0)))
    summed = jnp.zeros((count * SIDE * SIDE, MID), jnp.float32)
    for tap in range(9):
        row_off = tap // 3
        col_off = tap % 3
        window = padded[:, row_off : row_off + SIDE, col_off : col_off + SIDE, :].reshape(
            count * SIDE * SIDE, MID
        )
        summed = summed + jnp.dot(window, w_spatial[tap], preferred_element_type=jnp.float32)
    spatial = jax.nn.relu(summed).astype(jnp.bfloat16)
    output = jax.nn.relu(
        flat.astype(jnp.float32) + jnp.dot(spatial, w_expand, preferred_element_type=jnp.float32)
    )
    pooled = (jnp.sum(output.reshape(count, SIDE * SIDE, C), axis=1) / (SIDE * SIDE)).astype(
        jnp.bfloat16
    )
    return jnp.dot(pooled, w_embed, preferred_element_type=jnp.float32).astype(jnp.bfloat16)


def normalize(rows):
    values = rows.astype(jnp.float32)
    center = jnp.mean(values, axis=1, keepdims=True)
    spread = jnp.mean((values - center) ** 2, axis=1, keepdims=True)
    return ((values - center) * lax.rsqrt(spread + 1e-05)).astype(jnp.bfloat16)


def slide_of(positions, slide_tiles):
    ends = jnp.cumsum(slide_tiles)[:-1]
    return jnp.sum((positions[:, None] >= ends[None, :]).astype(jnp.int32), axis=1)


def shards(
    tiles, w_reduce, w_spatial, w_expand, w_embed, w_query, w_key, w_value, w_out, slide_tiles
):
    emb = encode(tiles, w_reduce, w_spatial, w_expand, w_embed)
    width = w_query.shape[1]
    heads_here = width // HD
    w_joined = jnp.concatenate([w_query, w_key, w_value], axis=1)
    joined = jnp.dot(
        normalize(lax.all_gather(emb, "tile", axis=0, tiled=True)),
        w_joined,
        preferred_element_type=jnp.float32,
    ).astype(jnp.bfloat16)
    length = joined.shape[0]
    query = joined[:, :width].reshape(length, heads_here, HD)
    key_value = joined[:, width:]
    query_pos = lax.axis_index("blk") * length + jnp.arange(length, dtype=jnp.int32)
    query_slide = slide_of(query_pos, slide_tiles)
    scale = 1.0 / math.sqrt(HD)
    piece = lax.all_gather(key_value, "blk", axis=0, tiled=True)
    rows = piece.shape[0]
    key_pos = jnp.arange(rows, dtype=jnp.int32)
    same = query_slide[:, None] == slide_of(key_pos, slide_tiles)[None, :]
    top_old = jnp.full((heads_here, length), -1e30, jnp.float32)
    keys = piece[:, :width].reshape(rows, heads_here, HD)
    values = piece[:, width:].reshape(rows, heads_here, HD)
    scores = jnp.einsum("qhd,khd->hqk", query, keys, preferred_element_type=jnp.float32) * scale
    scores = jnp.where(same[None], scores, -1e30)
    top_new = jnp.maximum(top_old, jnp.max(scores, axis=2))
    probs = jnp.where(same[None], jnp.exp(scores - top_new[:, :, None]), 0.0)
    total_new = jnp.sum(probs, axis=2)
    accum_new = jnp.einsum(
        "hqk,khd->hqd", probs.astype(jnp.bfloat16), values, preferred_element_type=jnp.float32
    )
    attended = (
        (accum_new / total_new[:, :, None])
        .transpose(1, 0, 2)
        .reshape(length, width)
        .astype(jnp.bfloat16)
    )
    summed = lax.psum_scatter(
        jnp.dot(attended, w_out, preferred_element_type=jnp.float32).astype(jnp.bfloat16),
        "tile",
        scatter_dimension=0,
        tiled=True,
    ).astype(jnp.float32)
    return (emb.astype(jnp.float32) + summed).astype(jnp.bfloat16)


def solution(mesh):
    placed = (
        P(("blk", "tile"), None, None, None),
        P(),
        P(),
        P(),
        P(),
        P(None, "tile"),
        P(None, "tile"),
        P(None, "tile"),
        P("tile", None),
        P(),
    )
    return jax.shard_map(
        shards, mesh=mesh, in_specs=placed, out_specs=P(("blk", "tile"), None), check_vma=False
    )
```

profile of v0, /device:TPU:0, one launch (start us, length us, event | category | flops | bytes accessed | tf_op | source)
XLA Modules:
  0.0 212.8 jit_solution(12164928790000753095)
XLA Ops:
  6.5 13.1 %maximum_convert_fusion.1 = bf16[3072,512]{1,0:T(8,128)(2,1)} fusion(bf16[3072,2048]{1,0:T(8,128)(2,1)} %bitcast.71, bf16[2048,512]{1,0:T(8,128)(2,1)} %param.11), kind=kOutput, calls=%fused_computation.10 | convolution fusion | flops 6445596672 | bytes 17825792 | tf_op jit(solution)/shard_map/dot_general | solution.py:17
  19.6 13.5 %pad_slice_fusion = (bf16[48,8,8,512]{3,2,1,0:T(8,128)(2,1)}, bf16[48,8,8,512]{3,2,1,0:T(8,128)(2,1)S(1)}, bf16[48,8,8,512]{3,2,1,0:T(8,128)(2,1)S(1)}, bf16[48,...) fusion(bf16[48,8,8,512]{3,2,1,0:T(8,128)(2,1)} %bitcast.81), kind=kLoop, calls=%fused_computation.1 | loop fusion | bytes 28311552 | tf_op jit(solution)/shard_map/slice | solution.py:26
  33.1 6.7 %fusion.40 = f32[3072,512]{1,0:T(8,128)} fusion(bf16[3072,512]{1,0:T(8,128)(2,1)} %maximum_convert_fusion.1, bf16[9,512,512]{2,1,0:T(8,128)(2,1)} %param.12), kind=kOutput, calls=%fused_computation.46 | convolution fusion | flops 1610612736 | bytes 9961472 | tf_op jit(solution)/shard_map/dot_general | solution.py:29
  39.8 4.5 %fusion.34 = f32[3072,512]{1,0:T(8,128)} fusion(bf16[3072,512]{1,0:T(8,128)(2,1)S(1)} %bitcast.80, bf16[9,512,512]{2,1,0:T(8,128)(2,1)S(1)} %copy-done.4), kind=kOutput, calls=%fused_computation.40 | convolution fusion | flops 1610612736 | bytes 9961472 | tf_op jit(solution)/shard_map/dot_general | solution.py:29
  44.3 4.5 %fusion.36 = f32[3072,512]{1,0:T(8,128)} fusion(bf16[3072,512]{1,0:T(8,128)(2,1)S(1)} %bitcast.79, bf16[9,512,512]{2,1,0:T(8,128)(2,1)S(1)} %copy-done.4), kind=kOutput, calls=%fused_computation.42 | convolution fusion | flops 1610612736 | bytes 9961472 | tf_op jit(solution)/shard_map/dot_general | solution.py:29
  48.8 4.4 %fusion.38 = f32[3072,512]{1,0:T(8,128)} fusion(bf16[3072,512]{1,0:T(8,128)(2,1)S(1)} %bitcast.78, bf16[9,512,512]{2,1,0:T(8,128)(2,1)S(1)} %copy-done.4), kind=kOutput, calls=%fused_computation.44 | convolution fusion | flops 1610612736 | bytes 9961472 | tf_op jit(solution)/shard_map/dot_general | solution.py:29
  53.2 4.4 %fusion.42 = f32[3072,512]{1,0:T(8,128)} fusion(bf16[3072,512]{1,0:T(8,128)(2,1)S(1)} %bitcast.77, bf16[9,512,512]{2,1,0:T(8,128)(2,1)S(1)} %copy-done.4), kind=kOutput, calls=%fused_computation.48 | convolution fusion | flops 1610612736 | bytes 9961472 | tf_op jit(solution)/shard_map/dot_general | solution.py:29
  57.7 4.5 %fusion.44 = f32[3072,512]{1,0:T(8,128)} fusion(bf16[3072,512]{1,0:T(8,128)(2,1)S(1)} %bitcast.76, bf16[9,512,512]{2,1,0:T(8,128)(2,1)S(1)} %copy-done.4), kind=kOutput, calls=%fused_computation.50 | convolution fusion | flops 1610612736 | bytes 9961472 | tf_op jit(solution)/shard_map/dot_general | solution.py:29
  62.1 4.4 %fusion.46 = f32[3072,512]{1,0:T(8,128)} fusion(bf16[3072,512]{1,0:T(8,128)(2,1)S(1)} %bitcast.75, bf16[9,512,512]{2,1,0:T(8,128)(2,1)S(1)} %copy-done.4), kind=kOutput, calls=%fused_computation.52 | convolution fusion | flops 1610612736 | bytes 9961472 | tf_op jit(solution)/shard_map/dot_general | solution.py:29
  66.5 4.5 %fusion.48 = f32[3072,512]{1,0:T(8,128)} fusion(bf16[3072,512]{1,0:T(8,128)(2,1)S(1)} %bitcast.74, bf16[9,512,512]{2,1,0:T(8,128)(2,1)S(1)} %copy-done.4), kind=kOutput, calls=%fused_computation.54 | convolution fusion | flops 1610612736 | bytes 9961472 | tf_op jit(solution)/shard_map/dot_general | solution.py:29
  71.0 33.0 %add_maximum_fusion = f32[3072,2048]{1,0:T(8,128)} fusion(bf16[3072,2048]{1,0:T(8,128)(2,1)} %bitcast.72, bf16[512,2048]{1,0:T(8,128)(2,1)S(1)} %copy-done, f32[3072,512]{1,0:T(8,128)} %fusion.34, f32[3072,512]{1,0:T(8,128)} %fusion.36, f32[3072,512]{1,0:T(8,128)} %fusion.38, f32[3072,512]{1,0:T(8,128)} %fusion.40, f32[3072,512]{1,0:T(8,128)} %fusion.42, ...), kind=kOutput, calls=%fused_computation | convolution fusion | flops 8087666688 | bytes 93847552 | tf_op jit(solution)/shard_map/dot_general | solution.py:32
  104.0 9.5 %reduce_sum.54 = f32[48,2048]{1,0:T(8,128)S(1)} reduce(f32[48,64,2048]{2,1,0:T(8,128)} %bitcast.70, f32[]{:T(128)} %constant.11.clone.1), dimensions={1}, to_apply=%region_0.1 | reduce | flops 6193152 | bytes 25559044 | tf_op jit(solution)/shard_map/reduce_sum | solution.py:34
  113.6 4.1 %convolution_convert_fusion.1 = bf16[48,1536]{1,0:T(8,128)(2,1)S(1)} fusion(bf16[2048,1536]{1,0:T(8,128)(2,1)} %param.14, f32[48,2048]{1,0:T(8,128)S(1)} %reduce_sum.54), kind=kOutput, calls=%fused_computation.26 | convolution fusion | flops 302260224 | bytes 6832128 | tf_op jit(solution)/shard_map/dot_general | solution.py:37
  117.6 11.8 %all_gather.6 = bf16[192,1536]{1,0:T(8,128)(2,1)S(1)} all-gather(bf16[48,1536]{1,0:T(8,128)(2,1)S(1)} %convolution_convert_fusion.1), channel_id=1, replica_groups=mesh['tile'=4,'blk'=8] {'tile'}, dimensions={0}, use_global_device_ids=true | all-gather | bytes 737280 | tf_op jit(solution)/shard_map/all_gather | solution.py:60
  129.9 1.0 fusion.9
  132.6 31.2 %all-gather.2.cloned.1.call-done = bf16[1536,768]{1,0:T(8,128)(2,1)} async-done(((bf16[192,768]{1,0:T(8,128)(2,1)}), bf16[1536,768]{1,0:T(8,128)(2,1)}) %all-gather.2.cloned.1.call-update) | async-done | bytes 2359312 | tf_op jit(solution)/shard_map/all_gather | solution.py:70
  163.8 2.9 %fusion.69 = (bf16[1536,384]{1,0:T(8,128)(2,1)}, bf16[1536,384]{1,0:T(8,128)(2,1)S(1)}) fusion(bf16[1536,768]{1,0:T(8,128)(2,1)} %all-gather.2.cloned.1.call-done), kind=kLoop, calls=%fused_computation.84 | loop fusion | bytes 4718592 | tf_op jit(solution)/shard_map/slice | solution.py:75
  166.7 1.6 copy.17
  168.2 3.2 %fusion = (f32[4,192]{1,0:T(4,128)S(1)}, f32[4,192,1536]{2,1,0:T(8,128)}) fusion(pred[192,1536]{1,0:T(8,128)(4,1)S(1)} %broadcast_compare_fusion, bf16[1536,4,96]{0,2,1:T(8,128)(2,1)S(1)} %bitcast.82, bf16[192,4,96]{2,1,0:T(4,128)(2,1)S(1)} %reshape.112), kind=kOutput, calls=%fused_computation.13 | convolution fusion | flops 230030592 | bytes 6343680 | tf_op jit(solution)/shard_map/qhd,khd->hqk/dot_general | solution.py:77
  172.1 4.0 %fusion.7 = f32[4,192]{1,0:T(4,128)S(1)} fusion(f32[4,192,1536]{2,1,0:T(8,128)} %get-tuple-element.16, f32[4,192]{1,0:T(4,128)S(1)} %broadcast_maximum_fusion, pred[192,1536]{1,0:T(8,128)(4,1)S(1)} %broadcast_compare_fusion), kind=kLoop, calls=%fused_computation.20 | loop fusion | flops 5897472 | bytes 5019648 | tf_op jit(solution)/shard_map/reduce_sum | solution.py:81
  176.1 2.5 %fusion.25 = bf16[192,4,96]{0,2,1:T(8,128)(2,1)S(1)} fusion(bf16[1536,4,96]{0,2,1:T(8,128)(2,1)S(1)} %bitcast.83, f32[4,192,1536]{2,1,0:T(8,128)S(1)} %copy-done.2, f32[4,192]{1,0:T(4,128)S(1)} %broadcast_maximum_fusion, pred[192,1536]{1,0:T(8,128)(4,1)} %copy-done.5, f32[192,4]{0,1:T(4,128)S(1)} %bitcast.85), kind=kOutput, calls=%fused_computation.35 | convolution fusion | flops 232538112 | bytes 6346752 | tf_op jit(solution)/shard_map/hqk,khd->hqd/dot_general | solution.py:82
  178.6 1.3 convolution_convert_fusion
  179.9 24.4 %reduce-scatter.2.cloned.1.call-done = bf16[48,1536]{1,0:T(8,128)(2,1)} async-done(((bf16[192,1536]{1,0:T(8,128)(2,1)}), bf16[48,1536]{1,0:T(8,128)(2,1)}) %reduce-scatter.2.cloned.1.call-update) | async-done | bytes 147472 | tf_op jit(solution)/shard_map/reduce_scatter | solution.py:91
  204.3 1.6 add_convert_fusion
  (41 shorter events, 2.8 us)
Async XLA Ops:
  6.5 64.5 %copy-start = (bf16[512,2048]{1,0:T(8,128)(2,1)S(1)}, bf16[512,2048]{1,0:T(8,128)(2,1)}, u32[]{:S(2)}) copy-start(bf16[512,2048]{1,0:T(8,128)(2,1)} %param.13) | copy-start | bytes 6291460
  6.5 157.2 %all-gather.2.cloned.1.call-start = ((), (), s32[]{:S(2)}) async-start(), calls=%async_computation.1 | async-start | bytes 2654208 | tf_op jit(solution)/shard_map/all_gather | solution.py:70
  33.1 6.7 %copy-start.3 = (bf16[48,8,8,512]{3,2,1,0:T(8,128)(2,1)S(1)}, bf16[48,8,8,512]{3,2,1,0:T(8,128)(2,1)}, u32[]{:S(2)}) copy-start(bf16[48,8,8,512]{3,2,1,0:T(8,128)(2,1)} %get-tuple-element.11) | copy-start | bytes 9437188
  33.1 6.7 %copy-start.4 = (bf16[9,512,512]{2,1,0:T(8,128)(2,1)S(1)}, bf16[9,512,512]{2,1,0:T(8,128)(2,1)}, u32[]{:S(2)}) copy-start(bf16[9,512,512]{2,1,0:T(8,128)(2,1)} %param.12) | copy-start | bytes 14155780
  113.5 16.4 %copy-start.7 = (bf16[1536,384]{1,0:T(8,128)(2,1)S(1)}, bf16[1536,384]{1,0:T(8,128)(2,1)}, u32[]{:S(2)}) copy-start(bf16[1536,384]{1,0:T(8,128)(2,1)} %param.17) | copy-start | bytes 3538948
  113.5 16.4 %copy-start.8 = (bf16[1536,384]{1,0:T(8,128)(2,1)S(1)}, bf16[1536,384]{1,0:T(8,128)(2,1)}, u32[]{:S(2)}) copy-start(bf16[1536,384]{1,0:T(8,128)(2,1)} %param.16) | copy-start | bytes 3538948
  113.6 16.3 %copy-start.9 = (bf16[1536,384]{1,0:T(8,128)(2,1)S(1)}, bf16[1536,384]{1,0:T(8,128)(2,1)}, u32[]{:S(2)}) copy-start(bf16[1536,384]{1,0:T(8,128)(2,1)} %param.15) | copy-start | bytes 3538948
  129.9 2.0 copy-start.10
  131.7 72.6 %reduce-scatter.2.cloned.1.call-start = ((), (), s32[]{:S(2)}) async-start(), calls=%async_computation.2 | async-start | bytes 737280 | tf_op jit(solution)/shard_map/reduce_scatter | solution.py:91
  132.6 39.5 %copy-start.5 = (pred[192,1536]{1,0:T(8,128)(4,1)}, pred[192,1536]{1,0:T(8,128)(4,1)S(1)}, u32[]{:S(2)}) copy-start(pred[192,1536]{1,0:T(8,128)(4,1)S(1)} %broadcast_compare_fusion) | copy-start | bytes 884740
  172.1 4.0 %copy-start.2 = (f32[4,192,1536]{2,1,0:T(8,128)S(1)}, f32[4,192,1536]{2,1,0:T(8,128)}, u32[]{:S(2)}) copy-start(f32[4,192,1536]{2,1,0:T(8,128)} %get-tuple-element.16) | copy-start | bytes 14155780
  176.0 29.9 %copy-start.1 = (bf16[512,2048]{1,0:T(8,128)(2,1)S(1)}, bf16[512,2048]{1,0:T(8,128)(2,1)}, u32[]{:S(2)}) copy-start(bf16[512,2048]{1,0:T(8,128)(2,1)} %param.13) | copy-start | bytes 6291460
  176.1 2.5 %copy-start.6 = (bf16[384,1536]{1,0:T(8,128)(2,1)S(1)}, bf16[384,1536]{1,0:T(8,128)(2,1)}, u32[]{:S(2)}) copy-start(bf16[384,1536]{1,0:T(8,128)(2,1)} %param.18) | copy-start | bytes 3538948
Sparse Core Ops, SparseCore 0:
  131.8 31.9 all-gather.1
  180.1 24.2 reduce-scatter.1
where the time goes:
time: 213 us
  matrix products  96 us (45%)
  waiting for transfers between devices  55.6 us (26%)
  local copies, waits for them, and re-layouts  19.5 us (9%)
  other arithmetic  16.2 us (8%)
  between operations  13.6 us (6%)
  blocking collectives  11.8 us (6%)
    dot_general x8, matrix products, encode(): jnp.dot(window, w_spatial[tap], preferred_element_type=jnp.float32)  37.8 us
    dot_general x1, matrix products, encode(): jnp.dot(spatial, w_expand, preferred_element_type=jnp.float32)  33 us
    all_gather x1, waiting for transfers between devices, shards(): piece = lax.all_gather(key_value, 'blk', axis=0, tiled=True)  31.2 us
    reduce_scatter x1, waiting for transfers between devices, shards(): lax.psum_scatter(jnp.dot(attended, w_out, preferred_element_type=jnp.floa...  24.4 us
    slice x1, local copies, waits for them, and re-layouts, encode(): padded[:, row_off:row_off + SIDE, col_off:col_off + SIDE, :]  13.5 us
    dot_general x1, matrix products, encode(): jnp.dot(flat, w_reduce, preferred_element_type=jnp.float32)  13.1 us
    all_gather x1, blocking collectives, shards(): lax.all_gather(emb, 'tile', axis=0, tiled=True)  11.8 us
    reduce_sum x1, other arithmetic, encode(): jnp.sum(output.reshape(count, SIDE * SIDE, C), axis=1) / (SIDE * SIDE)  9.51 us
  transfers between devices with their start and end apart: 2, of which 2 were waited for; matrix products, arithmetic and copies ran while one was open for 0% of the time, Pallas kernels for 0%

commit v1 on v0

v1 whole, which is shorter than its diff:
```python
import functools
import math

import jax
import jax.numpy as jnp
from jax import lax
from jax.experimental import pallas as pl
from jax.experimental.pallas import tpu as pltpu
from jax.sharding import PartitionSpec as P

SIDE = 8
HD = 96
LANES = 128
F32 = jnp.float32
BF16 = jnp.bfloat16
GROUP = 8


def dot(a, b):
    return jnp.dot(a, b, preferred_element_type=F32)


def neighbours(rows):
    col = lax.broadcasted_iota(jnp.int32, rows.shape, 1)
    left = jnp.where(col >= 1, pltpu.roll(rows, 1, axis=1), 0.0)
    right = jnp.where(col <= SIDE - 2, pltpu.roll(rows, SIDE - 1, axis=1), 0.0)
    return left, rows, right


def bottleneck(x, wr, ws, we, waits):
    total = x.shape[0]
    count = total // (SIDE * SIDE)
    mid = wr.shape[1]
    band = count * SIDE
    waits[0]()
    reduced = jnp.maximum(dot(x, wr[...]), 0.0)
    reduced = reduced.reshape(count, SIDE, SIDE, mid).swapaxes(0, 1).reshape(band, SIDE, mid)
    taps = jnp.concatenate([p.reshape(total, mid).astype(BF16) for p in neighbours(reduced)], axis=1)
    waits[1]()
    edge = jnp.zeros((band, mid), F32)
    summed = dot(taps, ws[1])
    summed = summed + jnp.concatenate([edge, dot(taps[:-band], ws[0])], axis=0)
    summed = summed + jnp.concatenate([dot(taps[band:], ws[2]), edge], axis=0)
    spatial = jnp.maximum(summed, 0.0).reshape(SIDE, count, SIDE, mid).swapaxes(0, 1)
    spatial = spatial.reshape(total, mid).astype(BF16)
    waits[2]()
    out = jnp.maximum(dot(spatial, we[...]) + x.astype(F32), 0.0)
    return jnp.sum(out.reshape(count, SIDE * SIDE, x.shape[1]), axis=1) * (1.0 / (SIDE * SIDE))


def encode_kernel(x, wr_hbm, ws_hbm, we_hbm, wm_hbm, emb, wr, ws, we, wm, pooled, sems):
    step = pl.program_id(0)
    last = pl.num_programs(0) - 1
    copies = [
        pltpu.make_async_copy(src, dst, sems.at[i])
        for i, (src, dst) in enumerate(((wr_hbm, wr), (ws_hbm, ws), (we_hbm, we), (wm_hbm, wm)))
    ]

    def run(waits):
        count = x.shape[0] // (SIDE * SIDE)
        value = bottleneck(x[...], wr, ws, we, waits)
        pooled[pl.ds(pl.multiple_of(step * count, count), count), :] = value

    @pl.when(step == 0)
    def _():
        for copy in copies:
            copy.start()
        run([copy.wait for copy in copies])

    @pl.when(step > 0)
    def _():
        run([lambda: None] * 3)

    @pl.when(step == last)
    def _():
        copies[3].wait()
        emb[...] = dot(pooled[...].astype(BF16), wm[...]).astype(BF16)


def encode(flat, wr, ws, we, wm):
    total, c = flat.shape
    count = total // (SIDE * SIDE)
    rows = GROUP * SIDE * SIDE
    anywhere = pl.BlockSpec(memory_space=pl.ANY)
    return pl.pallas_call(
        encode_kernel,
        grid=(count // GROUP,),
        in_specs=[pl.BlockSpec((rows, c), lambda i: (i, 0))] + [anywhere] * 4,
        out_specs=pl.BlockSpec((count, wm.shape[1]), lambda i: (0, 0)),
        out_shape=jax.ShapeDtypeStruct((count, wm.shape[1]), BF16),
        scratch_shapes=[
            pltpu.VMEM(wr.shape, BF16),
            pltpu.VMEM(ws.shape, BF16),
            pltpu.VMEM(we.shape, BF16),
            pltpu.VMEM(wm.shape, BF16),
            pltpu.VMEM((count, c), F32),
            pltpu.SemaphoreType.DMA((4,)),
        ],
        compiler_params=pltpu.CompilerParams(vmem_limit_bytes=56 << 20),
        name="encode",
    )(flat, wr, ws, we, wm)


def project_kernel(heads, spread_of, emb, wq, wk, wv, *outs):
    a = lax.axis_index("blk") // spread_of
    scratch = outs[-1]
    values = emb[...].astype(F32)
    center = jnp.mean(values, axis=1, keepdims=True)
    values = values - center
    spread = jnp.mean(values * values, axis=1, keepdims=True)
    normed = (values * lax.rsqrt(spread + 1e-05)).astype(BF16)
    scratch[...] = jnp.zeros_like(scratch)
    for part, w in enumerate((wq, wk, wv)):
        result = dot(normed, w[...]).astype(BF16)
        for head in range(heads):
            scratch[head, :, part * LANES : part * LANES + HD] = result[:, head * HD : (head + 1) * HD]
    for e in range(heads):
        outs[e][...] = scratch[a ^ e]


def project(emb, wq, wk, wv, heads, spread_of):
    rows = emb.shape[0]
    return pl.pallas_call(
        functools.partial(project_kernel, heads, spread_of),
        out_shape=[jax.ShapeDtypeStruct((rows, 3 * LANES), BF16)] * heads,
        scratch_shapes=[pltpu.VMEM((heads, rows, 3 * LANES), BF16)],
        compiler_params=pltpu.CompilerParams(vmem_limit_bytes=24 << 20),
        name="project",
    )(emb, wq, wk, wv)


def attend_kernel(heads, spread_of, tiles_of, slide_tiles, *refs):
    own = refs[:heads]
    others = refs[heads : heads + spread_of - 1]
    out, keys, values = refs[heads + spread_of - 1 :]
    blk = lax.axis_index("blk")
    a, c = blk // spread_of, lax.rem(blk, spread_of)
    length = own[0].shape[0]
    count = length // tiles_of
    ends = [slide_tiles[0], slide_tiles[0] + slide_tiles[1]]
    ends.append(ends[1] + slide_tiles[2])

    def slide_of(shape, dim, start):
        pos = lax.broadcasted_iota(jnp.int32, shape, dim) + start
        return sum((pos >= end).astype(jnp.int32) for end in ends)

    slides = []
    lane = lax.broadcasted_iota(jnp.int32, (length, LANES), 1)
    for f in range(spread_of):
        for e in range(heads):
            at = (f * heads + e) * length
            if f == 0:
                keys[at : at + length] = own[e][:, LANES : 2 * LANES]
                value = own[e][:, 2 * LANES :]
            else:
                keys[at : at + length] = others[f - 1][e * length : (e + 1) * length, :LANES]
                value = others[f - 1][e * length : (e + 1) * length, LANES:]
            values[at : at + length] = jnp.where(lane == HD, 1.0, value.astype(F32)).astype(BF16)
            slides.append(slide_of((1, length), 1, ((a ^ e) * spread_of + (c ^ f)) * length))
    key_slide = jnp.concatenate(slides, axis=1)
    scale = math.log2(math.e) / math.sqrt(HD)
    me = lax.axis_index("tile")
    for e in range(heads):
        query = own[e][:, :LANES]
        query_slide = slide_of((length, 1), 0, ((a ^ e) * spread_of + c) * length)
        scores = lax.dot_general(
            query, keys[...], (((1,), (1,)), ((), ())), preferred_element_type=F32
        )
        scores = jnp.where(query_slide == key_slide, scores, -1e30)
        top = jnp.max(scores, axis=1, keepdims=True)
        weights = jnp.exp2((scores - top) * scale).astype(BF16)
        product = dot(weights, values[...])
        result = (product / product[:, HD : HD + 1]).astype(BF16)
        for t in range(tiles_of):
            out[t * heads + (a ^ e)] = result[t * count : (t + 1) * count]


def attend(slide_tiles, own, others, heads, spread_of, tiles_of):
    length = own[0].shape[0]
    total = length * heads * spread_of
    whole = pl.BlockSpec(memory_space=pltpu.VMEM)
    return pl.pallas_call(
        functools.partial(attend_kernel, heads, spread_of, tiles_of),
        in_specs=[pl.BlockSpec(memory_space=pltpu.SMEM)] + [whole] * (heads + spread_of - 1),
        out_specs=whole,
        out_shape=jax.ShapeDtypeStruct((tiles_of * heads, length // tiles_of, LANES), BF16),
        scratch_shapes=[pltpu.VMEM((total, LANES), BF16), pltpu.VMEM((total, LANES), BF16)],
        compiler_params=pltpu.CompilerParams(vmem_limit_bytes=40 << 20),
        name="attend",
    )(slide_tiles, *own, *others)


def finish_kernel(parts, w_out, emb, out):
    attended = jnp.concatenate([parts[h][:, :HD].astype(F32) for h in range(parts.shape[0])], axis=1)
    out[...] = (emb[...].astype(F32) + dot(attended.astype(BF16), w_out[...])).astype(BF16)


def finish(parts, w_out, emb):
    return pl.pallas_call(
        finish_kernel,
        out_shape=jax.ShapeDtypeStruct(emb.shape, BF16),
        compiler_params=pltpu.CompilerParams(vmem_limit_bytes=24 << 20),
        name="finish",
    )(parts, w_out, emb)


def shards(tiles_of, blks, tiles, wr, ws, we, wm, wq, wk, wv, wo, slide_tiles):
    count = tiles.shape[0]
    flat = tiles.reshape(count * SIDE * SIDE, tiles.shape[3])
    mid = wr.shape[1]
    heads = wq.shape[1] // HD
    spread_of = blks // heads
    w_out = lax.all_gather(wo, "tile", axis=0, tiled=True)
    emb = encode(flat, wr, ws.reshape(3, 3 * mid, mid), we, wm)
    gathered = lax.all_gather(emb, "tile", axis=0, tiled=True)
    mine = project(gathered, wq, wk, wv, heads, spread_of)
    own = [mine[0]]
    for e in range(1, heads):
        pairs = [(i, i ^ (e * spread_of)) for i in range(blks)]
        own.append(lax.ppermute(mine[e], "blk", pairs))
    key_value = jnp.concatenate([piece[:, LANES:] for piece in own], axis=0)
    others = [
        lax.ppermute(key_value, "blk", [(i, i ^ f) for i in range(blks)]) for f in range(1, spread_of)
    ]
    attended = attend(slide_tiles, own, others, heads, spread_of, tiles_of)
    groups = [
        [t * blks + a * spread_of + c for t in range(tiles_of) for a in range(heads)]
        for c in range(spread_of)
    ]
    parts = lax.all_to_all(attended, ("tile", "blk"), 0, 0, axis_index_groups=groups, tiled=True)
    return finish(parts, w_out, emb)


def solution(mesh):
    placed = (
        P(("blk", "tile"), None, None, None),
        P(),
        P(),
        P(),
        P(),
        P(None, "tile"),
        P(None, "tile"),
        P(None, "tile"),
        P("tile", None),
        P(),
    )
    return jax.shard_map(
        functools.partial(shards, mesh.shape["tile"], mesh.shape["blk"]),
        mesh=mesh,
        in_specs=placed,
        out_specs=P(("blk", "tile"), None),
        check_vma=False,
    )
```

time: 213 us -> 108 us (0.51)
  matrix products: 96 us -> 0 us
  waiting for transfers between devices: 55.6 us -> 12.8 us
  Pallas kernels: 0 us -> 41.7 us
  blocking collectives: 11.8 us -> 33.1 us
  local copies, waits for them, and re-layouts: 19.5 us -> 2.39 us
  other arithmetic: 16.2 us -> 0.03 us
  starting transfers between devices: 0.04 us -> 4.53 us
    dot_general x15 -> x0, matrix products: 96 us -> none  [the longest x8 37.8 us: encode(): jnp.dot(window, w_spatial[tap], preferred_element_type=jnp.float32)]
    pallas_call x0 -> x4, Pallas kernels: none -> 41.7 us  [the longest x1 35.5 us: encode(): pl.pallas_call(encode_kernel, grid=(count // GROUP,), in_specs=[pl.BlockS...]
    all_gather x1, waiting for transfers between devices: 31.2 us -> 0.01 us  [shards(): w_out = lax.all_gather(wo, 'tile', axis=0, tiled=True)]
    reduce_scatter x1 -> x0, waiting for transfers between devices: 24.4 us -> none  [shards(): lax.psum_scatter(jnp.dot(attended, w_out, preferred_element_type=jnp.floa...]
    slice x6 -> x4, local copies, waits for them, and re-layouts: 19.3 us -> 0.03 us  [shards(): key_value = jnp.concatenate([piece[:, LANES:] for piece in own], axis=0)]
    all_to_all x0 -> x1, blocking collectives: none -> 14.7 us  [shards(): lax.all_to_all(attended, ('tile', 'blk'), 0, 0, axis_index_groups=groups,...]
    reduce_sum x6 -> x0, other arithmetic: 14.1 us -> none  [the longest x1 9.51 us: encode(): jnp.sum(output.reshape(count, SIDE * SIDE, C), axis=1) / (SIDE * SIDE)]
    ppermute x0 -> x4, waiting for transfers between devices: none -> 12.1 us  [the longest x3 10.4 us: shards(): own.append(lax.ppermute(mine[e], 'blk', pairs))]
  transfers between devices with their start and end apart: 2 -> 5, of which waited for: 2 -> 3; matrix products, arithmetic and copies ran while one was open for 0% -> 0% of each run, Pallas kernels for 0% -> 37%
where the time goes in v1:
time: 108 us
  Pallas kernels  41.7 us (39%)
  blocking collectives  33.1 us (31%)
  between operations  13.5 us (12%)
  waiting for transfers between devices  12.8 us (12%)
  starting transfers between devices  4.53 us (4%)
  local copies, waits for them, and re-layouts  2.39 us (2%)
    pallas_call x1, Pallas kernels, encode(): pl.pallas_call(encode_kernel, grid=(count // GROUP,), in_specs=[pl.BlockS...  35.5 us
    all_gather x1, blocking collectives, shards(): gathered = lax.all_gather(emb, 'tile', axis=0, tiled=True)  18.4 us
    all_to_all x1, blocking collectives, shards(): lax.all_to_all(attended, ('tile', 'blk'), 0, 0, axis_index_groups=groups,...  14.7 us
    ppermute x3, waiting for transfers between devices, shards(): own.append(lax.ppermute(mine[e], 'blk', pairs))  10.4 us
    ppermute x3, starting transfers between devices, shards(): own.append(lax.ppermute(mine[e], 'blk', pairs))  4.45 us
    pallas_call x1, Pallas kernels, attend(): pl.pallas_call(functools.partial(attend_kernel, heads, spread_of, tiles_o...  2.99 us
    unnamed x12, local copies, waits for them, and re-layouts  2.36 us
  transfers between devices with their start and end apart: 5, of which 3 were waited for; matrix products, arithmetic and copies ran while one was open for 0% of the time, Pallas kernels for 37%

profile of v1, /device:TPU:0, one launch (start us, length us, event | category | flops | bytes accessed | tf_op | source)
XLA Modules:
  0.0 108.1 jit_solution(7861183017878688710)
XLA Ops:
  6.5 0.0 all-gather.2.cloned.1.call-start
  6.5 0.7 all-gather.2.cloned.1.call-update
  7.3 0.0 copy-start.2
  7.3 0.0 copy-start.3
  7.3 0.0 copy-start.4
  7.3 35.5 %encode.1.emb = bf16[48,1536]{1,0:T(8,128)(2,1)} custom-call(bf16[3072,2048]{1,0:T(8,128)(2,1)} %bitcast.2, bf16[2048,512]{1,0:T(8,128)(2,1)} %wr_hbm.1, bf16[3,1536,512]{2,1,0:T(8,128)(2,1)} %bitcast.3, bf16[512,2048]{1,0:T(8,128)(2,1)} %we_hbm.1, bf16[2048,1536]{1,0:T(8,128)(2,1)} %wm_hbm.1), custom_call_target="tpu_custom_call" | custom-call | tf_op jit(solution)/shard_map/encode/pallas_call | solution.py:85
  42.8 18.4 %all_gather.6.emb = bf16[192,1536]{1,0:T(8,128)(2,1)S(1)} all-gather(bf16[48,1536]{1,0:T(8,128)(2,1)} %encode.1.emb), channel_id=1, replica_groups=mesh['tile'=4,'blk'=8] {'tile'}, dimensions={0}, use_global_device_ids=true | all-gather | bytes 737280 | tf_op jit(solution)/shard_map/all_gather | solution.py:215
  61.2 0.0 copy-done.2
  61.2 0.0 copy-start.5
  61.3 1.6 %project.1 = (bf16[192,384]{1,0:T(8,128)(2,1)S(1)}, bf16[192,384]{1,0:T(8,128)(2,1)S(1)}, bf16[192,384]{1,0:T(8,128)(2,1)S(1)}, bf16[192,384]{1,0:T(8,128)(2,1)S(1)}) custom-call(bf16[192,1536]{1,0:T(8,128)(2,1)S(1)} %all_gather.6.emb, bf16[1536,384]{1,0:T(8,128)(2,1)S(1)} %copy-done.2, bf16[1536,384]{1,0:T(8,128)(2,1)S(1)} %copy-done.3, ...), custom_call_target="tpu_custom_call" | custom-call | tf_op jit(solution)/shard_map/project/pallas_call | solution.py:123
  62.8 0.0 copy-start.1
  62.9 1.7 %collective-permute-start = (bf16[192,384]{1,0:T(8,128)(2,1)S(1)}, bf16[192,384]{1,0:T(8,128)(2,1)S(1)}, u32[]{:S(2)}, u32[]{:S(2)}) collective-permute-start(bf16[192,384]{1,0:T(8,128)(2,1)S(1)} %get-tuple-element.10), channel_id=1, source_target_pairs={{0,2},{1,3},{2,0},{3,1},{4,6},{5,7},{6,4},{7,5},{8,10},{9,11},{10,... | collective-permute-start | bytes 442376 | tf_op jit(solution)/shard_map/ppermute | solution.py:220
  64.5 2.6 %collective-permute-start.1 = (bf16[192,384]{1,0:T(8,128)(2,1)S(1)}, bf16[192,384]{1,0:T(8,128)(2,1)S(1)}, u32[]{:S(2)}, u32[]{:S(2)}) collective-permute-start(bf16[192,384]{1,0:T(8,128)(2,1)S(1)} %get-tuple-element.11), channel_id=1, source_target_pairs={{0,4},{1,5},{2,6},{3,7},{4,0},{5,1},{6,2},{7,3},{8,12},{9,13},{10,... | collective-permute-start | bytes 442376 | tf_op jit(solution)/shard_map/ppermute | solution.py:220
  67.1 0.2 collective-permute-start.2
  67.3 2.5 %collective-permute-done.refs_1_ = bf16[192,384]{1,0:T(8,128)(2,1)S(1)} collective-permute-done((bf16[192,384]{1,0:T(8,128)(2,1)S(1)}, bf16[192,384]{1,0:T(8,128)(2,1)S(1)}, u32[]{:S(2)}, u32[]{:S(2)}) %collective-permute-start) | collective-permute-done | bytes 147488 | tf_op jit(solution)/shard_map/ppermute | solution.py:220
  69.8 7.9 %collective-permute-done.1.refs_2_ = bf16[192,384]{1,0:T(8,128)(2,1)S(1)} collective-permute-done((bf16[192,384]{1,0:T(8,128)(2,1)S(1)}, bf16[192,384]{1,0:T(8,128)(2,1)S(1)}, u32[]{:S(2)}, u32[]{:S(2)}) %collective-permute-start.1) | collective-permute-done | bytes 147488 | tf_op jit(solution)/shard_map/ppermute | solution.py:220
  77.8 0.0 collective-permute-done.2.refs_3_
  77.8 0.1 collective-permute-start.3
  77.9 1.7 %collective-permute-done.3.refs_4_ = bf16[768,256]{1,0:T(8,128)(2,1)S(1)} collective-permute-done((bf16[768,256]{1,0:T(8,128)(2,1)S(1)}, bf16[768,256]{1,0:T(8,128)(2,1)S(1)}, u32[]{:S(2)}, u32[]{:S(2)}) %collective-permute-start.3) | collective-permute-done | bytes 393248 | tf_op jit(solution)/shard_map/ppermute | solution.py:223
  79.6 3.0 %attend.1 = bf16[16,48,128]{2,1,0:T(8,128)(2,1)S(1)} custom-call(s32[4]{0:T(128)S(1)} %copy-done.5, bf16[192,384]{1,0:T(8,128)(2,1)S(1)} %get-tuple-element.9.refs_0_, bf16[192,384]{1,0:T(8,128)(2,1)S(1)} %collective-permute-done.refs_1_, bf16[192,384]{1,0:T(8,128)(2,1)S(1)} %collective-permute-done.1.refs_2_, ...), custom_call_target="tpu_custom_call" | custom-call | tf_op jit(solution)/shard_map/attend/pallas_call | solution.py:182
  82.6 14.7 %all_to_all.5.parts = bf16[16,48,128]{2,1,0:T(8,128)(2,1)S(1)} all-to-all(bf16[16,48,128]{2,1,0:T(8,128)(2,1)S(1)} %attend.1), channel_id=1, replica_groups={{0,2,4,6,8,10,12,14,16,18,20,22,24,26,28,30},{1,3,5,7,9,11,13,15,17,19,..., dimensions={0} | all-to-all | bytes 393216 | tf_op jit(solution)/shard_map/all_to_all | solution.py:230
  97.3 0.0 copy-done.1
  97.3 2.3 %copy-done = bf16[1536,1536]{1,0:T(8,128)(2,1)S(1)} copy-done((bf16[1536,1536]{1,0:T(8,128)(2,1)S(1)}, bf16[1536,1536]{1,0:T(8,128)(2,1)}, u32[]{:S(2)}) %copy-start) | copy-done | bytes 4718616
  99.6 1.6 %finish.1 = bf16[48,1536]{1,0:T(8,128)(2,1)} custom-call(bf16[16,48,128]{2,1,0:T(8,128)(2,1)S(1)} %all_to_all.5.parts, bf16[1536,1536]{1,0:T(8,128)(2,1)S(1)} %copy-done, bf16[48,1536]{1,0:T(8,128)(2,1)S(1)} %copy-done.1), custom_call_target="tpu_custom_call" | custom-call | tf_op jit(solution)/shard_map/finish/pallas_call | solution.py:199
  (10 shorter events, 0.1 us)
Async XLA Ops:
  6.5 90.8 %all-gather.2.cloned.1.call-start = ((), (), s32[]{:S(2)}) async-start(), calls=%async_computation.1 | async-start | bytes 5898240 | tf_op jit(solution)/shard_map/all_gather | solution.py:213
  7.3 54.0 %copy-start.2 = (bf16[1536,384]{1,0:T(8,128)(2,1)S(1)}, bf16[1536,384]{1,0:T(8,128)(2,1)}, u32[]{:S(2)}) copy-start(bf16[1536,384]{1,0:T(8,128)(2,1)} %wq.1) | copy-start | bytes 3538948
  7.3 54.0 %copy-start.3 = (bf16[1536,384]{1,0:T(8,128)(2,1)S(1)}, bf16[1536,384]{1,0:T(8,128)(2,1)}, u32[]{:S(2)}) copy-start(bf16[1536,384]{1,0:T(8,128)(2,1)} %wk.1) | copy-start | bytes 3538948
  7.3 54.0 %copy-start.4 = (bf16[1536,384]{1,0:T(8,128)(2,1)S(1)}, bf16[1536,384]{1,0:T(8,128)(2,1)}, u32[]{:S(2)}) copy-start(bf16[1536,384]{1,0:T(8,128)(2,1)} %wv.1) | copy-start | bytes 3538948
  61.2 18.4 %copy-start.5 = (s32[4]{0:T(128)S(1)}, s32[4]{0:T(128)}, u32[]{:S(2)}) copy-start(s32[4]{0:T(128)} %slide_tiles.1) | copy-start | bytes 52
  62.8 34.4 %copy-start.1 = (bf16[48,1536]{1,0:T(8,128)(2,1)S(1)}, bf16[48,1536]{1,0:T(8,128)(2,1)}, u32[]{:S(2)}) copy-start(bf16[48,1536]{1,0:T(8,128)(2,1)} %encode.1.emb) | copy-start | bytes 442372
  62.9 7.0 %collective-permute-start = (bf16[192,384]{1,0:T(8,128)(2,1)S(1)}, bf16[192,384]{1,0:T(8,128)(2,1)S(1)}, u32[]{:S(2)}, u32[]{:S(2)}) collective-permute-start(bf16[192,384]{1,0:T(8,128)(2,1)S(1)} %get-tuple-element.10), channel_id=1, source_target_pairs={{0,2},{1,3},{2,0},{3,1},{4,6},{5,7},{6,4},{7,5},{8,10},{9,11},{10,... | collective-permute-start | bytes 442376 | tf_op jit(solution)/shard_map/ppermute | solution.py:220
  64.5 13.2 %collective-permute-start.1 = (bf16[192,384]{1,0:T(8,128)(2,1)S(1)}, bf16[192,384]{1,0:T(8,128)(2,1)S(1)}, u32[]{:S(2)}, u32[]{:S(2)}) collective-permute-start(bf16[192,384]{1,0:T(8,128)(2,1)S(1)} %get-tuple-element.11), channel_id=1, source_target_pairs={{0,4},{1,5},{2,6},{3,7},{4,0},{5,1},{6,2},{7,3},{8,12},{9,13},{10,... | collective-permute-start | bytes 442376 | tf_op jit(solution)/shard_map/ppermute | solution.py:220
  67.1 10.6 %collective-permute-start.2 = (bf16[192,384]{1,0:T(8,128)(2,1)S(1)}, bf16[192,384]{1,0:T(8,128)(2,1)S(1)}, u32[]{:S(2)}, u32[]{:S(2)}) collective-permute-start(bf16[192,384]{1,0:T(8,128)(2,1)S(1)} %get-tuple-element.12), channel_id=1, source_target_pairs={{0,6},{1,7},{2,4},{3,5},{4,2},{5,3},{6,0},{7,1},{8,14},{9,15},{10,... | collective-permute-start | bytes 442376 | tf_op jit(solution)/shard_map/ppermute | solution.py:220
  77.8 1.8 %collective-permute-start.3 = (bf16[768,256]{1,0:T(8,128)(2,1)S(1)}, bf16[768,256]{1,0:T(8,128)(2,1)S(1)}, u32[]{:S(2)}, u32[]{:S(2)}) collective-permute-start(bf16[768,256]{1,0:T(8,128)(2,1)S(1)} %pad_maximum_fusion), channel_id=1, source_target_pairs={{0,1},{1,0},{2,3},{3,2},{4,5},{5,4},{6,7},{7,6},{8,9},{9,8},{10,11... | collective-permute-start | bytes 1179656 | tf_op jit(solution)/shard_map/ppermute | solution.py:223
  97.3 2.3 %copy-start = (bf16[1536,1536]{1,0:T(8,128)(2,1)S(1)}, bf16[1536,1536]{1,0:T(8,128)(2,1)}, u32[]{:S(2)}) copy-start(bf16[1536,1536]{1,0:T(8,128)(2,1)} %all-gather.2.cloned.1.call-done.w_out) | copy-start | bytes 14155780
Sparse Core Ops, SparseCore 0:
  9.2 64.5 all-gather.1

commit v2 on v1

--- a/solution.py
+++ b/solution.py
@@ -10,6 +10,7 @@
 
 SIDE = 8
 HD = 96
+THIRD = HD // 3
 LANES = 128
 F32 = jnp.float32
 BF16 = jnp.bfloat16
@@ -104,38 +105,74 @@
 def project_kernel(heads, spread_of, emb, wq, wk, wv, *outs):
     a = lax.axis_index("blk") // spread_of
     scratch = outs[-1]
+    rows = emb.shape[0]
     values = emb[...].astype(F32)
     center = jnp.mean(values, axis=1, keepdims=True)
     values = values - center
     spread = jnp.mean(values * values, axis=1, keepdims=True)
     normed = (values * lax.rsqrt(spread + 1e-05)).astype(BF16)
-    scratch[...] = jnp.zeros_like(scratch)
-    for part, w in enumerate((wq, wk, wv)):
-        result = dot(normed, w[...]).astype(BF16)
-        for head in range(heads):
-            scratch[head, :, part * LANES : part * LANES + HD] = result[:, head * HD : (head + 1) * HD]
+    query, key, value = (dot(normed, w[...]) for w in (wq, wk, wv))
+    for head in range(heads):
+        q, k, v = (r[:, head * HD : (head + 1) * HD] for r in (query, key, value))
+        first = jnp.concatenate([q, v[:, 2 * THIRD :]], axis=1)
+        second = jnp.concatenate([k, v[:, THIRD : 2 * THIRD]], axis=1)
+        quarter = rows // 4
+        third = jnp.concatenate([v[i * quarter : (i + 1) * quarter, :THIRD] for i in range(4)], axis=1)
+        scratch[head] = jnp.concatenate([first, second, third], axis=0).astype(BF16)
     for e in range(heads):
         outs[e][...] = scratch[a ^ e]
 
 
 def project(emb, wq, wk, wv, heads, spread_of):
     rows = emb.shape[0]
+    packed = 2 * rows + rows // 4
     return pl.pallas_call(
         functools.partial(project_kernel, heads, spread_of),
-        out_shape=[jax.ShapeDtypeStruct((rows, 3 * LANES), BF16)] * heads,
-        scratch_shapes=[pltpu.VMEM((heads, rows, 3 * LANES), BF16)],
+        out_shape=[jax.ShapeDtypeStruct((packed, LANES), BF16)] * heads,
+        scratch_shapes=[pltpu.VMEM((heads, packed, LANES), BF16)],
         compiler_params=pltpu.CompilerParams(vmem_limit_bytes=24 << 20),
         name="project",
     )(emb, wq, wk, wv)
 
 
+def unpack_kernel(heads, *refs):
+    own, out = refs[:heads], refs[heads]
+    rows = own[0].shape[0] * 4 // 9
+    quarter = rows // 4
+    lane = lax.broadcasted_iota(jnp.int32, (rows, LANES), 1)
+    for e in range(heads):
+        first = own[e][:rows].astype(F32)
+        second = own[e][rows : 2 * rows].astype(F32)
+        third = own[e][2 * rows :].astype(F32)
+        low = jnp.concatenate(
+            [third] + [pltpu.roll(third, LANES - i * THIRD, axis=1) for i in range(1, 4)], axis=0
+        )
+        middle = pltpu.roll(second, 2 * THIRD, axis=1)
+        high = pltpu.roll(first, 3 * THIRD, axis=1)
+        value = jnp.where(lane < THIRD, low, jnp.where(lane < 2 * THIRD, middle, high))
+        value = jnp.where(lane < HD, value, jnp.where(lane == HD, 1.0, 0.0))
+        key = jnp.where(lane < HD, second, 0.0)
+        out[e * rows : (e + 1) * rows, :LANES] = key.astype(BF16)
+        out[e * rows : (e + 1) * rows, LANES:] = value.astype(BF16)
+
+
+def unpack(own):
+    rows = own[0].shape[0] * 4 // 9
+    return pl.pallas_call(
+        functools.partial(unpack_kernel, len(own)),
+        out_shape=jax.ShapeDtypeStruct((len(own) * rows, 2 * LANES), BF16),
+        compiler_params=pltpu.CompilerParams(vmem_limit_bytes=24 << 20),
+        name="unpack",
+    )(*own)
+
+
 def attend_kernel(heads, spread_of, tiles_of, slide_tiles, *refs):
     own = refs[:heads]
-    others = refs[heads : heads + spread_of - 1]
-    out, keys, values = refs[heads + spread_of - 1 :]
+    sets = refs[heads : heads + spread_of]
+    out = refs[heads + spread_of]
     blk = lax.axis_index("blk")
     a, c = blk // spread_of, lax.rem(blk, spread_of)
-    length = own[0].shape[0]
+    length = sets[0].shape[0] // heads
     count = length // tiles_of
     ends = [slide_tiles[0], slide_tiles[0] + slide_tiles[1]]
     ends.append(ends[1] + slide_tiles[2])
@@ -144,64 +181,86 @@
         pos = lax.broadcasted_iota(jnp.int32, shape, dim) + start
         return sum((pos >= end).astype(jnp.int32) for end in ends)
 
-    slides = []
-    lane = lax.broadcasted_iota(jnp.int32, (length, LANES), 1)
-    for f in range(spread_of):
-        for e in range(heads):
-            at = (f * heads + e) * length
-            if f == 0:
-                keys[at : at + length] = own[e][:, LANES : 2 * LANES]
-                value = own[e][:, 2 * LANES :]
-            else:
-                keys[at : at + length] = others[f - 1][e * length : (e + 1) * length, :LANES]
-                value = others[f - 1][e * length : (e + 1) * length, LANES:]
-            values[at : at + length] = jnp.where(lane == HD, 1.0, value.astype(F32)).astype(BF16)
-            slides.append(slide_of((1, length), 1, ((a ^ e) * spread_of + (c ^ f)) * length))
-    key_slide = jnp.concatenate(slides, axis=1)
+    key_slides = [
+        jnp.concatenate(
+            [slide_of((1, length), 1, ((a ^ e) * spread_of + (c ^ f)) * length) for e in range(heads)],
+            axis=1,
+        )
+        for f in range(spread_of)
+    ]
     scale = math.log2(math.e) / math.sqrt(HD)
-    me = lax.axis_index("tile")
     for e in range(heads):
-        query = own[e][:, :LANES]
+        query = own[e][:length]
         query_slide = slide_of((length, 1), 0, ((a ^ e) * spread_of + c) * length)
-        scores = lax.dot_general(
-            query, keys[...], (((1,), (1,)), ((), ())), preferred_element_type=F32
+        scores = []
+        for f in range(spread_of):
+            part = lax.dot_general(
+                query, sets[f][:, :LANES], (((1,), (1,)), ((), ())), preferred_element_type=F32
+            )
+            scores.append(jnp.where(query_slide == key_slides[f], part, -1e30))
+        top = functools.reduce(jnp.maximum, [jnp.max(s, axis=1, keepdims=True) for s in scores])
+        product = sum(
+            dot(jnp.exp2((s - top) * scale).astype(BF16), sets[f][:, LANES:])
+            for f, s in enumerate(scores)
         )
-        scores = jnp.where(query_slide == key_slide, scores, -1e30)
-        top = jnp.max(scores, axis=1, keepdims=True)
-        weights = jnp.exp2((scores - top) * scale).astype(BF16)
-        product = dot(weights, values[...])
         result = (product / product[:, HD : HD + 1]).astype(BF16)
         for t in range(tiles_of):
             out[t * heads + (a ^ e)] = result[t * count : (t + 1) * count]
 
 
-def attend(slide_tiles, own, others, heads, spread_of, tiles_of):
-    length = own[0].shape[0]
-    total = length * heads * spread_of
+def attend(slide_tiles, own, sets, tiles_of):
+    heads, spread_of = len(own), len(sets)
+    length = sets[0].shape[0] // heads
     whole = pl.BlockSpec(memory_space=pltpu.VMEM)
     return pl.pallas_call(
         functools.partial(attend_kernel, heads, spread_of, tiles_of),
-        in_specs=[pl.BlockSpec(memory_space=pltpu.SMEM)] + [whole] * (heads + spread_of - 1),
+        in_specs=[pl.BlockSpec(memory_space=pltpu.SMEM)] + [whole] * (heads + spread_of),
         out_specs=whole,
         out_shape=jax.ShapeDtypeStruct((tiles_of * heads, length // tiles_of, LANES), BF16),
-        scratch_shapes=[pltpu.VMEM((total, LANES), BF16), pltpu.VMEM((total, LANES), BF16)],
         compiler_params=pltpu.CompilerParams(vmem_limit_bytes=40 << 20),
         name="attend",
-    )(slide_tiles, *own, *others)
-
-
-def finish_kernel(parts, w_out, emb, out):
-    attended = jnp.concatenate([parts[h][:, :HD].astype(F32) for h in range(parts.shape[0])], axis=1)
-    out[...] = (emb[...].astype(F32) + dot(attended.astype(BF16), w_out[...])).astype(BF16)
-
-
-def finish(parts, w_out, emb):
-    return pl.pallas_call(
-        finish_kernel,
+    )(slide_tiles, *own, *sets)
+
+
+def finish_kernel(heads, order, parts, emb, *refs):
+    out = refs[-1]
+    total = emb[...].astype(F32)
+    for where, w in zip(order(), refs[:-1]):
+        attended = jnp.concatenate(
+            [parts[where * heads + h][:, :HD].astype(F32) for h in range(w.shape[0] // HD)], axis=1
+        )
+        total = total + dot(attended.astype(BF16), w[...])
+    out[...] = total.astype(BF16)
+
+
+def finish(parts, emb, w_outs, heads, order):
+    return pl.pallas_call(
+        functools.partial(finish_kernel, heads, order),
         out_shape=jax.ShapeDtypeStruct(emb.shape, BF16),
         compiler_params=pltpu.CompilerParams(vmem_limit_bytes=24 << 20),
         name="finish",
-    )(parts, w_out, emb)
+    )(parts, emb, *w_outs)
+
+
+def gather_w_out(w_out, tiles_of, blks):
+    if tiles_of != 4:
+        return [lax.all_gather(w_out, "tile", axis=0, tiled=True)], lambda: (0,)
+
+    def fetch(x, flip):
+        pairs = [
+            (t * blks + b, (t ^ flip[b % 2]) * blks + b) for t in range(tiles_of) for b in range(blks)
+        ]
+        return lax.ppermute(x, ("tile", "blk"), pairs)
+
+    first = fetch(w_out, (1, 2))
+    second = lax.ppermute(first, "blk", [(b, b ^ 1) for b in range(blks)])
+    third = fetch(first, (2, 1))
+
+    def order():
+        t, core = lax.axis_index("tile"), lax.rem(lax.axis_index("blk"), 2)
+        return t, t ^ (1 + core), t ^ (2 - core), t ^ 3
+
+    return [w_out, first, second, third], order
 
 
 def shards(tiles_of, blks, tiles, wr, ws, we, wm, wq, wk, wv, wo, slide_tiles):
@@ -210,7 +269,7 @@
     mid = wr.shape[1]
     heads = wq.shape[1] // HD
     spread_of = blks // heads
-    w_out = lax.all_gather(wo, "tile", axis=0, tiled=True)
+    w_outs, order = gather_w_out(wo, tiles_of, blks)
     emb = encode(flat, wr, ws.reshape(3, 3 * mid, mid), we, wm)
     gathered = lax.all_gather(emb, "tile", axis=0, tiled=True)
     mine = project(gathered, wq, wk, wv, heads, spread_of)
@@ -218,17 +277,16 @@
     for e in range(1, heads):
         pairs = [(i, i ^ (e * spread_of)) for i in range(blks)]
         own.append(lax.ppermute(mine[e], "blk", pairs))
-    key_value = jnp.concatenate([piece[:, LANES:] for piece in own], axis=0)
-    others = [
-        lax.ppermute(key_value, "blk", [(i, i ^ f) for i in range(blks)]) for f in range(1, spread_of)
-    ]
-    attended = attend(slide_tiles, own, others, heads, spread_of, tiles_of)
+    sets = [unpack(own)]
+    for f in range(1, spread_of):
+        sets.append(lax.ppermute(sets[0], "blk", [(i, i ^ f) for i in range(blks)]))
+    attended = attend(slide_tiles, own, sets, tiles_of)
     groups = [
         [t * blks + a * spread_of + c for t in range(tiles_of) for a in range(heads)]
         for c in range(spread_of)
     ]
     parts = lax.all_to_all(attended, ("tile", "blk"), 0, 0, axis_index_groups=groups, tiled=True)
-    return finish(parts, w_out, emb)
+    return finish(parts, emb, w_outs, heads, order)
 
 
 def solution(mesh):

time: 108 us -> 101 us (0.935)
  between operations: 13.5 us -> 0.09 us
  waiting for transfers between devices: 12.8 us -> 24 us
  blocking collectives: 33.1 us -> 25.7 us
  starting transfers between devices: 4.53 us -> 9.52 us
  local copies, waits for them, and re-layouts: 2.39 us -> 0.02 us
    ppermute x1 -> x4, waiting for transfers between devices: 1.71 us -> 16.1 us  [the longest x2 14.4 us: fetch(): return lax.ppermute(x, ('tile', 'blk'), pairs)]
    all_gather x1, blocking collectives: 18.4 us -> 11.2 us  [shards(): gathered = lax.all_gather(emb, 'tile', axis=0, tiled=True)]
    ppermute x1 -> x4, starting transfers between devices: 0.07 us -> 5.06 us  [the longest x2 4.99 us: fetch(): return lax.ppermute(x, ('tile', 'blk'), pairs)]
    ppermute x3, waiting for transfers between devices: 10.4 us -> 7.89 us  [shards(): own.append(lax.ppermute(mine[e], 'blk', pairs))]
    unnamed x12, local copies, waits for them, and re-layouts: 2.36 us -> 0.02 us
  transfers between devices with their start and end apart: 5 -> 7, of which waited for: 3 -> 4; matrix products, arithmetic and copies ran while one was open for 0% -> 0% of each run, Pallas kernels for 37% -> 40%
where the time goes in v2:
time: 101 us
  Pallas kernels  41.8 us (41%)
  blocking collectives  25.7 us (25%)
  waiting for transfers between devices  24 us (24%)
  starting transfers between devices  9.52 us (9%)
    pallas_call x1, Pallas kernels, encode(): pl.pallas_call(encode_kernel, grid=(count // GROUP,), in_specs=[pl.BlockS...  35.5 us
    all_to_all x1, blocking collectives, shards(): lax.all_to_all(attended, ('tile', 'blk'), 0, 0, axis_index_groups=groups,...  14.5 us
    ppermute x2, waiting for transfers between devices, fetch(): return lax.ppermute(x, ('tile', 'blk'), pairs)  14.4 us
    all_gather x1, blocking collectives, shards(): gathered = lax.all_gather(emb, 'tile', axis=0, tiled=True)  11.2 us
    ppermute x3, waiting for transfers between devices, shards(): own.append(lax.ppermute(mine[e], 'blk', pairs))  7.89 us
    ppermute x2, starting transfers between devices, fetch(): return lax.ppermute(x, ('tile', 'blk'), pairs)  4.99 us
    ppermute x3, starting transfers between devices, shards(): own.append(lax.ppermute(mine[e], 'blk', pairs))  4.45 us
    pallas_call x1, Pallas kernels, attend(): pl.pallas_call(functools.partial(attend_kernel, heads, spread_of, tiles_o...  2.88 us
  transfers between devices with their start and end apart: 7, of which 4 were waited for; matrix products, arithmetic and copies ran while one was open for 0% of the time, Pallas kernels for 40%

profile of v2, /device:TPU:0, one launch (start us, length us, event | category | flops | bytes accessed | tf_op | source)
XLA Modules:
  0.0 101.1 jit_solution(11950827543955532775)
XLA Ops:
  0.0 2.9 %collective-permute-start.4 = (bf16[384,1536]{1,0:T(8,128)(2,1)}, bf16[384,1536]{1,0:T(8,128)(2,1)S(1)}, u32[]{:S(2)}, u32[]{:S(2)}) collective-permute-start(bf16[384,1536]{1,0:T(8,128)(2,1)} %refs_0_.1), channel_id=1, source_target_pairs={{0,8},{1,17},{2,10},{3,19},{4,12},{5,21},{6,14},{7,23},{8,0},{9,25... | collective-permute-start | bytes 3538952 | tf_op jit(solution)/shard_map/ppermute | solution.py:253
  2.9 14.4 %collective-permute-done.4.refs_1_ = bf16[384,1536]{1,0:T(8,128)(2,1)S(1)} collective-permute-done((bf16[384,1536]{1,0:T(8,128)(2,1)}, bf16[384,1536]{1,0:T(8,128)(2,1)S(1)}, u32[]{:S(2)}, u32[]{:S(2)}) %collective-permute-start.4) | collective-permute-done | bytes 1179680 | tf_op jit(solution)/shard_map/ppermute | solution.py:253
  17.3 2.1 %collective-permute-start.6 = (bf16[384,1536]{1,0:T(8,128)(2,1)S(1)}, bf16[384,1536]{1,0:T(8,128)(2,1)S(1)}, u32[]{:S(2)}, u32[]{:S(2)}) collective-permute-start(bf16[384,1536]{1,0:T(8,128)(2,1)S(1)} %collective-permute-done.4.refs_1_), channel_id=1, source_target_pairs={{0,16},{1,9},{2,18},{3,11},{4,20},{5,13},{6,22},{7,15},{8,24},{9,1... | collective-permute-start | bytes 3538952 | tf_op jit(solution)/shard_map/ppermute | solution.py:253
  19.4 0.0 collective-permute-start.5
  19.4 35.5 %encode.1.emb = bf16[48,1536]{1,0:T(8,128)(2,1)} custom-call(bf16[3072,2048]{1,0:T(8,128)(2,1)} %bitcast.2, bf16[2048,512]{1,0:T(8,128)(2,1)} %wr_hbm.1, bf16[3,1536,512]{2,1,0:T(8,128)(2,1)} %bitcast.3, bf16[512,2048]{1,0:T(8,128)(2,1)} %we_hbm.1, bf16[2048,1536]{1,0:T(8,128)(2,1)} %wm_hbm.1), custom_call_target="tpu_custom_call" | custom-call | tf_op jit(solution)/shard_map/encode/pallas_call | solution.py:86
  54.9 11.2 %all_gather.3.emb = bf16[192,1536]{1,0:T(8,128)(2,1)S(1)} all-gather(bf16[48,1536]{1,0:T(8,128)(2,1)} %encode.1.emb), channel_id=1, replica_groups=mesh['tile'=4,'blk'=8] {'tile'}, dimensions={0}, use_global_device_ids=true | all-gather | bytes 737280 | tf_op jit(solution)/shard_map/all_gather | solution.py:274
  66.2 0.0 copy-done.2
  66.2 0.0 copy-start.5
  66.2 1.5 %project.1 = (bf16[432,128]{1,0:T(8,128)(2,1)S(1)}, bf16[432,128]{1,0:T(8,128)(2,1)S(1)}, bf16[432,128]{1,0:T(8,128)(2,1)S(1)}, bf16[432,128]{1,0:T(8,128)(2,1)S(1)}) custom-call(bf16[192,1536]{1,0:T(8,128)(2,1)S(1)} %all_gather.3.emb, bf16[1536,384]{1,0:T(8,128)(2,1)S(1)} %copy-done.2, bf16[1536,384]{1,0:T(8,128)(2,1)S(1)} %copy-done.3, ...), custom_call_target="tpu_custom_call" | custom-call | tf_op jit(solution)/shard_map/project/pallas_call | solution.py:129
  67.7 1.6 %collective-permute-start = (bf16[432,128]{1,0:T(8,128)(2,1)S(1)}, bf16[432,128]{1,0:T(8,128)(2,1)S(1)}, u32[]{:S(2)}, u32[]{:S(2)}) collective-permute-start(bf16[432,128]{1,0:T(8,128)(2,1)S(1)} %get-tuple-element.10), channel_id=1, source_target_pairs={{0,2},{1,3},{2,0},{3,1},{4,6},{5,7},{6,4},{7,5},{8,10},{9,11},{10,... | collective-permute-start | bytes 331784 | tf_op jit(solution)/shard_map/ppermute | solution.py:279
  69.4 2.6 %collective-permute-start.1 = (bf16[432,128]{1,0:T(8,128)(2,1)S(1)}, bf16[432,128]{1,0:T(8,128)(2,1)S(1)}, u32[]{:S(2)}, u32[]{:S(2)}) collective-permute-start(bf16[432,128]{1,0:T(8,128)(2,1)S(1)} %get-tuple-element.11), channel_id=1, source_target_pairs={{0,4},{1,5},{2,6},{3,7},{4,0},{5,1},{6,2},{7,3},{8,12},{9,13},{10,... | collective-permute-start | bytes 331784 | tf_op jit(solution)/shard_map/ppermute | solution.py:279
  72.0 0.2 collective-permute-start.2
  72.2 1.4 %collective-permute-done.refs_1_ = bf16[432,128]{1,0:T(8,128)(2,1)S(1)} collective-permute-done((bf16[432,128]{1,0:T(8,128)(2,1)S(1)}, bf16[432,128]{1,0:T(8,128)(2,1)S(1)}, u32[]{:S(2)}, u32[]{:S(2)}) %collective-permute-start) | collective-permute-done | bytes 110624 | tf_op jit(solution)/shard_map/ppermute | solution.py:279
  73.6 6.4 %collective-permute-done.1.refs_2_ = bf16[432,128]{1,0:T(8,128)(2,1)S(1)} collective-permute-done((bf16[432,128]{1,0:T(8,128)(2,1)S(1)}, bf16[432,128]{1,0:T(8,128)(2,1)S(1)}, u32[]{:S(2)}, u32[]{:S(2)}) %collective-permute-start.1) | collective-permute-done | bytes 110624 | tf_op jit(solution)/shard_map/ppermute | solution.py:279
  80.1 0.0 collective-permute-done.2.refs_3_
  80.1 0.2 unpack.1.refs_4_
  80.3 0.1 collective-permute-start.3
  80.4 1.7 %collective-permute-done.3.refs_5_ = bf16[768,256]{1,0:T(8,128)(2,1)S(1)} collective-permute-done((bf16[768,256]{1,0:T(8,128)(2,1)S(1)}, bf16[768,256]{1,0:T(8,128)(2,1)S(1)}, u32[]{:S(2)}, u32[]{:S(2)}) %collective-permute-start.3) | collective-permute-done | bytes 393248 | tf_op jit(solution)/shard_map/ppermute | solution.py:282
  82.1 2.9 %attend.1 = bf16[16,48,128]{2,1,0:T(8,128)(2,1)S(1)} custom-call(s32[4]{0:T(128)S(1)} %copy-done.5, bf16[432,128]{1,0:T(8,128)(2,1)S(1)} %get-tuple-element.9.refs_0_, bf16[432,128]{1,0:T(8,128)(2,1)S(1)} %collective-permute-done.refs_1_, bf16[432,128]{1,0:T(8,128)(2,1)S(1)} %collective-permute-done.1.refs_2_, ...), custom_call_target="tpu_custom_call" | custom-call | tf_op jit(solution)/shard_map/attend/pallas_call | solution.py:215
  85.0 14.5 %all_to_all.5.parts = bf16[16,48,128]{2,1,0:T(8,128)(2,1)S(1)} all-to-all(bf16[16,48,128]{2,1,0:T(8,128)(2,1)S(1)} %attend.1), channel_id=1, replica_groups={{0,2,4,6,8,10,12,14,16,18,20,22,24,26,28,30},{1,3,5,7,9,11,13,15,17,19,..., dimensions={0} | all-to-all | bytes 393216 | tf_op jit(solution)/shard_map/all_to_all | solution.py:288
  99.4 0.0 collective-permute-done.6.refs_3_
  99.4 0.0 collective-permute-done.5.refs_2_
  99.4 0.0 copy-done
  99.5 1.7 %finish.1 = bf16[48,1536]{1,0:T(8,128)(2,1)} custom-call(bf16[16,48,128]{2,1,0:T(8,128)(2,1)S(1)} %all_to_all.5.parts, bf16[48,1536]{1,0:T(8,128)(2,1)S(1)} %copy-done, bf16[384,1536]{1,0:T(8,128)(2,1)S(1)} %copy-done.1, bf16[384,1536]{1,0:T(8,128)(2,1)S(1)} %collective-permute-done.4.refs_1_, bf16[384,1536]{1,0:T(8,128)(2,1)S(1)} %collective-permute-done.5.refs_2_, ...), custom_call_target="tpu_custom_call" | custom-call | tf_op jit(solution)/shard_map/finish/pallas_call | solution.py:237
  (9 shorter events, 0.0 us)
Async XLA Ops:
  0.0 17.3 %collective-permute-start.4 = (bf16[384,1536]{1,0:T(8,128)(2,1)}, bf16[384,1536]{1,0:T(8,128)(2,1)S(1)}, u32[]{:S(2)}, u32[]{:S(2)}) collective-permute-start(bf16[384,1536]{1,0:T(8,128)(2,1)} %refs_0_.1), channel_id=1, source_target_pairs={{0,8},{1,17},{2,10},{3,19},{4,12},{5,21},{6,14},{7,23},{8,0},{9,25... | collective-permute-start | bytes 3538952 | tf_op jit(solution)/shard_map/ppermute | solution.py:253
  17.3 82.1 %collective-permute-start.6 = (bf16[384,1536]{1,0:T(8,128)(2,1)S(1)}, bf16[384,1536]{1,0:T(8,128)(2,1)S(1)}, u32[]{:S(2)}, u32[]{:S(2)}) collective-permute-start(bf16[384,1536]{1,0:T(8,128)(2,1)S(1)} %collective-permute-done.4.refs_1_), channel_id=1, source_target_pairs={{0,16},{1,9},{2,18},{3,11},{4,20},{5,13},{6,22},{7,15},{8,24},{9,1... | collective-permute-start | bytes 3538952 | tf_op jit(solution)/shard_map/ppermute | solution.py:253
  19.4 80.1 %collective-permute-start.5 = (bf16[384,1536]{1,0:T(8,128)(2,1)S(1)}, bf16[384,1536]{1,0:T(8,128)(2,1)S(1)}, u32[]{:S(2)}, u32[]{:S(2)}) collective-permute-start(bf16[384,1536]{1,0:T(8,128)(2,1)S(1)} %collective-permute-done.4.refs_1_), channel_id=1, source_target_pairs={{0,1},{1,0},{2,3},{3,2},{4,5},{5,4},{6,7},{7,6},{8,9},{9,8},{10,11... | collective-permute-start | bytes 3538952 | tf_op jit(solution)/shard_map/ppermute | solution.py:256
  19.4 46.8 %copy-start.2 = (bf16[1536,384]{1,0:T(8,128)(2,1)S(1)}, bf16[1536,384]{1,0:T(8,128)(2,1)}, u32[]{:S(2)}) copy-start(bf16[1536,384]{1,0:T(8,128)(2,1)} %wq.1) | copy-start | bytes 3538948
  19.4 46.8 %copy-start.3 = (bf16[1536,384]{1,0:T(8,128)(2,1)S(1)}, bf16[1536,384]{1,0:T(8,128)(2,1)}, u32[]{:S(2)}) copy-start(bf16[1536,384]{1,0:T(8,128)(2,1)} %wk.1) | copy-start | bytes 3538948
  19.4 46.8 %copy-start.4 = (bf16[1536,384]{1,0:T(8,128)(2,1)S(1)}, bf16[1536,384]{1,0:T(8,128)(2,1)}, u32[]{:S(2)}) copy-start(bf16[1536,384]{1,0:T(8,128)(2,1)} %wv.1) | copy-start | bytes 3538948
  66.2 15.9 %copy-start.5 = (s32[4]{0:T(128)S(1)}, s32[4]{0:T(128)}, u32[]{:S(2)}) copy-start(s32[4]{0:T(128)} %slide_tiles.1) | copy-start | bytes 52
  67.7 5.9 %collective-permute-start = (bf16[432,128]{1,0:T(8,128)(2,1)S(1)}, bf16[432,128]{1,0:T(8,128)(2,1)S(1)}, u32[]{:S(2)}, u32[]{:S(2)}) collective-permute-start(bf16[432,128]{1,0:T(8,128)(2,1)S(1)} %get-tuple-element.10), channel_id=1, source_target_pairs={{0,2},{1,3},{2,0},{3,1},{4,6},{5,7},{6,4},{7,5},{8,10},{9,11},{10,... | collective-permute-start | bytes 331784 | tf_op jit(solution)/shard_map/ppermute | solution.py:279
  69.4 10.7 %collective-permute-start.1 = (bf16[432,128]{1,0:T(8,128)(2,1)S(1)}, bf16[432,128]{1,0:T(8,128)(2,1)S(1)}, u32[]{:S(2)}, u32[]{:S(2)}) collective-permute-start(bf16[432,128]{1,0:T(8,128)(2,1)S(1)} %get-tuple-element.11), channel_id=1, source_target_pairs={{0,4},{1,5},{2,6},{3,7},{4,0},{5,1},{6,2},{7,3},{8,12},{9,13},{10,... | collective-permute-start | bytes 331784 | tf_op jit(solution)/shard_map/ppermute | solution.py:279
  72.0 8.1 %collective-permute-start.2 = (bf16[432,128]{1,0:T(8,128)(2,1)S(1)}, bf16[432,128]{1,0:T(8,128)(2,1)S(1)}, u32[]{:S(2)}, u32[]{:S(2)}) collective-permute-start(bf16[432,128]{1,0:T(8,128)(2,1)S(1)} %get-tuple-element.12), channel_id=1, source_target_pairs={{0,6},{1,7},{2,4},{3,5},{4,2},{5,3},{6,0},{7,1},{8,14},{9,15},{10,... | collective-permute-start | bytes 331784 | tf_op jit(solution)/shard_map/ppermute | solution.py:279
  80.1 19.4 %copy-start = (bf16[48,1536]{1,0:T(8,128)(2,1)S(1)}, bf16[48,1536]{1,0:T(8,128)(2,1)}, u32[]{:S(2)}) copy-start(bf16[48,1536]{1,0:T(8,128)(2,1)} %encode.1.emb) | copy-start | bytes 442372
  80.1 19.4 %copy-start.1 = (bf16[384,1536]{1,0:T(8,128)(2,1)S(1)}, bf16[384,1536]{1,0:T(8,128)(2,1)}, u32[]{:S(2)}) copy-start(bf16[384,1536]{1,0:T(8,128)(2,1)} %refs_0_.1) | copy-start | bytes 3538948
  80.3 1.8 %collective-permute-start.3 = (bf16[768,256]{1,0:T(8,128)(2,1)S(1)}, bf16[768,256]{1,0:T(8,128)(2,1)S(1)}, u32[]{:S(2)}, u32[]{:S(2)}) collective-permute-start(bf16[768,256]{1,0:T(8,128)(2,1)S(1)} %unpack.1.refs_4_), channel_id=1, source_target_pairs={{0,1},{1,0},{2,3},{3,2},{4,5},{5,4},{6,7},{7,6},{8,9},{9,8},{10,11... | collective-permute-start | bytes 1179656 | tf_op jit(solution)/shard_map/ppermute | solution.py:282

commit v3 on v2

--- a/solution.py
+++ b/solution.py
@@ -98,6 +98,11 @@
             pltpu.SemaphoreType.DMA((4,)),
         ],
         compiler_params=pltpu.CompilerParams(vmem_limit_bytes=56 << 20),
+        cost_estimate=pl.CostEstimate(
+            flops=2 * total * (2 * c * wr.shape[1] + 9 * wr.shape[1] ** 2),
+            bytes_accessed=2 * (total * c + wr.size + ws.size + we.size + wm.size),
+            transcendentals=0,
+        ),
         name="encode",
     )(flat, wr, ws, we, wm)
 
@@ -242,25 +247,14 @@
     )(parts, emb, *w_outs)
 
 
-def gather_w_out(w_out, tiles_of, blks):
-    if tiles_of != 4:
-        return [lax.all_gather(w_out, "tile", axis=0, tiled=True)], lambda: (0,)
-
-    def fetch(x, flip):
-        pairs = [
-            (t * blks + b, (t ^ flip[b % 2]) * blks + b) for t in range(tiles_of) for b in range(blks)
-        ]
-        return lax.ppermute(x, ("tile", "blk"), pairs)
-
-    first = fetch(w_out, (1, 2))
-    second = lax.ppermute(first, "blk", [(b, b ^ 1) for b in range(blks)])
-    third = fetch(first, (2, 1))
-
-    def order():
-        t, core = lax.axis_index("tile"), lax.rem(lax.axis_index("blk"), 2)
-        return t, t ^ (1 + core), t ^ (2 - core), t ^ 3
-
-    return [w_out, first, second, third], order
+def fetch(x, flip, tiles_of, blks):
+    pairs = [(t * blks + b, (t ^ flip[b % 2]) * blks + b) for t in range(tiles_of) for b in range(blks)]
+    return lax.ppermute(x, ("tile", "blk"), pairs)
+
+
+def tile_order():
+    t, core = lax.axis_index("tile"), lax.rem(lax.axis_index("blk"), 2)
+    return t, t ^ (1 + core), t ^ (2 - core), t ^ 3
 
 
 def shards(tiles_of, blks, tiles, wr, ws, we, wm, wq, wk, wv, wo, slide_tiles):
@@ -269,7 +263,8 @@
     mid = wr.shape[1]
     heads = wq.shape[1] // HD
     spread_of = blks // heads
-    w_outs, order = gather_w_out(wo, tiles_of, blks)
+    relay = tiles_of == 4
+    first = fetch(wo, (1, 2), tiles_of, blks) if relay else lax.all_gather(wo, "tile", axis=0, tiled=True)
     emb = encode(flat, wr, ws.reshape(3, 3 * mid, mid), we, wm)
     gathered = lax.all_gather(emb, "tile", axis=0, tiled=True)
     mine = project(gathered, wq, wk, wv, heads, spread_of)
@@ -277,6 +272,13 @@
     for e in range(1, heads):
         pairs = [(i, i ^ (e * spread_of)) for i in range(blks)]
         own.append(lax.ppermute(mine[e], "blk", pairs))
+    if relay:
+        first, *_ = lax.optimization_barrier((first, *own))
+        second = lax.ppermute(first, "blk", [(b, b ^ 1) for b in range(blks)])
+        third = fetch(first, (2, 1), tiles_of, blks)
+        w_outs, order = [wo, first, second, third], tile_order
+    else:
+        w_outs, order = [first], lambda: (0,)
     sets = [unpack(own)]
     for f in range(1, spread_of):
         sets.append(lax.ppermute(sets[0], "blk", [(i, i ^ f) for i in range(blks)]))

time: 101 us -> 85.2 us (0.84)
  waiting for transfers between devices: 24 us -> 8.99 us
  blocking collectives: 25.7 us -> 24.6 us
    ppermute x2, waiting for transfers between devices: 14.4 us -> 0.01 us  [fetch(): return lax.ppermute(x, ('tile', 'blk'), pairs)]
    ppermute x3, waiting for transfers between devices: 7.89 us -> 6.38 us  [shards(): own.append(lax.ppermute(mine[e], 'blk', pairs))]
  transfers between devices with their start and end apart: 7 -> 7, of which waited for: 4 -> 4; matrix products, arithmetic and copies ran while one was open for 0% -> 0% of each run, Pallas kernels for 40% -> 47%
where the time goes in v3:
time: 85.2 us; the launch traced here: 85 us
  Pallas kernels  41.8 us (49%)
  blocking collectives  24.6 us (29%)
  starting transfers between devices  9.4 us (11%)
  waiting for transfers between devices  8.99 us (11%)
    pallas_call x1, Pallas kernels, encode(): pl.pallas_call(encode_kernel, grid=(count // GROUP,), in_specs=[pl.BlockS...  35.5 us
    all_to_all x1, blocking collectives, shards(): lax.all_to_all(attended, ('tile', 'blk'), 0, 0, axis_index_groups=groups,...  14.3 us
    all_gather x1, blocking collectives, shards(): gathered = lax.all_gather(emb, 'tile', axis=0, tiled=True)  10.3 us
    ppermute x3, waiting for transfers between devices, shards(): own.append(lax.ppermute(mine[e], 'blk', pairs))  6.38 us
    ppermute x3, starting transfers between devices, shards(): own.append(lax.ppermute(mine[e], 'blk', pairs))  4.45 us
    ppermute x2, starting transfers between devices, fetch(): return lax.ppermute(x, ('tile', 'blk'), pairs)  4.38 us
    pallas_call x1, Pallas kernels, attend(): pl.pallas_call(functools.partial(attend_kernel, heads, spread_of, tiles_o...  2.89 us
    ppermute x1, waiting for transfers between devices, shards(): sets.append(lax.ppermute(sets[0], 'blk', [(i, i ^ f) for i in range(blks)]))  2.61 us
  transfers between devices with their start and end apart: 7, of which 4 were waited for; matrix products, arithmetic and copies ran while one was open for 0% of the time, Pallas kernels for 47%

profile of v3, /device:TPU:0, one launch (start us, length us, event | category | flops | bytes accessed | tf_op | source)
XLA Modules:
  0.0 85.0 jit_solution(17295301067472641357)
XLA Ops:
  0.0 2.9 %collective-permute-start.4 = (bf16[384,1536]{1,0:T(8,128)(2,1)}, bf16[384,1536]{1,0:T(8,128)(2,1)S(1)}, u32[]{:S(2)}, u32[]{:S(2)}) collective-permute-start(bf16[384,1536]{1,0:T(8,128)(2,1)} %refs_0_.1), channel_id=1, source_target_pairs={{0,8},{1,17},{2,10},{3,19},{4,12},{5,21},{6,14},{7,23},{8,0},{9,25... | collective-permute-start | bytes 3538952 | tf_op jit(solution)/shard_map/ppermute | solution.py:252
  2.9 35.5 %encode.1.emb = bf16[48,1536]{1,0:T(8,128)(2,1)} custom-call(bf16[3072,2048]{1,0:T(8,128)(2,1)} %bitcast.2, bf16[2048,512]{1,0:T(8,128)(2,1)} %wr_hbm.1, bf16[3,1536,512]{2,1,0:T(8,128)(2,1)} %bitcast.3, bf16[512,2048]{1,0:T(8,128)(2,1)} %we_hbm.1, bf16[2048,1536]{1,0:T(8,128)(2,1)} %wm_hbm.1), custom_call_target="tpu_custom_call" | custom-call | flops 27380416512 | bytes 27787264 | tf_op jit(solution)/shard_map/encode/pallas_call | solution.py:86
  38.5 10.3 %all_gather.3.emb = bf16[192,1536]{1,0:T(8,128)(2,1)S(1)} all-gather(bf16[48,1536]{1,0:T(8,128)(2,1)} %encode.1.emb), channel_id=1, replica_groups=mesh['tile'=4,'blk'=8] {'tile'}, dimensions={0}, use_global_device_ids=true | all-gather | bytes 737280 | tf_op jit(solution)/shard_map/all_gather | solution.py:269
  48.8 0.0 copy-start.5
  48.8 1.5 %project.1 = (bf16[432,128]{1,0:T(8,128)(2,1)S(1)}, bf16[432,128]{1,0:T(8,128)(2,1)S(1)}, bf16[432,128]{1,0:T(8,128)(2,1)S(1)}, bf16[432,128]{1,0:T(8,128)(2,1)S(1)}) custom-call(bf16[192,1536]{1,0:T(8,128)(2,1)S(1)} %all_gather.3.emb, bf16[1536,384]{1,0:T(8,128)(2,1)S(1)} %copy-done.1, bf16[1536,384]{1,0:T(8,128)(2,1)S(1)} %copy-done.2, ...), custom_call_target="tpu_custom_call" | custom-call | tf_op jit(solution)/shard_map/project/pallas_call | solution.py:134
  50.4 1.6 %collective-permute-start = (bf16[432,128]{1,0:T(8,128)(2,1)S(1)}, bf16[432,128]{1,0:T(8,128)(2,1)S(1)}, u32[]{:S(2)}, u32[]{:S(2)}) collective-permute-start(bf16[432,128]{1,0:T(8,128)(2,1)S(1)} %get-tuple-element.11), channel_id=1, source_target_pairs={{0,2},{1,3},{2,0},{3,1},{4,6},{5,7},{6,4},{7,5},{8,10},{9,11},{10,... | collective-permute-start | bytes 331784 | tf_op jit(solution)/shard_map/ppermute | solution.py:274
  52.0 2.6 %collective-permute-start.1 = (bf16[432,128]{1,0:T(8,128)(2,1)S(1)}, bf16[432,128]{1,0:T(8,128)(2,1)S(1)}, u32[]{:S(2)}, u32[]{:S(2)}) collective-permute-start(bf16[432,128]{1,0:T(8,128)(2,1)S(1)} %get-tuple-element.12), channel_id=1, source_target_pairs={{0,4},{1,5},{2,6},{3,7},{4,0},{5,1},{6,2},{7,3},{8,12},{9,13},{10,... | collective-permute-start | bytes 331784 | tf_op jit(solution)/shard_map/ppermute | solution.py:274
  54.6 0.2 collective-permute-start.2
  54.8 0.7 collective-permute-done.refs_1_
  55.5 4.4 %collective-permute-done.1.refs_2_ = bf16[432,128]{1,0:T(8,128)(2,1)S(1)} collective-permute-done((bf16[432,128]{1,0:T(8,128)(2,1)S(1)}, bf16[432,128]{1,0:T(8,128)(2,1)S(1)}, u32[]{:S(2)}, u32[]{:S(2)}) %collective-permute-start.1) | collective-permute-done | bytes 110624 | tf_op jit(solution)/shard_map/ppermute | solution.py:274
  59.9 1.3 %collective-permute-done.2.refs_3_ = bf16[432,128]{1,0:T(8,128)(2,1)S(1)} collective-permute-done((bf16[432,128]{1,0:T(8,128)(2,1)S(1)}, bf16[432,128]{1,0:T(8,128)(2,1)S(1)}, u32[]{:S(2)}, u32[]{:S(2)}) %collective-permute-start.2) | collective-permute-done | bytes 110624 | tf_op jit(solution)/shard_map/ppermute | solution.py:274
  61.2 0.0 collective-permute-done.4.refs_1_
  61.2 1.4 %collective-permute-start.6 = (bf16[384,1536]{1,0:T(8,128)(2,1)S(1)}, bf16[384,1536]{1,0:T(8,128)(2,1)S(1)}, u32[]{:S(2)}, u32[]{:S(2)}) collective-permute-start(bf16[384,1536]{1,0:T(8,128)(2,1)S(1)} %collective-permute-done.4.refs_1_), channel_id=1, source_target_pairs={{0,16},{1,9},{2,18},{3,11},{4,20},{5,13},{6,22},{7,15},{8,24},{9,1... | collective-permute-start | bytes 3538952 | tf_op jit(solution)/shard_map/ppermute | solution.py:252
  62.6 0.0 collective-permute-start.5
  62.6 0.2 unpack.1.refs_4_
  62.9 0.6 collective-permute-start.3
  63.4 2.6 %collective-permute-done.3.refs_5_ = bf16[768,256]{1,0:T(8,128)(2,1)S(1)} collective-permute-done((bf16[768,256]{1,0:T(8,128)(2,1)S(1)}, bf16[768,256]{1,0:T(8,128)(2,1)S(1)}, u32[]{:S(2)}, u32[]{:S(2)}) %collective-permute-start.3) | collective-permute-done | bytes 393248 | tf_op jit(solution)/shard_map/ppermute | solution.py:284
  66.1 0.0 copy-done.5
  66.1 2.9 %attend.1 = bf16[16,48,128]{2,1,0:T(8,128)(2,1)S(1)} custom-call(s32[4]{0:T(128)S(1)} %copy-done.5, bf16[432,128]{1,0:T(8,128)(2,1)S(1)} %get-tuple-element.10.refs_0_, bf16[432,128]{1,0:T(8,128)(2,1)S(1)} %collective-permute-done.refs_1_, bf16[432,128]{1,0:T(8,128)(2,1)S(1)} %collective-permute-done.1.refs_2_, ...), custom_call_target="tpu_custom_call" | custom-call | tf_op jit(solution)/shard_map/attend/pallas_call | solution.py:220
  68.9 14.3 %all_to_all.5.parts = bf16[16,48,128]{2,1,0:T(8,128)(2,1)S(1)} all-to-all(bf16[16,48,128]{2,1,0:T(8,128)(2,1)S(1)} %attend.1), channel_id=1, replica_groups={{0,2,4,6,8,10,12,14,16,18,20,22,24,26,28,30},{1,3,5,7,9,11,13,15,17,19,..., dimensions={0} | all-to-all | bytes 393216 | tf_op jit(solution)/shard_map/all_to_all | solution.py:290
  83.3 0.0 collective-permute-done.6.refs_3_
  83.3 0.0 collective-permute-done.5.refs_2_
  83.3 0.0 copy-done.4
  83.3 1.7 %finish.1 = bf16[48,1536]{1,0:T(8,128)(2,1)} custom-call(bf16[16,48,128]{2,1,0:T(8,128)(2,1)S(1)} %all_to_all.5.parts, bf16[48,1536]{1,0:T(8,128)(2,1)S(1)} %copy-done.4, bf16[384,1536]{1,0:T(8,128)(2,1)S(1)} %copy-done, bf16[384,1536]{1,0:T(8,128)(2,1)S(1)} %collective-permute-done.4.refs_1_, bf16[384,1536]{1,0:T(8,128)(2,1)S(1)} %collective-permute-done.5.refs_2_, ...), custom_call_target="tpu_custom_call" | custom-call | tf_op jit(solution)/shard_map/finish/pallas_call | solution.py:242
  (9 shorter events, 0.0 us)
Async XLA Ops:
  0.0 61.2 %collective-permute-start.4 = (bf16[384,1536]{1,0:T(8,128)(2,1)}, bf16[384,1536]{1,0:T(8,128)(2,1)S(1)}, u32[]{:S(2)}, u32[]{:S(2)}) collective-permute-start(bf16[384,1536]{1,0:T(8,128)(2,1)} %refs_0_.1), channel_id=1, source_target_pairs={{0,8},{1,17},{2,10},{3,19},{4,12},{5,21},{6,14},{7,23},{8,0},{9,25... | collective-permute-start | bytes 3538952 | tf_op jit(solution)/shard_map/ppermute | solution.py:252
  2.9 45.9 %copy-start.1 = (bf16[1536,384]{1,0:T(8,128)(2,1)S(1)}, bf16[1536,384]{1,0:T(8,128)(2,1)}, u32[]{:S(2)}) copy-start(bf16[1536,384]{1,0:T(8,128)(2,1)} %wq.1) | copy-start | bytes 3538948
  2.9 45.9 %copy-start.2 = (bf16[1536,384]{1,0:T(8,128)(2,1)S(1)}, bf16[1536,384]{1,0:T(8,128)(2,1)}, u32[]{:S(2)}) copy-start(bf16[1536,384]{1,0:T(8,128)(2,1)} %wk.1) | copy-start | bytes 3538948
  2.9 45.9 %copy-start.3 = (bf16[1536,384]{1,0:T(8,128)(2,1)S(1)}, bf16[1536,384]{1,0:T(8,128)(2,1)}, u32[]{:S(2)}) copy-start(bf16[1536,384]{1,0:T(8,128)(2,1)} %wv.1) | copy-start | bytes 3538948
  48.8 17.2 %copy-start.5 = (s32[4]{0:T(128)S(1)}, s32[4]{0:T(128)}, u32[]{:S(2)}) copy-start(s32[4]{0:T(128)} %slide_tiles.1) | copy-start | bytes 52
  50.4 5.1 %collective-permute-start = (bf16[432,128]{1,0:T(8,128)(2,1)S(1)}, bf16[432,128]{1,0:T(8,128)(2,1)S(1)}, u32[]{:S(2)}, u32[]{:S(2)}) collective-permute-start(bf16[432,128]{1,0:T(8,128)(2,1)S(1)} %get-tuple-element.11), channel_id=1, source_target_pairs={{0,2},{1,3},{2,0},{3,1},{4,6},{5,7},{6,4},{7,5},{8,10},{9,11},{10,... | collective-permute-start | bytes 331784 | tf_op jit(solution)/shard_map/ppermute | solution.py:274
  52.0 7.9 %collective-permute-start.1 = (bf16[432,128]{1,0:T(8,128)(2,1)S(1)}, bf16[432,128]{1,0:T(8,128)(2,1)S(1)}, u32[]{:S(2)}, u32[]{:S(2)}) collective-permute-start(bf16[432,128]{1,0:T(8,128)(2,1)S(1)} %get-tuple-element.12), channel_id=1, source_target_pairs={{0,4},{1,5},{2,6},{3,7},{4,0},{5,1},{6,2},{7,3},{8,12},{9,13},{10,... | collective-permute-start | bytes 331784 | tf_op jit(solution)/shard_map/ppermute | solution.py:274
  54.6 6.6 %collective-permute-start.2 = (bf16[432,128]{1,0:T(8,128)(2,1)S(1)}, bf16[432,128]{1,0:T(8,128)(2,1)S(1)}, u32[]{:S(2)}, u32[]{:S(2)}) collective-permute-start(bf16[432,128]{1,0:T(8,128)(2,1)S(1)} %get-tuple-element.13), channel_id=1, source_target_pairs={{0,6},{1,7},{2,4},{3,5},{4,2},{5,3},{6,0},{7,1},{8,14},{9,15},{10,... | collective-permute-start | bytes 331784 | tf_op jit(solution)/shard_map/ppermute | solution.py:274
  61.2 22.1 %copy-start = (bf16[384,1536]{1,0:T(8,128)(2,1)S(1)}, bf16[384,1536]{1,0:T(8,128)(2,1)}, u32[]{:S(2)}) copy-start(bf16[384,1536]{1,0:T(8,128)(2,1)} %refs_0_.1) | copy-start | bytes 3538948
  61.2 22.1 %copy-start.4 = (bf16[48,1536]{1,0:T(8,128)(2,1)S(1)}, bf16[48,1536]{1,0:T(8,128)(2,1)}, u32[]{:S(2)}) copy-start(bf16[48,1536]{1,0:T(8,128)(2,1)} %encode.1.emb) | copy-start | bytes 442372
  61.2 22.1 %collective-permute-start.6 = (bf16[384,1536]{1,0:T(8,128)(2,1)S(1)}, bf16[384,1536]{1,0:T(8,128)(2,1)S(1)}, u32[]{:S(2)}, u32[]{:S(2)}) collective-permute-start(bf16[384,1536]{1,0:T(8,128)(2,1)S(1)} %collective-permute-done.4.refs_1_), channel_id=1, source_target_pairs={{0,16},{1,9},{2,18},{3,11},{4,20},{5,13},{6,22},{7,15},{8,24},{9,1... | collective-permute-start | bytes 3538952 | tf_op jit(solution)/shard_map/ppermute | solution.py:252
  62.6 20.6 %collective-permute-start.5 = (bf16[384,1536]{1,0:T(8,128)(2,1)S(1)}, bf16[384,1536]{1,0:T(8,128)(2,1)S(1)}, u32[]{:S(2)}, u32[]{:S(2)}) collective-permute-start(bf16[384,1536]{1,0:T(8,128)(2,1)S(1)} %collective-permute-done.4.refs_1_), channel_id=1, source_target_pairs={{0,1},{1,0},{2,3},{3,2},{4,5},{5,4},{6,7},{7,6},{8,9},{9,8},{10,11... | collective-permute-start | bytes 3538952 | tf_op jit(solution)/shard_map/ppermute | solution.py:277
  62.9 3.2 %collective-permute-start.3 = (bf16[768,256]{1,0:T(8,128)(2,1)S(1)}, bf16[768,256]{1,0:T(8,128)(2,1)S(1)}, u32[]{:S(2)}, u32[]{:S(2)}) collective-permute-start(bf16[768,256]{1,0:T(8,128)(2,1)S(1)} %unpack.1.refs_4_), channel_id=1, source_target_pairs={{0,1},{1,0},{2,3},{3,2},{4,5},{5,4},{6,7},{7,6},{8,9},{9,8},{10,11... | collective-permute-start | bytes 1179656 | tf_op jit(solution)/shard_map/ppermute | solution.py:284

commit v4 on v3

--- a/solution.py
+++ b/solution.py
@@ -14,7 +14,8 @@
 LANES = 128
 F32 = jnp.float32
 BF16 = jnp.bfloat16
-GROUP = 8
+GROUP = 16
+PART = 8
 
 
 def dot(a, b):
@@ -28,78 +29,154 @@
     return left, rows, right
 
 
-def bottleneck(x, wr, ws, we, waits):
-    total = x.shape[0]
-    count = total // (SIDE * SIDE)
+def row_combinations(d):
+    even, odd = d[4] - 4.0 * d[2], d[3] - 4.0 * d[1]
+    even2, odd2 = d[4] - d[2], 2.0 * (d[3] - d[1])
+    return (
+        d[0] - 1.25 * d[2] + 0.25 * d[4],
+        even + odd,
+        even - odd,
+        even2 + odd2,
+        even2 - odd2,
+        4.0 * d[1] - 5.0 * d[3] + d[5],
+    )
+
+
+def tap_combinations(g):
+    near, far = g[0] + g[2], g[0] + g[2] * 4
+    double = g[1] * 2
+    return near + g[1], near - g[1], far + double, far - double
+
+
+def four_rows(m):
+    near, near_odd = (m[1] + m[2]) * (-1 / 6), (m[1] - m[2]) * (-1 / 6)
+    far, far_odd = (m[3] + m[4]) * (1 / 24), (m[3] - m[4]) * (1 / 24)
+    return (
+        m[0] + near + far,
+        near_odd + 2.0 * far_odd,
+        near + 4.0 * far,
+        near_odd + 8.0 * far_odd + m[5],
+    )
+
+
+def encode_kernel(
+    x_hbm, wr_hbm, ws_hbm, we_hbm, wm_hbm, emb,
+    x, wr, ws, we, wm, mixed_taps, reduced, products, pooled, x_sems, tap_sems, sems,
+):
+    step = pl.program_id(0)
+    count, c = pooled.shape
+    area = SIDE * SIDE
     mid = wr.shape[1]
-    band = count * SIDE
-    waits[0]()
-    reduced = jnp.maximum(dot(x, wr[...]), 0.0)
-    reduced = reduced.reshape(count, SIDE, SIDE, mid).swapaxes(0, 1).reshape(band, SIDE, mid)
-    taps = jnp.concatenate([p.reshape(total, mid).astype(BF16) for p in neighbours(reduced)], axis=1)
-    waits[1]()
-    edge = jnp.zeros((band, mid), F32)
-    summed = dot(taps, ws[1])
-    summed = summed + jnp.concatenate([edge, dot(taps[:-band], ws[0])], axis=0)
-    summed = summed + jnp.concatenate([dot(taps[band:], ws[2]), edge], axis=0)
-    spatial = jnp.maximum(summed, 0.0).reshape(SIDE, count, SIDE, mid).swapaxes(0, 1)
-    spatial = spatial.reshape(total, mid).astype(BF16)
-    waits[2]()
-    out = jnp.maximum(dot(spatial, we[...]) + x.astype(F32), 0.0)
-    return jnp.sum(out.reshape(count, SIDE * SIDE, x.shape[1]), axis=1) * (1.0 / (SIDE * SIDE))
-
-
-def encode_kernel(x, wr_hbm, ws_hbm, we_hbm, wm_hbm, emb, wr, ws, we, wm, pooled, sems):
-    step = pl.program_id(0)
-    last = pl.num_programs(0) - 1
-    copies = [
+    groups = count // GROUP
+    per = GROUP // PART
+    parts = groups * per
+    chunk = 3 * mid // parts
+
+    def x_copy(g):
+        at = pl.ds(pl.multiple_of(g * PART * area, PART * area), PART * area)
+        return pltpu.make_async_copy(x_hbm.at[at], x.at[at], x_sems.at[g])
+
+    def tap_copy(g):
+        at = pl.ds(pl.multiple_of(g * chunk, chunk), chunk)
+        return pltpu.make_async_copy(ws_hbm.at[:, at], ws.at[:, at], tap_sems.at[g])
+
+    wr_copy, we_copy, wm_copy = (
         pltpu.make_async_copy(src, dst, sems.at[i])
-        for i, (src, dst) in enumerate(((wr_hbm, wr), (ws_hbm, ws), (we_hbm, we), (wm_hbm, wm)))
-    ]
-
-    def run(waits):
-        count = x.shape[0] // (SIDE * SIDE)
-        value = bottleneck(x[...], wr, ws, we, waits)
-        pooled[pl.ds(pl.multiple_of(step * count, count), count), :] = value
+        for i, (src, dst) in enumerate(((wr_hbm, wr), (we_hbm, we), (wm_hbm, wm)))
+    )
 
     @pl.when(step == 0)
     def _():
-        for copy in copies:
-            copy.start()
-        run([copy.wait for copy in copies])
-
-    @pl.when(step > 0)
-    def _():
-        run([lambda: None] * 3)
-
-    @pl.when(step == last)
-    def _():
-        copies[3].wait()
+        x_copy(0).start()
+        wr_copy.start()
+        x_copy(1).start()
+        wr_copy.wait()
+        tap_copy(0).start()
+        tap_copy(1).start()
+
+    @pl.when(step < groups)
+    def _():
+        for i in range(per):
+            g = step * per + i
+            x_copy(g).wait()
+
+            @pl.when(g + 2 < parts)
+            def _():
+                x_copy(g + 2).start()
+                tap_copy(g + 2).start()
+
+            rows = x[pl.ds(pl.multiple_of(g * PART * area, PART * area), PART * area), :]
+            maps = jnp.maximum(dot(rows, wr[...]), 0.0).reshape(PART, SIDE, SIDE, mid)
+            reduced[:, pl.ds(pl.multiple_of(g * PART, PART), PART)] = maps.swapaxes(0, 1)
+            tap_copy(g).wait()
+            at = pl.ds(pl.multiple_of(g * chunk, chunk), chunk)
+            for k, taps in enumerate(tap_combinations([ws[dy, at, :] for dy in range(3)])):
+                mixed_taps[k, at, :] = taps
+
+    @pl.when(step == groups - 1)
+    def _():
+        we_copy.start()
+
+    @pl.when(step == groups)
+    def _():
+        wm_copy.start()
+        we_copy.wait()
+
+    @pl.when(step >= groups)
+    def _():
+        g = step - groups
+        band = GROUP * SIDE
+        maps = reduced[:, pl.ds(pl.multiple_of(g * GROUP, GROUP), GROUP)].reshape(SIDE, band, mid)
+        edge = jnp.zeros((band, mid), F32)
+        d = [edge] + [maps[i] for i in range(SIDE)] + [edge]
+        upper, lower = row_combinations(d[0:6]), row_combinations(d[4:10])
+        taps = [ws.at[0]] + [mixed_taps.at[k] for k in range(4)] + [ws.at[2]]
+        for k in range(6):
+            both = jnp.concatenate([upper[k], lower[k]], axis=0).reshape(2 * GROUP, SIDE, mid)
+            window = [p.reshape(2 * band, mid).astype(BF16) for p in neighbours(both)]
+            products[k] = dot(jnp.concatenate(window, axis=1), taps[k][...])
+        rows = four_rows([products[k, :band] for k in range(6)])
+        rows += four_rows([products[k, band:] for k in range(6)])
+        spatial = jnp.stack([jnp.maximum(r, 0.0).reshape(GROUP, SIDE, mid) for r in rows], axis=0)
+        spatial = spatial.swapaxes(0, 1).reshape(GROUP * area, mid).astype(BF16)
+        at = pl.ds(pl.multiple_of(g * GROUP * area, GROUP * area), GROUP * area)
+        out = jnp.maximum(dot(spatial, we[...]) + x[at, :].astype(F32), 0.0)
+        mean = jnp.sum(out.reshape(GROUP, area, c), axis=1) * (1.0 / area)
+        pooled[pl.ds(pl.multiple_of(g * GROUP, GROUP), GROUP), :] = mean
+
+    @pl.when(step == 2 * groups - 1)
+    def _():
+        wm_copy.wait()
         emb[...] = dot(pooled[...].astype(BF16), wm[...]).astype(BF16)
 
 
 def encode(flat, wr, ws, we, wm):
     total, c = flat.shape
     count = total // (SIDE * SIDE)
-    rows = GROUP * SIDE * SIDE
-    anywhere = pl.BlockSpec(memory_space=pl.ANY)
+    mid = wr.shape[1]
     return pl.pallas_call(
         encode_kernel,
-        grid=(count // GROUP,),
-        in_specs=[pl.BlockSpec((rows, c), lambda i: (i, 0))] + [anywhere] * 4,
+        grid=(2 * count // GROUP,),
+        in_specs=[pl.BlockSpec(memory_space=pl.ANY)] * 5,
         out_specs=pl.BlockSpec((count, wm.shape[1]), lambda i: (0, 0)),
         out_shape=jax.ShapeDtypeStruct((count, wm.shape[1]), BF16),
         scratch_shapes=[
+            pltpu.VMEM(flat.shape, BF16),
             pltpu.VMEM(wr.shape, BF16),
             pltpu.VMEM(ws.shape, BF16),
             pltpu.VMEM(we.shape, BF16),
             pltpu.VMEM(wm.shape, BF16),
+            pltpu.VMEM((4,) + ws.shape[1:], BF16),
+            pltpu.VMEM((SIDE, count, SIDE, mid), F32),
+            pltpu.VMEM((6, 2 * GROUP * SIDE, mid), F32),
             pltpu.VMEM((count, c), F32),
-            pltpu.SemaphoreType.DMA((4,)),
+            pltpu.SemaphoreType.DMA((count // PART,)),
+            pltpu.SemaphoreType.DMA((count // PART,)),
+            pltpu.SemaphoreType.DMA((3,)),
         ],
-        compiler_params=pltpu.CompilerParams(vmem_limit_bytes=56 << 20),
+        compiler_params=pltpu.CompilerParams(vmem_limit_bytes=62 << 20),
         cost_estimate=pl.CostEstimate(
-            flops=2 * total * (2 * c * wr.shape[1] + 9 * wr.shape[1] ** 2),
+            flops=2 * total * (2 * c * mid + 9 * mid**2),
             bytes_accessed=2 * (total * c + wr.size + ws.size + we.size + wm.size),
             transcendentals=0,
         ),

time: 85.2 us -> 84 us (0.986)
  Pallas kernels: 41.8 us -> 36.8 us
  local copies, waits for them, and re-layouts: 0.02 us -> 3.82 us
    pallas_call x1, Pallas kernels: 35.5 us -> 30.5 us  [encode(): pl.pallas_call(encode_kernel, grid=(2 * count // GROUP,), in_specs=[pl.Bl...]
    unnamed x12, local copies, waits for them, and re-layouts: 0.02 us -> 3.82 us
  transfers between devices with their start and end apart: 7 -> 7, of which waited for: 4 -> 4; matrix products, arithmetic and copies ran while one was open for 0% -> 0% of each run, Pallas kernels for 47% -> 42%
where the time goes in v4:
time: 84 us; the launch traced here: 83.8 us
  Pallas kernels  36.8 us (44%)
  blocking collectives  24.7 us (29%)
  starting transfers between devices  9.39 us (11%)
  waiting for transfers between devices  9.01 us (11%)
  local copies, waits for them, and re-layouts  3.82 us (5%)
    pallas_call x1, Pallas kernels, encode(): pl.pallas_call(encode_kernel, grid=(2 * count // GROUP,), in_specs=[pl.Bl...  30.5 us
    all_to_all x1, blocking collectives, shards(): lax.all_to_all(attended, ('tile', 'blk'), 0, 0, axis_index_groups=groups,...  14.3 us
    all_gather x1, blocking collectives, shards(): gathered = lax.all_gather(emb, 'tile', axis=0, tiled=True)  10.3 us
    ppermute x3, waiting for transfers between devices, shards(): own.append(lax.ppermute(mine[e], 'blk', pairs))  6.39 us
    ppermute x3, starting transfers between devices, shards(): own.append(lax.ppermute(mine[e], 'blk', pairs))  4.45 us
    ppermute x2, starting transfers between devices, fetch(): return lax.ppermute(x, ('tile', 'blk'), pairs)  4.36 us
    unnamed x12, local copies, waits for them, and re-layouts  3.82 us
    pallas_call x1, Pallas kernels, attend(): pl.pallas_call(functools.partial(attend_kernel, heads, spread_of, tiles_o...  2.92 us
  transfers between devices with their start and end apart: 7, of which 4 were waited for; matrix products, arithmetic and copies ran while one was open for 0% of the time, Pallas kernels for 42%

profile of v4, /device:TPU:0, one launch (start us, length us, event | category | flops | bytes accessed | tf_op | source)
XLA Modules:
  0.0 83.8 jit_solution(7101295068874557196)
XLA Ops:
  0.0 2.9 %collective-permute-start.4 = (bf16[384,1536]{1,0:T(8,128)(2,1)}, bf16[384,1536]{1,0:T(8,128)(2,1)S(1)}, u32[]{:S(2)}, u32[]{:S(2)}) collective-permute-start(bf16[384,1536]{1,0:T(8,128)(2,1)} %refs_0_.1), channel_id=1, source_target_pairs={{0,8},{1,17},{2,10},{3,19},{4,12},{5,21},{6,14},{7,23},{8,0},{9,25... | collective-permute-start | bytes 3538952 | tf_op jit(solution)/shard_map/ppermute | solution.py:329
  2.9 30.5 %encode.1.emb = bf16[48,1536]{1,0:T(8,128)(2,1)} custom-call(bf16[3072,2048]{1,0:T(8,128)(2,1)} %bitcast.2, bf16[2048,512]{1,0:T(8,128)(2,1)} %wr_hbm.1, bf16[3,1536,512]{2,1,0:T(8,128)(2,1)} %bitcast.3, bf16[512,2048]{1,0:T(8,128)(2,1)} %we_hbm.1, bf16[2048,1536]{1,0:T(8,128)(2,1)} %wm_hbm.1), custom_call_target="tpu_custom_call" | custom-call | flops 27380416512 | bytes 27787264 | tf_op jit(solution)/shard_map/encode/pallas_call | solution.py:157
  33.5 10.3 %all_gather.3.emb = bf16[192,1536]{1,0:T(8,128)(2,1)S(1)} all-gather(bf16[48,1536]{1,0:T(8,128)(2,1)} %encode.1.emb), channel_id=1, replica_groups=mesh['tile'=4,'blk'=8] {'tile'}, dimensions={0}, use_global_device_ids=true | all-gather | bytes 737280 | tf_op jit(solution)/shard_map/all_gather | solution.py:346
  43.8 1.3 %copy-done.1 = bf16[1536,384]{1,0:T(8,128)(2,1)S(1)} copy-done((bf16[1536,384]{1,0:T(8,128)(2,1)S(1)}, bf16[1536,384]{1,0:T(8,128)(2,1)}, u32[]{:S(2)}) %copy-start.1) | copy-done | bytes 1179672
  45.0 1.3 %copy-done.2 = bf16[1536,384]{1,0:T(8,128)(2,1)S(1)} copy-done((bf16[1536,384]{1,0:T(8,128)(2,1)S(1)}, bf16[1536,384]{1,0:T(8,128)(2,1)}, u32[]{:S(2)}) %copy-start.2) | copy-done | bytes 1179672
  46.3 1.3 %copy-done.3 = bf16[1536,384]{1,0:T(8,128)(2,1)S(1)} copy-done((bf16[1536,384]{1,0:T(8,128)(2,1)S(1)}, bf16[1536,384]{1,0:T(8,128)(2,1)}, u32[]{:S(2)}) %copy-start.3) | copy-done | bytes 1179672
  47.6 1.5 %project.1 = (bf16[432,128]{1,0:T(8,128)(2,1)S(1)}, bf16[432,128]{1,0:T(8,128)(2,1)S(1)}, bf16[432,128]{1,0:T(8,128)(2,1)S(1)}, bf16[432,128]{1,0:T(8,128)(2,1)S(1)}) custom-call(bf16[192,1536]{1,0:T(8,128)(2,1)S(1)} %all_gather.3.emb, bf16[1536,384]{1,0:T(8,128)(2,1)S(1)} %copy-done.1, bf16[1536,384]{1,0:T(8,128)(2,1)S(1)} %copy-done.2, ...), custom_call_target="tpu_custom_call" | custom-call | tf_op jit(solution)/shard_map/project/pallas_call | solution.py:211
  49.1 1.6 %collective-permute-start = (bf16[432,128]{1,0:T(8,128)(2,1)S(1)}, bf16[432,128]{1,0:T(8,128)(2,1)S(1)}, u32[]{:S(2)}, u32[]{:S(2)}) collective-permute-start(bf16[432,128]{1,0:T(8,128)(2,1)S(1)} %get-tuple-element.11), channel_id=1, source_target_pairs={{0,2},{1,3},{2,0},{3,1},{4,6},{5,7},{6,4},{7,5},{8,10},{9,11},{10,... | collective-permute-start | bytes 331784 | tf_op jit(solution)/shard_map/ppermute | solution.py:351
  50.7 2.6 %collective-permute-start.1 = (bf16[432,128]{1,0:T(8,128)(2,1)S(1)}, bf16[432,128]{1,0:T(8,128)(2,1)S(1)}, u32[]{:S(2)}, u32[]{:S(2)}) collective-permute-start(bf16[432,128]{1,0:T(8,128)(2,1)S(1)} %get-tuple-element.12), channel_id=1, source_target_pairs={{0,4},{1,5},{2,6},{3,7},{4,0},{5,1},{6,2},{7,3},{8,12},{9,13},{10,... | collective-permute-start | bytes 331784 | tf_op jit(solution)/shard_map/ppermute | solution.py:351
  53.3 0.2 collective-permute-start.2
  53.6 0.7 collective-permute-done.refs_1_
  54.2 4.4 %collective-permute-done.1.refs_2_ = bf16[432,128]{1,0:T(8,128)(2,1)S(1)} collective-permute-done((bf16[432,128]{1,0:T(8,128)(2,1)S(1)}, bf16[432,128]{1,0:T(8,128)(2,1)S(1)}, u32[]{:S(2)}, u32[]{:S(2)}) %collective-permute-start.1) | collective-permute-done | bytes 110624 | tf_op jit(solution)/shard_map/ppermute | solution.py:351
  58.6 1.3 %collective-permute-done.2.refs_3_ = bf16[432,128]{1,0:T(8,128)(2,1)S(1)} collective-permute-done((bf16[432,128]{1,0:T(8,128)(2,1)S(1)}, bf16[432,128]{1,0:T(8,128)(2,1)S(1)}, u32[]{:S(2)}, u32[]{:S(2)}) %collective-permute-start.2) | collective-permute-done | bytes 110624 | tf_op jit(solution)/shard_map/ppermute | solution.py:351
  59.9 0.0 collective-permute-done.4.refs_1_
  60.0 1.4 %collective-permute-start.6 = (bf16[384,1536]{1,0:T(8,128)(2,1)S(1)}, bf16[384,1536]{1,0:T(8,128)(2,1)S(1)}, u32[]{:S(2)}, u32[]{:S(2)}) collective-permute-start(bf16[384,1536]{1,0:T(8,128)(2,1)S(1)} %collective-permute-done.4.refs_1_), channel_id=1, source_target_pairs={{0,16},{1,9},{2,18},{3,11},{4,20},{5,13},{6,22},{7,15},{8,24},{9,1... | collective-permute-start | bytes 3538952 | tf_op jit(solution)/shard_map/ppermute | solution.py:329
  61.4 0.0 collective-permute-start.5
  61.4 0.2 unpack.1.refs_4_
  61.6 0.6 collective-permute-start.3
  62.2 2.6 %collective-permute-done.3.refs_5_ = bf16[768,256]{1,0:T(8,128)(2,1)S(1)} collective-permute-done((bf16[768,256]{1,0:T(8,128)(2,1)S(1)}, bf16[768,256]{1,0:T(8,128)(2,1)S(1)}, u32[]{:S(2)}, u32[]{:S(2)}) %collective-permute-start.3) | collective-permute-done | bytes 393248 | tf_op jit(solution)/shard_map/ppermute | solution.py:361
  64.8 2.9 %attend.1 = bf16[16,48,128]{2,1,0:T(8,128)(2,1)S(1)} custom-call(s32[4]{0:T(128)S(1)} %copy-done.5, bf16[432,128]{1,0:T(8,128)(2,1)S(1)} %get-tuple-element.10.refs_0_, bf16[432,128]{1,0:T(8,128)(2,1)S(1)} %collective-permute-done.refs_1_, bf16[432,128]{1,0:T(8,128)(2,1)S(1)} %collective-permute-done.1.refs_2_, ...), custom_call_target="tpu_custom_call" | custom-call | tf_op jit(solution)/shard_map/attend/pallas_call | solution.py:297
  67.7 14.3 %all_to_all.5.parts = bf16[16,48,128]{2,1,0:T(8,128)(2,1)S(1)} all-to-all(bf16[16,48,128]{2,1,0:T(8,128)(2,1)S(1)} %attend.1), channel_id=1, replica_groups={{0,2,4,6,8,10,12,14,16,18,20,22,24,26,28,30},{1,3,5,7,9,11,13,15,17,19,..., dimensions={0} | all-to-all | bytes 393216 | tf_op jit(solution)/shard_map/all_to_all | solution.py:367
  82.1 0.0 collective-permute-done.6.refs_3_
  82.1 0.0 collective-permute-done.5.refs_2_
  82.1 1.7 %finish.1 = bf16[48,1536]{1,0:T(8,128)(2,1)} custom-call(bf16[16,48,128]{2,1,0:T(8,128)(2,1)S(1)} %all_to_all.5.parts, bf16[48,1536]{1,0:T(8,128)(2,1)S(1)} %copy-done.4, bf16[384,1536]{1,0:T(8,128)(2,1)S(1)} %copy-done, bf16[384,1536]{1,0:T(8,128)(2,1)S(1)} %collective-permute-done.4.refs_1_, bf16[384,1536]{1,0:T(8,128)(2,1)S(1)} %collective-permute-done.5.refs_2_, ...), custom_call_target="tpu_custom_call" | custom-call | tf_op jit(solution)/shard_map/finish/pallas_call | solution.py:319
  (9 shorter events, 0.0 us)
Async XLA Ops:
  0.0 59.9 %collective-permute-start.4 = (bf16[384,1536]{1,0:T(8,128)(2,1)}, bf16[384,1536]{1,0:T(8,128)(2,1)S(1)}, u32[]{:S(2)}, u32[]{:S(2)}) collective-permute-start(bf16[384,1536]{1,0:T(8,128)(2,1)} %refs_0_.1), channel_id=1, source_target_pairs={{0,8},{1,17},{2,10},{3,19},{4,12},{5,21},{6,14},{7,23},{8,0},{9,25... | collective-permute-start | bytes 3538952 | tf_op jit(solution)/shard_map/ppermute | solution.py:329
  43.8 1.3 %copy-start.1 = (bf16[1536,384]{1,0:T(8,128)(2,1)S(1)}, bf16[1536,384]{1,0:T(8,128)(2,1)}, u32[]{:S(2)}) copy-start(bf16[1536,384]{1,0:T(8,128)(2,1)} %wq.1) | copy-start | bytes 3538948
  45.0 1.3 %copy-start.2 = (bf16[1536,384]{1,0:T(8,128)(2,1)S(1)}, bf16[1536,384]{1,0:T(8,128)(2,1)}, u32[]{:S(2)}) copy-start(bf16[1536,384]{1,0:T(8,128)(2,1)} %wk.1) | copy-start | bytes 3538948
  46.3 1.3 %copy-start.3 = (bf16[1536,384]{1,0:T(8,128)(2,1)S(1)}, bf16[1536,384]{1,0:T(8,128)(2,1)}, u32[]{:S(2)}) copy-start(bf16[1536,384]{1,0:T(8,128)(2,1)} %wv.1) | copy-start | bytes 3538948
  47.6 17.2 %copy-start.5 = (s32[4]{0:T(128)S(1)}, s32[4]{0:T(128)}, u32[]{:S(2)}) copy-start(s32[4]{0:T(128)} %slide_tiles.1) | copy-start | bytes 52
  49.1 5.1 %collective-permute-start = (bf16[432,128]{1,0:T(8,128)(2,1)S(1)}, bf16[432,128]{1,0:T(8,128)(2,1)S(1)}, u32[]{:S(2)}, u32[]{:S(2)}) collective-permute-start(bf16[432,128]{1,0:T(8,128)(2,1)S(1)} %get-tuple-element.11), channel_id=1, source_target_pairs={{0,2},{1,3},{2,0},{3,1},{4,6},{5,7},{6,4},{7,5},{8,10},{9,11},{10,... | collective-permute-start | bytes 331784 | tf_op jit(solution)/shard_map/ppermute | solution.py:351
  50.7 7.9 %collective-permute-start.1 = (bf16[432,128]{1,0:T(8,128)(2,1)S(1)}, bf16[432,128]{1,0:T(8,128)(2,1)S(1)}, u32[]{:S(2)}, u32[]{:S(2)}) collective-permute-start(bf16[432,128]{1,0:T(8,128)(2,1)S(1)} %get-tuple-element.12), channel_id=1, source_target_pairs={{0,4},{1,5},{2,6},{3,7},{4,0},{5,1},{6,2},{7,3},{8,12},{9,13},{10,... | collective-permute-start | bytes 331784 | tf_op jit(solution)/shard_map/ppermute | solution.py:351
  53.3 6.6 %collective-permute-start.2 = (bf16[432,128]{1,0:T(8,128)(2,1)S(1)}, bf16[432,128]{1,0:T(8,128)(2,1)S(1)}, u32[]{:S(2)}, u32[]{:S(2)}) collective-permute-start(bf16[432,128]{1,0:T(8,128)(2,1)S(1)} %get-tuple-element.13), channel_id=1, source_target_pairs={{0,6},{1,7},{2,4},{3,5},{4,2},{5,3},{6,0},{7,1},{8,14},{9,15},{10,... | collective-permute-start | bytes 331784 | tf_op jit(solution)/shard_map/ppermute | solution.py:351
  60.0 22.1 %copy-start = (bf16[384,1536]{1,0:T(8,128)(2,1)S(1)}, bf16[384,1536]{1,0:T(8,128)(2,1)}, u32[]{:S(2)}) copy-start(bf16[384,1536]{1,0:T(8,128)(2,1)} %refs_0_.1) | copy-start | bytes 3538948
  60.0 22.1 %copy-start.4 = (bf16[48,1536]{1,0:T(8,128)(2,1)S(1)}, bf16[48,1536]{1,0:T(8,128)(2,1)}, u32[]{:S(2)}) copy-start(bf16[48,1536]{1,0:T(8,128)(2,1)} %encode.1.emb) | copy-start | bytes 442372
  60.0 22.1 %collective-permute-start.6 = (bf16[384,1536]{1,0:T(8,128)(2,1)S(1)}, bf16[384,1536]{1,0:T(8,128)(2,1)S(1)}, u32[]{:S(2)}, u32[]{:S(2)}) collective-permute-start(bf16[384,1536]{1,0:T(8,128)(2,1)S(1)} %collective-permute-done.4.refs_1_), channel_id=1, source_target_pairs={{0,16},{1,9},{2,18},{3,11},{4,20},{5,13},{6,22},{7,15},{8,24},{9,1... | collective-permute-start | bytes 3538952 | tf_op jit(solution)/shard_map/ppermute | solution.py:329
  61.4 20.7 %collective-permute-start.5 = (bf16[384,1536]{1,0:T(8,128)(2,1)S(1)}, bf16[384,1536]{1,0:T(8,128)(2,1)S(1)}, u32[]{:S(2)}, u32[]{:S(2)}) collective-permute-start(bf16[384,1536]{1,0:T(8,128)(2,1)S(1)} %collective-permute-done.4.refs_1_), channel_id=1, source_target_pairs={{0,1},{1,0},{2,3},{3,2},{4,5},{5,4},{6,7},{7,6},{8,9},{9,8},{10,11... | collective-permute-start | bytes 3538952 | tf_op jit(solution)/shard_map/ppermute | solution.py:354
  61.6 3.2 %collective-permute-start.3 = (bf16[768,256]{1,0:T(8,128)(2,1)S(1)}, bf16[768,256]{1,0:T(8,128)(2,1)S(1)}, u32[]{:S(2)}, u32[]{:S(2)}) collective-permute-start(bf16[768,256]{1,0:T(8,128)(2,1)S(1)} %unpack.1.refs_4_), channel_id=1, source_target_pairs={{0,1},{1,0},{2,3},{3,2},{4,5},{5,4},{6,7},{7,6},{8,9},{9,8},{10,11... | collective-permute-start | bytes 1179656 | tf_op jit(solution)/shard_map/ppermute | solution.py:361

commit v5 on v4

--- a/solution.py
+++ b/solution.py
@@ -61,7 +61,7 @@
 
 def encode_kernel(
     x_hbm, wr_hbm, ws_hbm, we_hbm, wm_hbm, emb,
-    x, wr, ws, we, wm, mixed_taps, reduced, products, pooled, x_sems, tap_sems, sems,
+    x, wr, ws, we, mixed_taps, reduced, products, pooled, x_sems, tap_sems, sems,
 ):
     step = pl.program_id(0)
     count, c = pooled.shape
@@ -80,6 +80,7 @@
         at = pl.ds(pl.multiple_of(g * chunk, chunk), chunk)
         return pltpu.make_async_copy(ws_hbm.at[:, at], ws.at[:, at], tap_sems.at[g])
 
+    wm = x.at[: wm_hbm.shape[0], : wm_hbm.shape[1]]
     wr_copy, we_copy, wm_copy = (
         pltpu.make_async_copy(src, dst, sems.at[i])
         for i, (src, dst) in enumerate(((wr_hbm, wr), (we_hbm, we), (wm_hbm, wm)))
@@ -119,8 +120,11 @@
 
     @pl.when(step == groups)
     def _():
+        we_copy.wait()
+
+    @pl.when(step == 2 * groups - 1)
+    def _():
         wm_copy.start()
-        we_copy.wait()
 
     @pl.when(step >= groups)
     def _():
@@ -153,6 +157,7 @@
 def encode(flat, wr, ws, we, wm):
     total, c = flat.shape
     count = total // (SIDE * SIDE)
+    assert wm.shape[0] <= total - GROUP * SIDE * SIDE and wm.shape[1] <= c
     mid = wr.shape[1]
     return pl.pallas_call(
         encode_kernel,
@@ -165,7 +170,6 @@
             pltpu.VMEM(wr.shape, BF16),
             pltpu.VMEM(ws.shape, BF16),
             pltpu.VMEM(we.shape, BF16),
-            pltpu.VMEM(wm.shape, BF16),
             pltpu.VMEM((4,) + ws.shape[1:], BF16),
             pltpu.VMEM((SIDE, count, SIDE, mid), F32),
             pltpu.VMEM((6, 2 * GROUP * SIDE, mid), F32),
@@ -174,7 +178,7 @@
             pltpu.SemaphoreType.DMA((count // PART,)),
             pltpu.SemaphoreType.DMA((3,)),
         ],
-        compiler_params=pltpu.CompilerParams(vmem_limit_bytes=62 << 20),
+        compiler_params=pltpu.CompilerParams(vmem_limit_bytes=54 << 20),
         cost_estimate=pl.CostEstimate(
             flops=2 * total * (2 * c * mid + 9 * mid**2),
             bytes_accessed=2 * (total * c + wr.size + ws.size + we.size + wm.size),
@@ -248,90 +252,153 @@
     )(*own)
 
 
-def attend_kernel(heads, spread_of, tiles_of, slide_tiles, *refs):
-    own = refs[:heads]
-    sets = refs[heads : heads + spread_of]
-    out = refs[heads + spread_of]
-    blk = lax.axis_index("blk")
-    a, c = blk // spread_of, lax.rem(blk, spread_of)
-    length = sets[0].shape[0] // heads
+class Slides:
+    def __init__(self, slide_tiles, heads, spread_of, length):
+        blk = lax.axis_index("blk")
+        self.a, self.c = blk // spread_of, lax.rem(blk, spread_of)
+        self.heads, self.spread_of, self.length = heads, spread_of, length
+        first = slide_tiles[0]
+        second = first + slide_tiles[1]
+        self.ends = (first, second, second + slide_tiles[2])
+
+    def of(self, e, f, dim):
+        shape = (self.length, 1) if dim == 0 else (1, self.length)
+        start = ((self.a ^ e) * self.spread_of + (self.c ^ f)) * self.length
+        pos = lax.broadcasted_iota(jnp.int32, shape, dim) + start
+        return sum((pos >= end).astype(jnp.int32) for end in self.ends)
+
+    def of_keys(self, f):
+        return jnp.concatenate([self.of(e, f, 1) for e in range(self.heads)], axis=1)
+
+
+SCALE = math.log2(math.e) / math.sqrt(HD)
+
+
+def masked_scores(query, keys, query_slide, key_slide):
+    scores = lax.dot_general(query, keys, (((1,), (1,)), ((), ())), preferred_element_type=F32)
+    return jnp.where(query_slide == key_slide, scores, -1e30)
+
+
+def attend_own_kernel(heads, spread_of, slide_tiles, *refs):
+    own, key_value, out = refs[:heads], refs[heads], refs[heads + 1]
+    length = key_value.shape[0] // heads
+    slides = Slides(slide_tiles, heads, spread_of, length)
+    key_slide = slides.of_keys(0)
+    lane = lax.broadcasted_iota(jnp.int32, (length, LANES), 1)
+    for e in range(heads):
+        scores = masked_scores(own[e][:length], key_value[:, :LANES], slides.of(e, 0, 0), key_slide)
+        top = jnp.max(scores, axis=1, keepdims=True)
+        product = dot(jnp.exp2((scores - top) * SCALE).astype(BF16), key_value[:, LANES:])
+        out[e] = jnp.where(lane == HD + 1, top, product)
+
+
+def attend_others_kernel(heads, spread_of, slide_tiles, *refs):
+    own, partial, others = refs[:heads], refs[heads], refs[heads + 1 : heads + spread_of]
+    outs = refs[heads + spread_of :]
+    length = partial.shape[1]
+    slides = Slides(slide_tiles, heads, spread_of, length)
+    key_slides = [slides.of_keys(f) for f in range(1, spread_of)]
+    quarter = length // 4
+    for e in range(heads):
+        query_slide = slides.of(e, 0, 0)
+        scores = [
+            masked_scores(own[e][:length], other[:, :LANES], query_slide, key_slide)
+            for other, key_slide in zip(others, key_slides)
+        ]
+        before = partial[e]
+        top_before = before[:, HD + 1 : HD + 2]
+        top = functools.reduce(
+            jnp.maximum, [jnp.max(s, axis=1, keepdims=True) for s in scores], top_before
+        )
+        product = before * jnp.exp2((top_before - top) * SCALE)
+        for other, s in zip(others, scores):
+            product = product + dot(jnp.exp2((s - top) * SCALE).astype(BF16), other[:, LANES:])
+        result = product[:, :HD] / product[:, HD : HD + 1]
+        rest = result[3 * quarter :]
+        rest = jnp.concatenate([rest[:, i * THIRD : (i + 1) * THIRD] for i in range(3)], axis=0)
+        outs[e][...] = jnp.concatenate([result[: 3 * quarter], rest], axis=1).astype(BF16)
+
+
+def attend(slide_tiles, own, key_value, exchange):
+    heads = len(own)
+    length = key_value.shape[0] // heads
+    others = exchange(key_value)
+    spread_of = len(others) + 1
+    small = pl.BlockSpec(memory_space=pltpu.SMEM)
+    whole = pl.BlockSpec(memory_space=pltpu.VMEM)
+    params = pltpu.CompilerParams(vmem_limit_bytes=40 << 20)
+    rows = length * heads
+    cost = pl.CostEstimate(
+        flops=4 * rows * rows * LANES, bytes_accessed=6 * rows * LANES, transcendentals=rows * rows
+    )
+    partial = pl.pallas_call(
+        functools.partial(attend_own_kernel, heads, spread_of),
+        in_specs=[small] + [whole] * (heads + 1),
+        out_specs=whole,
+        out_shape=jax.ShapeDtypeStruct((heads, length, LANES), F32),
+        compiler_params=params,
+        cost_estimate=cost,
+        name="attend_own",
+    )(slide_tiles, *own, key_value)
+    return pl.pallas_call(
+        functools.partial(attend_others_kernel, heads, spread_of),
+        in_specs=[small] + [whole] * (heads + spread_of),
+        out_specs=[whole] * heads,
+        out_shape=[jax.ShapeDtypeStruct((length * 3 // 4, LANES), BF16)] * heads,
+        compiler_params=params,
+        name="attend_others",
+    )(slide_tiles, *own, partial, *others)
+
+
+def partial_out_kernel(heads, tiles_of, spread_of, *refs):
+    parts, w_out, outs = refs[:heads], refs[heads], refs[heads + 1 : heads + 1 + tiles_of]
+    sorted_heads, sums = refs[heads + 1 + tiles_of :]
+    a, t = lax.axis_index("blk") // spread_of, lax.axis_index("tile")
+    quarter = parts[0].shape[0] // 3
+    for e in range(heads):
+        packed = parts[e][...].astype(F32)
+        tail = packed[:, HD:]
+        rest = jnp.concatenate([tail[i * quarter : (i + 1) * quarter] for i in range(3)], axis=1)
+        sorted_heads[a ^ e] = jnp.concatenate([packed[:, :HD], rest], axis=0)
+    attended = jnp.concatenate([sorted_heads[h] for h in range(heads)], axis=1).astype(BF16)
+    product = dot(attended, w_out[...])
+    count = product.shape[0] // tiles_of
+    for block in range(tiles_of):
+        sums[block] = product[block * count : (block + 1) * count]
+    for d in range(tiles_of):
+        outs[d][...] = sums[t ^ d].astype(outs[d].dtype)
+
+
+def partial_out(parts, w_out, tiles_of, spread_of):
+    heads, width = len(parts), w_out.shape[1]
+    length = parts[0].shape[0] * 4 // 3
     count = length // tiles_of
-    ends = [slide_tiles[0], slide_tiles[0] + slide_tiles[1]]
-    ends.append(ends[1] + slide_tiles[2])
-
-    def slide_of(shape, dim, start):
-        pos = lax.broadcasted_iota(jnp.int32, shape, dim) + start
-        return sum((pos >= end).astype(jnp.int32) for end in ends)
-
-    key_slides = [
-        jnp.concatenate(
-            [slide_of((1, length), 1, ((a ^ e) * spread_of + (c ^ f)) * length) for e in range(heads)],
-            axis=1,
-        )
-        for f in range(spread_of)
-    ]
-    scale = math.log2(math.e) / math.sqrt(HD)
-    for e in range(heads):
-        query = own[e][:length]
-        query_slide = slide_of((length, 1), 0, ((a ^ e) * spread_of + c) * length)
-        scores = []
-        for f in range(spread_of):
-            part = lax.dot_general(
-                query, sets[f][:, :LANES], (((1,), (1,)), ((), ())), preferred_element_type=F32
-            )
-            scores.append(jnp.where(query_slide == key_slides[f], part, -1e30))
-        top = functools.reduce(jnp.maximum, [jnp.max(s, axis=1, keepdims=True) for s in scores])
-        product = sum(
-            dot(jnp.exp2((s - top) * scale).astype(BF16), sets[f][:, LANES:])
-            for f, s in enumerate(scores)
-        )
-        result = (product / product[:, HD : HD + 1]).astype(BF16)
-        for t in range(tiles_of):
-            out[t * heads + (a ^ e)] = result[t * count : (t + 1) * count]
-
-
-def attend(slide_tiles, own, sets, tiles_of):
-    heads, spread_of = len(own), len(sets)
-    length = sets[0].shape[0] // heads
     whole = pl.BlockSpec(memory_space=pltpu.VMEM)
     return pl.pallas_call(
-        functools.partial(attend_kernel, heads, spread_of, tiles_of),
-        in_specs=[pl.BlockSpec(memory_space=pltpu.SMEM)] + [whole] * (heads + spread_of),
-        out_specs=whole,
-        out_shape=jax.ShapeDtypeStruct((tiles_of * heads, length // tiles_of, LANES), BF16),
-        compiler_params=pltpu.CompilerParams(vmem_limit_bytes=40 << 20),
-        name="attend",
-    )(slide_tiles, *own, *sets)
-
-
-def finish_kernel(heads, order, parts, emb, *refs):
-    out = refs[-1]
+        functools.partial(partial_out_kernel, heads, tiles_of, spread_of),
+        in_specs=[whole] * (heads + 1),
+        out_specs=[whole] * tiles_of,
+        out_shape=[jax.ShapeDtypeStruct((count, width), F32 if d == 0 else BF16) for d in range(tiles_of)],
+        scratch_shapes=[pltpu.VMEM((heads, length, HD), F32), pltpu.VMEM((tiles_of, count, width), F32)],
+        compiler_params=pltpu.CompilerParams(vmem_limit_bytes=24 << 20),
+        name="partial_out",
+    )(*parts, w_out)
+
+
+def finish_kernel(emb, *refs):
     total = emb[...].astype(F32)
-    for where, w in zip(order(), refs[:-1]):
-        attended = jnp.concatenate(
-            [parts[where * heads + h][:, :HD].astype(F32) for h in range(w.shape[0] // HD)], axis=1
-        )
-        total = total + dot(attended.astype(BF16), w[...])
-    out[...] = total.astype(BF16)
-
-
-def finish(parts, emb, w_outs, heads, order):
-    return pl.pallas_call(
-        functools.partial(finish_kernel, heads, order),
+    for ref in refs[:-1]:
+        total = total + ref[...].astype(F32)
+    refs[-1][...] = total.astype(BF16)
+
+
+def finish(emb, sums):
+    return pl.pallas_call(
+        finish_kernel,
         out_shape=jax.ShapeDtypeStruct(emb.shape, BF16),
         compiler_params=pltpu.CompilerParams(vmem_limit_bytes=24 << 20),
         name="finish",
-    )(parts, emb, *w_outs)
-
-
-def fetch(x, flip, tiles_of, blks):
-    pairs = [(t * blks + b, (t ^ flip[b % 2]) * blks + b) for t in range(tiles_of) for b in range(blks)]
-    return lax.ppermute(x, ("tile", "blk"), pairs)
-
-
-def tile_order():
-    t, core = lax.axis_index("tile"), lax.rem(lax.axis_index("blk"), 2)
-    return t, t ^ (1 + core), t ^ (2 - core), t ^ 3
+    )(emb, *sums)
 
 
 def shards(tiles_of, blks, tiles, wr, ws, we, wm, wq, wk, wv, wo, slide_tiles):
@@ -340,32 +407,22 @@
     mid = wr.shape[1]
     heads = wq.shape[1] // HD
     spread_of = blks // heads
-    relay = tiles_of == 4
-    first = fetch(wo, (1, 2), tiles_of, blks) if relay else lax.all_gather(wo, "tile", axis=0, tiled=True)
+
+    def along(x, axis, size, step):
+        return lax.ppermute(x, axis, [(i, i ^ step) for i in range(size)])
+
+    def over_heads(blocks):
+        return [blocks[0]] + [along(blocks[e], "blk", blks, e * spread_of) for e in range(1, heads)]
+
     emb = encode(flat, wr, ws.reshape(3, 3 * mid, mid), we, wm)
     gathered = lax.all_gather(emb, "tile", axis=0, tiled=True)
-    mine = project(gathered, wq, wk, wv, heads, spread_of)
-    own = [mine[0]]
-    for e in range(1, heads):
-        pairs = [(i, i ^ (e * spread_of)) for i in range(blks)]
-        own.append(lax.ppermute(mine[e], "blk", pairs))
-    if relay:
-        first, *_ = lax.optimization_barrier((first, *own))
-        second = lax.ppermute(first, "blk", [(b, b ^ 1) for b in range(blks)])
-        third = fetch(first, (2, 1), tiles_of, blks)
-        w_outs, order = [wo, first, second, third], tile_order
-    else:
-        w_outs, order = [first], lambda: (0,)
-    sets = [unpack(own)]
-    for f in range(1, spread_of):
-        sets.append(lax.ppermute(sets[0], "blk", [(i, i ^ f) for i in range(blks)]))
-    attended = attend(slide_tiles, own, sets, tiles_of)
-    groups = [
-        [t * blks + a * spread_of + c for t in range(tiles_of) for a in range(heads)]
-        for c in range(spread_of)
-    ]
-    parts = lax.all_to_all(attended, ("tile", "blk"), 0, 0, axis_index_groups=groups, tiled=True)
-    return finish(parts, emb, w_outs, heads, order)
+    own = over_heads(project(gathered, wq, wk, wv, heads, spread_of))
+    attended = attend(
+        slide_tiles, own, unpack(own), lambda x: [along(x, "blk", blks, f) for f in range(1, spread_of)]
+    )
+    sums = partial_out(over_heads(attended), wo, tiles_of, spread_of)
+    sums = [sums[0]] + [along(sums[d], "tile", tiles_of, d) for d in range(1, tiles_of)]
+    return finish(emb, sums)
 
 
 def solution(mesh):

time: 84 us -> 81.6 us (0.971)
  blocking collectives: 24.7 us -> 12.4 us
  waiting for transfers between devices: 9.01 us -> 16.8 us
  local copies, waits for them, and re-layouts: 3.82 us -> 0.03 us
  starting transfers between devices: 9.39 us -> 12.5 us
  Pallas kernels: 36.8 us -> 39.5 us
    all_to_all x1 -> x0, blocking collectives: 14.3 us -> none  [shards(): lax.all_to_all(attended, ('tile', 'blk'), 0, 0, axis_index_groups=groups,...]
    ppermute x7 -> x10, waiting for transfers between devices: 9.01 us -> 16.8 us  [along(): return lax.ppermute(x, axis, [(i, i ^ step) for i in range(size)])]
    unnamed x12, local copies, waits for them, and re-layouts: 3.82 us -> 0.03 us
    ppermute x7 -> x10, starting transfers between devices: 9.39 us -> 12.5 us  [along(): return lax.ppermute(x, axis, [(i, i ^ step) for i in range(size)])]
    all_gather x1, blocking collectives: 10.3 us -> 12.4 us  [shards(): gathered = lax.all_gather(emb, 'tile', axis=0, tiled=True)]
    pallas_call x2 -> x4, Pallas kernels: 4.59 us -> 6.57 us  [the longest x1 2.98 us: attend(): pl.pallas_call(functools.partial(attend_others_kernel, heads, spread_of),...]
  transfers between devices with their start and end apart: 7 -> 10, of which waited for: 4 -> 6; matrix products, arithmetic and copies ran while one was open for 0% -> 0% of each run, Pallas kernels for 42% -> 3%
where the time goes in v5:
time: 81.6 us; the launch traced here: 81.4 us
  Pallas kernels  39.5 us (48%)
  waiting for transfers between devices  16.8 us (21%)
  starting transfers between devices  12.5 us (15%)
  blocking collectives  12.4 us (15%)
    pallas_call x1, Pallas kernels, encode(): pl.pallas_call(encode_kernel, grid=(2 * count // GROUP,), in_specs=[pl.Bl...  31.2 us
    ppermute x10, waiting for transfers between devices, along(): return lax.ppermute(x, axis, [(i, i ^ step) for i in range(size)])  16.8 us
    ppermute x10, starting transfers between devices, along(): return lax.ppermute(x, axis, [(i, i ^ step) for i in range(size)])  12.5 us
    all_gather x1, blocking collectives, shards(): gathered = lax.all_gather(emb, 'tile', axis=0, tiled=True)  12.4 us
    pallas_call x1, Pallas kernels, attend(): pl.pallas_call(functools.partial(attend_others_kernel, heads, spread_of),...  2.98 us
    pallas_call x1, Pallas kernels, attend(): pl.pallas_call(functools.partial(attend_own_kernel, heads, spread_of), in...  2.14 us
  transfers between devices with their start and end apart: 10, of which 6 were waited for; matrix products, arithmetic and copies ran while one was open for 0% of the time, Pallas kernels for 3%

profile of v5, /device:TPU:0, one launch (start us, length us, event | category | flops | bytes accessed | tf_op | source)
XLA Modules:
  0.0 81.4 jit_solution(2578854119749820365)
XLA Ops:
  0.0 31.2 %encode.1.emb = bf16[48,1536]{1,0:T(8,128)(2,1)} custom-call(bf16[3072,2048]{1,0:T(8,128)(2,1)} %bitcast.2, bf16[2048,512]{1,0:T(8,128)(2,1)} %wr_hbm.1, bf16[3,1536,512]{2,1,0:T(8,128)(2,1)} %bitcast.3, bf16[512,2048]{1,0:T(8,128)(2,1)} %we_hbm.1, bf16[2048,1536]{1,0:T(8,128)(2,1)} %wm_hbm.1), custom_call_target="tpu_custom_call" | custom-call | flops 27380416512 | bytes 27787264 | tf_op jit(solution)/shard_map/encode/pallas_call | solution.py:162
  31.2 12.4 %all_gather.3.emb = bf16[192,1536]{1,0:T(8,128)(2,1)S(1)} all-gather(bf16[48,1536]{1,0:T(8,128)(2,1)} %encode.1.emb), channel_id=1, replica_groups=mesh['tile'=4,'blk'=8] {'tile'}, dimensions={0}, use_global_device_ids=true | all-gather | bytes 737280 | tf_op jit(solution)/shard_map/all_gather | solution.py:418
  43.7 1.5 %project.1 = (bf16[432,128]{1,0:T(8,128)(2,1)S(1)}, bf16[432,128]{1,0:T(8,128)(2,1)S(1)}, bf16[432,128]{1,0:T(8,128)(2,1)S(1)}, bf16[432,128]{1,0:T(8,128)(2,1)S(1)}) custom-call(bf16[192,1536]{1,0:T(8,128)(2,1)S(1)} %all_gather.3.emb, bf16[1536,384]{1,0:T(8,128)(2,1)S(1)} %copy-done.1, bf16[1536,384]{1,0:T(8,128)(2,1)S(1)} %copy-done.2, ...), custom_call_target="tpu_custom_call" | custom-call | tf_op jit(solution)/shard_map/project/pallas_call | solution.py:215
  45.3 1.6 %collective-permute-start = (bf16[432,128]{1,0:T(8,128)(2,1)S(1)}, bf16[432,128]{1,0:T(8,128)(2,1)S(1)}, u32[]{:S(2)}, u32[]{:S(2)}) collective-permute-start(bf16[432,128]{1,0:T(8,128)(2,1)S(1)} %get-tuple-element.18), channel_id=1, source_target_pairs={{0,2},{1,3},{2,0},{3,1},{4,6},{5,7},{6,4},{7,5},{8,10},{9,11},{10,... | collective-permute-start | bytes 331784 | tf_op jit(solution)/shard_map/ppermute | solution.py:412
  46.9 2.6 %collective-permute-start.1 = (bf16[432,128]{1,0:T(8,128)(2,1)S(1)}, bf16[432,128]{1,0:T(8,128)(2,1)S(1)}, u32[]{:S(2)}, u32[]{:S(2)}) collective-permute-start(bf16[432,128]{1,0:T(8,128)(2,1)S(1)} %get-tuple-element.19), channel_id=1, source_target_pairs={{0,4},{1,5},{2,6},{3,7},{4,0},{5,1},{6,2},{7,3},{8,12},{9,13},{10,... | collective-permute-start | bytes 331784 | tf_op jit(solution)/shard_map/ppermute | solution.py:412
  49.5 0.2 collective-permute-start.2
  49.7 1.3 %collective-permute-done.refs_1_ = bf16[432,128]{1,0:T(8,128)(2,1)S(1)} collective-permute-done((bf16[432,128]{1,0:T(8,128)(2,1)S(1)}, bf16[432,128]{1,0:T(8,128)(2,1)S(1)}, u32[]{:S(2)}, u32[]{:S(2)}) %collective-permute-start) | collective-permute-done | bytes 110624 | tf_op jit(solution)/shard_map/ppermute | solution.py:412
  51.0 6.0 %collective-permute-done.1.refs_2_ = bf16[432,128]{1,0:T(8,128)(2,1)S(1)} collective-permute-done((bf16[432,128]{1,0:T(8,128)(2,1)S(1)}, bf16[432,128]{1,0:T(8,128)(2,1)S(1)}, u32[]{:S(2)}, u32[]{:S(2)}) %collective-permute-start.1) | collective-permute-done | bytes 110624 | tf_op jit(solution)/shard_map/ppermute | solution.py:412
  57.0 0.2 unpack.1.refs_4_
  57.3 0.1 collective-permute-start.3
  57.3 2.1 %attend_own.1.refs_4_ = f32[4,192,128]{2,1,0:T(8,128)S(1)} custom-call(s32[4]{0:T(128)S(1)} %copy-done.5, bf16[432,128]{1,0:T(8,128)(2,1)S(1)} %get-tuple-element.17.refs_0_, bf16[432,128]{1,0:T(8,128)(2,1)S(1)} %collective-permute-done.refs_1_, bf16[432,128]{1,0:T(8,128)(2,1)S(1)} %collective-permute-done.1.refs_2_, ...), custom_call_target="tpu_custom_call" | custom-call | flops 301989888 | bytes 589824 | tf_op jit(solution)/shard_map/attend_own/pallas_call | solution.py:334
  59.5 3.0 %attend_others.1 = (bf16[144,128]{1,0:T(8,128)(2,1)S(1)}, bf16[144,128]{1,0:T(8,128)(2,1)S(1)}, bf16[144,128]{1,0:T(8,128)(2,1)S(1)}, bf16[144,128]{1,0:T(8,128)(2,1)S(1)}) custom-call(s32[4]{0:T(128)S(1)} %copy-done.5, bf16[432,128]{1,0:T(8,128)(2,1)S(1)} %get-tuple-element.17.refs_0_, bf16[432,128]{1,0:T(8,128)(2,1)S(1)} %collective-permute-done.refs_1_, ...), custom_call_target="tpu_custom_call" | custom-call | tf_op jit(solution)/shard_map/attend_others/pallas_call | solution.py:343
  62.5 1.8 %collective-permute-start.4 = (bf16[144,128]{1,0:T(8,128)(2,1)S(1)}, bf16[144,128]{1,0:T(8,128)(2,1)S(1)}, u32[]{:S(2)}, u32[]{:S(2)}) collective-permute-start(bf16[144,128]{1,0:T(8,128)(2,1)S(1)} %get-tuple-element.22), channel_id=1, source_target_pairs={{0,2},{1,3},{2,0},{3,1},{4,6},{5,7},{6,4},{7,5},{8,10},{9,11},{10,... | collective-permute-start | bytes 110600 | tf_op jit(solution)/shard_map/ppermute | solution.py:412
  64.3 1.3 %collective-permute-start.5 = (bf16[144,128]{1,0:T(8,128)(2,1)S(1)}, bf16[144,128]{1,0:T(8,128)(2,1)S(1)}, u32[]{:S(2)}, u32[]{:S(2)}) collective-permute-start(bf16[144,128]{1,0:T(8,128)(2,1)S(1)} %get-tuple-element.23), channel_id=1, source_target_pairs={{0,4},{1,5},{2,6},{3,7},{4,0},{5,1},{6,2},{7,3},{8,12},{9,13},{10,... | collective-permute-start | bytes 110600 | tf_op jit(solution)/shard_map/ppermute | solution.py:412
  65.6 1.3 %collective-permute-start.6 = (bf16[144,128]{1,0:T(8,128)(2,1)S(1)}, bf16[144,128]{1,0:T(8,128)(2,1)S(1)}, u32[]{:S(2)}, u32[]{:S(2)}) collective-permute-start(bf16[144,128]{1,0:T(8,128)(2,1)S(1)} %get-tuple-element.24), channel_id=1, source_target_pairs={{0,6},{1,7},{2,4},{3,5},{4,2},{5,3},{6,0},{7,1},{8,14},{9,15},{10,... | collective-permute-start | bytes 110600 | tf_op jit(solution)/shard_map/ppermute | solution.py:412
  66.9 3.0 %collective-permute-done.5.refs_2_ = bf16[144,128]{1,0:T(8,128)(2,1)S(1)} collective-permute-done((bf16[144,128]{1,0:T(8,128)(2,1)S(1)}, bf16[144,128]{1,0:T(8,128)(2,1)S(1)}, u32[]{:S(2)}, u32[]{:S(2)}) %collective-permute-start.5) | collective-permute-done | bytes 36896 | tf_op jit(solution)/shard_map/ppermute | solution.py:412
  69.9 1.5 %collective-permute-done.6.refs_3_ = bf16[144,128]{1,0:T(8,128)(2,1)S(1)} collective-permute-done((bf16[144,128]{1,0:T(8,128)(2,1)S(1)}, bf16[144,128]{1,0:T(8,128)(2,1)S(1)}, u32[]{:S(2)}, u32[]{:S(2)}) %collective-permute-start.6) | collective-permute-done | bytes 36896 | tf_op jit(solution)/shard_map/ppermute | solution.py:412
  71.4 0.7 partial_out.1
  72.1 0.2 collective-permute-start.7
  72.3 1.8 %collective-permute-start.8 = (bf16[48,1536]{1,0:T(8,128)(2,1)S(1)}, bf16[48,1536]{1,0:T(8,128)(2,1)S(1)}, u32[]{:S(2)}, u32[]{:S(2)}) collective-permute-start(bf16[48,1536]{1,0:T(8,128)(2,1)S(1)} %get-tuple-element.27), channel_id=1, source_target_pairs={{0,16},{8,24},{16,0},{24,8},{1,17},{9,25},{17,1},{25,9},{2,18},{10... | collective-permute-start | bytes 442376 | tf_op jit(solution)/shard_map/ppermute | solution.py:412
  74.2 1.5 %collective-permute-start.9 = (bf16[48,1536]{1,0:T(8,128)(2,1)S(1)}, bf16[48,1536]{1,0:T(8,128)(2,1)S(1)}, u32[]{:S(2)}, u32[]{:S(2)}) collective-permute-start(bf16[48,1536]{1,0:T(8,128)(2,1)S(1)} %get-tuple-element.28), channel_id=1, source_target_pairs={{0,24},{8,16},{16,8},{24,0},{1,25},{9,17},{17,9},{25,1},{2,26},{10... | collective-permute-start | bytes 442376 | tf_op jit(solution)/shard_map/ppermute | solution.py:412
  75.6 2.8 %collective-permute-done.7.refs_1_ = bf16[48,1536]{1,0:T(8,128)(2,1)S(1)} collective-permute-done((bf16[48,1536]{1,0:T(8,128)(2,1)S(1)}, bf16[48,1536]{1,0:T(8,128)(2,1)S(1)}, u32[]{:S(2)}, u32[]{:S(2)}) %collective-permute-start.7) | collective-permute-done | bytes 147488 | tf_op jit(solution)/shard_map/ppermute | solution.py:412
  78.4 2.2 %collective-permute-done.8.refs_2_ = bf16[48,1536]{1,0:T(8,128)(2,1)S(1)} collective-permute-done((bf16[48,1536]{1,0:T(8,128)(2,1)S(1)}, bf16[48,1536]{1,0:T(8,128)(2,1)S(1)}, u32[]{:S(2)}, u32[]{:S(2)}) %collective-permute-start.8) | collective-permute-done | bytes 147488 | tf_op jit(solution)/shard_map/ppermute | solution.py:412
  80.6 0.7 finish.1
  (16 shorter events, 0.0 us)
Async XLA Ops:
  0.0 43.7 %copy-start.1 = (bf16[1536,384]{1,0:T(8,128)(2,1)S(1)}, bf16[1536,384]{1,0:T(8,128)(2,1)}, u32[]{:S(2)}) copy-start(bf16[1536,384]{1,0:T(8,128)(2,1)} %wq.1) | copy-start | bytes 3538948
  0.0 43.7 %copy-start.2 = (bf16[1536,384]{1,0:T(8,128)(2,1)S(1)}, bf16[1536,384]{1,0:T(8,128)(2,1)}, u32[]{:S(2)}) copy-start(bf16[1536,384]{1,0:T(8,128)(2,1)} %wk.1) | copy-start | bytes 3538948
  0.0 43.7 %copy-start.3 = (bf16[1536,384]{1,0:T(8,128)(2,1)S(1)}, bf16[1536,384]{1,0:T(8,128)(2,1)}, u32[]{:S(2)}) copy-start(bf16[1536,384]{1,0:T(8,128)(2,1)} %wv.1) | copy-start | bytes 3538948
  43.7 13.6 %copy-start.5 = (s32[4]{0:T(128)S(1)}, s32[4]{0:T(128)}, u32[]{:S(2)}) copy-start(s32[4]{0:T(128)} %slide_tiles.3) | copy-start | bytes 52
  45.2 26.1 %copy-start = (bf16[384,1536]{1,0:T(8,128)(2,1)S(1)}, bf16[384,1536]{1,0:T(8,128)(2,1)}, u32[]{:S(2)}) copy-start(bf16[384,1536]{1,0:T(8,128)(2,1)} %refs_4_.1) | copy-start | bytes 3538948
  45.3 5.8 %collective-permute-start = (bf16[432,128]{1,0:T(8,128)(2,1)S(1)}, bf16[432,128]{1,0:T(8,128)(2,1)S(1)}, u32[]{:S(2)}, u32[]{:S(2)}) collective-permute-start(bf16[432,128]{1,0:T(8,128)(2,1)S(1)} %get-tuple-element.18), channel_id=1, source_target_pairs={{0,2},{1,3},{2,0},{3,1},{4,6},{5,7},{6,4},{7,5},{8,10},{9,11},{10,... | collective-permute-start | bytes 331784 | tf_op jit(solution)/shard_map/ppermute | solution.py:412
  46.9 10.1 %collective-permute-start.1 = (bf16[432,128]{1,0:T(8,128)(2,1)S(1)}, bf16[432,128]{1,0:T(8,128)(2,1)S(1)}, u32[]{:S(2)}, u32[]{:S(2)}) collective-permute-start(bf16[432,128]{1,0:T(8,128)(2,1)S(1)} %get-tuple-element.19), channel_id=1, source_target_pairs={{0,4},{1,5},{2,6},{3,7},{4,0},{5,1},{6,2},{7,3},{8,12},{9,13},{10,... | collective-permute-start | bytes 331784 | tf_op jit(solution)/shard_map/ppermute | solution.py:412
  49.5 7.5 %collective-permute-start.2 = (bf16[432,128]{1,0:T(8,128)(2,1)S(1)}, bf16[432,128]{1,0:T(8,128)(2,1)S(1)}, u32[]{:S(2)}, u32[]{:S(2)}) collective-permute-start(bf16[432,128]{1,0:T(8,128)(2,1)S(1)} %get-tuple-element.20), channel_id=1, source_target_pairs={{0,6},{1,7},{2,4},{3,5},{4,2},{5,3},{6,0},{7,1},{8,14},{9,15},{10,... | collective-permute-start | bytes 331784 | tf_op jit(solution)/shard_map/ppermute | solution.py:412
  57.2 23.4 %copy-start.4 = (bf16[48,1536]{1,0:T(8,128)(2,1)S(1)}, bf16[48,1536]{1,0:T(8,128)(2,1)}, u32[]{:S(2)}) copy-start(bf16[48,1536]{1,0:T(8,128)(2,1)} %encode.1.emb) | copy-start | bytes 442372
  57.3 2.2 %collective-permute-start.3 = (bf16[768,256]{1,0:T(8,128)(2,1)S(1)}, bf16[768,256]{1,0:T(8,128)(2,1)S(1)}, u32[]{:S(2)}, u32[]{:S(2)}) collective-permute-start(bf16[768,256]{1,0:T(8,128)(2,1)S(1)} %unpack.1.refs_4_), channel_id=1, source_target_pairs={{0,1},{1,0},{2,3},{3,2},{4,5},{5,4},{6,7},{7,6},{8,9},{9,8},{10,11... | collective-permute-start | bytes 1179656 | tf_op jit(solution)/shard_map/ppermute | solution.py:412
  62.5 4.4 %collective-permute-start.4 = (bf16[144,128]{1,0:T(8,128)(2,1)S(1)}, bf16[144,128]{1,0:T(8,128)(2,1)S(1)}, u32[]{:S(2)}, u32[]{:S(2)}) collective-permute-start(bf16[144,128]{1,0:T(8,128)(2,1)S(1)} %get-tuple-element.22), channel_id=1, source_target_pairs={{0,2},{1,3},{2,0},{3,1},{4,6},{5,7},{6,4},{7,5},{8,10},{9,11},{10,... | collective-permute-start | bytes 110600 | tf_op jit(solution)/shard_map/ppermute | solution.py:412
  64.3 5.6 %collective-permute-start.5 = (bf16[144,128]{1,0:T(8,128)(2,1)S(1)}, bf16[144,128]{1,0:T(8,128)(2,1)S(1)}, u32[]{:S(2)}, u32[]{:S(2)}) collective-permute-start(bf16[144,128]{1,0:T(8,128)(2,1)S(1)} %get-tuple-element.23), channel_id=1, source_target_pairs={{0,4},{1,5},{2,6},{3,7},{4,0},{5,1},{6,2},{7,3},{8,12},{9,13},{10,... | collective-permute-start | bytes 110600 | tf_op jit(solution)/shard_map/ppermute | solution.py:412
  65.6 5.8 %collective-permute-start.6 = (bf16[144,128]{1,0:T(8,128)(2,1)S(1)}, bf16[144,128]{1,0:T(8,128)(2,1)S(1)}, u32[]{:S(2)}, u32[]{:S(2)}) collective-permute-start(bf16[144,128]{1,0:T(8,128)(2,1)S(1)} %get-tuple-element.24), channel_id=1, source_target_pairs={{0,6},{1,7},{2,4},{3,5},{4,2},{5,3},{6,0},{7,1},{8,14},{9,15},{10,... | collective-permute-start | bytes 110600 | tf_op jit(solution)/shard_map/ppermute | solution.py:412
  72.1 6.3 %collective-permute-start.7 = (bf16[48,1536]{1,0:T(8,128)(2,1)S(1)}, bf16[48,1536]{1,0:T(8,128)(2,1)S(1)}, u32[]{:S(2)}, u32[]{:S(2)}) collective-permute-start(bf16[48,1536]{1,0:T(8,128)(2,1)S(1)} %get-tuple-element.26), channel_id=1, source_target_pairs={{0,8},{8,0},{16,24},{24,16},{1,9},{9,1},{17,25},{25,17},{2,10},{10... | collective-permute-start | bytes 442376 | tf_op jit(solution)/shard_map/ppermute | solution.py:412
  72.3 8.3 %collective-permute-start.8 = (bf16[48,1536]{1,0:T(8,128)(2,1)S(1)}, bf16[48,1536]{1,0:T(8,128)(2,1)S(1)}, u32[]{:S(2)}, u32[]{:S(2)}) collective-permute-start(bf16[48,1536]{1,0:T(8,128)(2,1)S(1)} %get-tuple-element.27), channel_id=1, source_target_pairs={{0,16},{8,24},{16,0},{24,8},{1,17},{9,25},{17,1},{25,9},{2,18},{10... | collective-permute-start | bytes 442376 | tf_op jit(solution)/shard_map/ppermute | solution.py:412
  74.2 6.5 %collective-permute-start.9 = (bf16[48,1536]{1,0:T(8,128)(2,1)S(1)}, bf16[48,1536]{1,0:T(8,128)(2,1)S(1)}, u32[]{:S(2)}, u32[]{:S(2)}) collective-permute-start(bf16[48,1536]{1,0:T(8,128)(2,1)S(1)} %get-tuple-element.28), channel_id=1, source_target_pairs={{0,24},{8,16},{16,8},{24,0},{1,25},{9,17},{17,9},{25,1},{2,26},{10... | collective-permute-start | bytes 442376 | tf_op jit(solution)/shard_map/ppermute | solution.py:412

commit v6 on v5

--- a/solution.py
+++ b/solution.py
@@ -70,7 +70,9 @@
     groups = count // GROUP
     per = GROUP // PART
     parts = groups * per
-    chunk = 3 * mid // parts
+    early = 2 * per
+    chunk = 3 * mid // early
+    last = 2 * groups - 1
 
     def x_copy(g):
         at = pl.ds(pl.multiple_of(g * PART * area, PART * area), PART * area)
@@ -91,44 +93,50 @@
         x_copy(0).start()
         wr_copy.start()
         x_copy(1).start()
+        tap_copy(0).start()
         wr_copy.wait()
-        tap_copy(0).start()
-        tap_copy(1).start()
-
-    @pl.when(step < groups)
-    def _():
-        for i in range(per):
-            g = step * per + i
+
+    @pl.when((step == 0) | ((lax.rem(step, 2) == 1) & (step < last)))
+    def _():
+        @pl.loop(0, per)
+        def _(i):
+            g = (step + 1) // 2 * per + i
             x_copy(g).wait()
 
             @pl.when(g + 2 < parts)
             def _():
                 x_copy(g + 2).start()
-                tap_copy(g + 2).start()
+
+            @pl.when(g + 1 < early)
+            def _():
+                tap_copy(g + 1).start()
+
+            @pl.when(g == early - 1)
+            def _():
+                we_copy.start()
 
             rows = x[pl.ds(pl.multiple_of(g * PART * area, PART * area), PART * area), :]
             maps = jnp.maximum(dot(rows, wr[...]), 0.0).reshape(PART, SIDE, SIDE, mid)
             reduced[:, pl.ds(pl.multiple_of(g * PART, PART), PART)] = maps.swapaxes(0, 1)
-            tap_copy(g).wait()
-            at = pl.ds(pl.multiple_of(g * chunk, chunk), chunk)
-            for k, taps in enumerate(tap_combinations([ws[dy, at, :] for dy in range(3)])):
-                mixed_taps[k, at, :] = taps
-
-    @pl.when(step == groups - 1)
-    def _():
-        we_copy.start()
-
-    @pl.when(step == groups)
+
+            @pl.when(g < early)
+            def _():
+                tap_copy(g).wait()
+                at = pl.ds(pl.multiple_of(g * chunk, chunk), chunk)
+                for k, taps in enumerate(tap_combinations([ws[dy, at, :] for dy in range(3)])):
+                    mixed_taps[k, at, :] = taps
+
+    @pl.when(step == 2)
     def _():
         we_copy.wait()
 
-    @pl.when(step == 2 * groups - 1)
+    @pl.when(step == last)
     def _():
         wm_copy.start()
 
-    @pl.when(step >= groups)
-    def _():
-        g = step - groups
+    @pl.when(((lax.rem(step, 2) == 0) & (step > 0)) | (step == last))
+    def _():
+        g = jnp.where(step == last, groups - 1, step // 2 - 1)
         band = GROUP * SIDE
         maps = reduced[:, pl.ds(pl.multiple_of(g * GROUP, GROUP), GROUP)].reshape(SIDE, band, mid)
         edge = jnp.zeros((band, mid), F32)
@@ -148,7 +156,7 @@
         mean = jnp.sum(out.reshape(GROUP, area, c), axis=1) * (1.0 / area)
         pooled[pl.ds(pl.multiple_of(g * GROUP, GROUP), GROUP), :] = mean
 
-    @pl.when(step == 2 * groups - 1)
+    @pl.when(step == last)
     def _():
         wm_copy.wait()
         emb[...] = dot(pooled[...].astype(BF16), wm[...]).astype(BF16)
@@ -175,7 +183,7 @@
             pltpu.VMEM((6, 2 * GROUP * SIDE, mid), F32),
             pltpu.VMEM((count, c), F32),
             pltpu.SemaphoreType.DMA((count // PART,)),
-            pltpu.SemaphoreType.DMA((count // PART,)),
+            pltpu.SemaphoreType.DMA((2 * GROUP // PART,)),
             pltpu.SemaphoreType.DMA((3,)),
         ],
         compiler_params=pltpu.CompilerParams(vmem_limit_bytes=54 << 20),
@@ -222,9 +230,8 @@
 
 
 def unpack_kernel(heads, *refs):
-    own, out = refs[:heads], refs[heads]
+    own, query, key_value = refs[:heads], refs[heads], refs[heads + 1]
     rows = own[0].shape[0] * 4 // 9
-    quarter = rows // 4
     lane = lax.broadcasted_iota(jnp.int32, (rows, LANES), 1)
     for e in range(heads):
         first = own[e][:rows].astype(F32)
@@ -238,15 +245,19 @@
         value = jnp.where(lane < THIRD, low, jnp.where(lane < 2 * THIRD, middle, high))
         value = jnp.where(lane < HD, value, jnp.where(lane == HD, 1.0, 0.0))
         key = jnp.where(lane < HD, second, 0.0)
-        out[e * rows : (e + 1) * rows, :LANES] = key.astype(BF16)
-        out[e * rows : (e + 1) * rows, LANES:] = value.astype(BF16)
+        query[e * rows : (e + 1) * rows] = own[e][:rows]
+        key_value[e * rows : (e + 1) * rows, :LANES] = key.astype(BF16)
+        key_value[e * rows : (e + 1) * rows, LANES:] = value.astype(BF16)
 
 
 def unpack(own):
-    rows = own[0].shape[0] * 4 // 9
-    return pl.pallas_call(
-        functools.partial(unpack_kernel, len(own)),
-        out_shape=jax.ShapeDtypeStruct((len(own) * rows, 2 * LANES), BF16),
+    heads, rows = len(own), own[0].shape[0] * 4 // 9
+    return pl.pallas_call(
+        functools.partial(unpack_kernel, heads),
+        out_shape=[
+            jax.ShapeDtypeStruct((heads * rows, LANES), BF16),
+            jax.ShapeDtypeStruct((heads * rows, 2 * LANES), BF16),
+        ],
         compiler_params=pltpu.CompilerParams(vmem_limit_bytes=24 << 20),
         name="unpack",
     )(*own)
@@ -267,6 +278,9 @@
         pos = lax.broadcasted_iota(jnp.int32, shape, dim) + start
         return sum((pos >= end).astype(jnp.int32) for end in self.ends)
 
+    def of_rows(self):
+        return jnp.concatenate([self.of(e, 0, 0) for e in range(self.heads)], axis=0)
+
     def of_keys(self, f):
         return jnp.concatenate([self.of(e, f, 1) for e in range(self.heads)], axis=1)
 
@@ -279,75 +293,69 @@
     return jnp.where(query_slide == key_slide, scores, -1e30)
 
 
-def attend_own_kernel(heads, spread_of, slide_tiles, *refs):
-    own, key_value, out = refs[:heads], refs[heads], refs[heads + 1]
-    length = key_value.shape[0] // heads
+def attend_own_kernel(heads, spread_of, slide_tiles, queries, key_value, out):
+    rows = queries.shape[0]
+    slides = Slides(slide_tiles, heads, spread_of, rows // heads)
+    lane = lax.broadcasted_iota(jnp.int32, (rows, LANES), 1)
+    scores = masked_scores(queries[...], key_value[:, :LANES], slides.of_rows(), slides.of_keys(0))
+    top = jnp.max(scores, axis=1, keepdims=True)
+    product = dot(jnp.exp2((scores - top) * SCALE).astype(BF16), key_value[:, LANES:])
+    out[...] = jnp.where(lane == HD + 1, top, product)
+
+
+def attend_others_kernel(heads, spread_of, slide_tiles, queries, before, *refs):
+    others, outs = refs[: spread_of - 1], refs[spread_of - 1 :]
+    length = queries.shape[0] // heads
     slides = Slides(slide_tiles, heads, spread_of, length)
-    key_slide = slides.of_keys(0)
-    lane = lax.broadcasted_iota(jnp.int32, (length, LANES), 1)
+    query_slide = slides.of_rows()
+    quarter = length // 4
+    scores = [
+        masked_scores(queries[...], other[:, :LANES], query_slide, slides.of_keys(f))
+        for f, other in enumerate(others, start=1)
+    ]
+    top_before = before[:, HD + 1 : HD + 2]
+    top = functools.reduce(jnp.maximum, [jnp.max(s, axis=1, keepdims=True) for s in scores], top_before)
+    product = before[...] * jnp.exp2((top_before - top) * SCALE)
+    for other, s in zip(others, scores):
+        product = product + dot(jnp.exp2((s - top) * SCALE).astype(BF16), other[:, LANES:])
+    result = product[:, :HD] / product[:, HD : HD + 1]
     for e in range(heads):
-        scores = masked_scores(own[e][:length], key_value[:, :LANES], slides.of(e, 0, 0), key_slide)
-        top = jnp.max(scores, axis=1, keepdims=True)
-        product = dot(jnp.exp2((scores - top) * SCALE).astype(BF16), key_value[:, LANES:])
-        out[e] = jnp.where(lane == HD + 1, top, product)
-
-
-def attend_others_kernel(heads, spread_of, slide_tiles, *refs):
-    own, partial, others = refs[:heads], refs[heads], refs[heads + 1 : heads + spread_of]
-    outs = refs[heads + spread_of :]
-    length = partial.shape[1]
-    slides = Slides(slide_tiles, heads, spread_of, length)
-    key_slides = [slides.of_keys(f) for f in range(1, spread_of)]
-    quarter = length // 4
-    for e in range(heads):
-        query_slide = slides.of(e, 0, 0)
-        scores = [
-            masked_scores(own[e][:length], other[:, :LANES], query_slide, key_slide)
-            for other, key_slide in zip(others, key_slides)
-        ]
-        before = partial[e]
-        top_before = before[:, HD + 1 : HD + 2]
-        top = functools.reduce(
-            jnp.maximum, [jnp.max(s, axis=1, keepdims=True) for s in scores], top_before
-        )
-        product = before * jnp.exp2((top_before - top) * SCALE)
-        for other, s in zip(others, scores):
-            product = product + dot(jnp.exp2((s - top) * SCALE).astype(BF16), other[:, LANES:])
-        result = product[:, :HD] / product[:, HD : HD + 1]
-        rest = result[3 * quarter :]
+        head = result[e * length : e * length + 3 * quarter]
+        rest = result[e * length + 3 * quarter : (e + 1) * length]
         rest = jnp.concatenate([rest[:, i * THIRD : (i + 1) * THIRD] for i in range(3)], axis=0)
-        outs[e][...] = jnp.concatenate([result[: 3 * quarter], rest], axis=1).astype(BF16)
-
-
-def attend(slide_tiles, own, key_value, exchange):
-    heads = len(own)
-    length = key_value.shape[0] // heads
+        outs[e][...] = jnp.concatenate([head, rest], axis=1).astype(BF16)
+
+
+def attend(slide_tiles, own, exchange):
+    queries, key_value = unpack(own)
+    heads, rows = len(own), queries.shape[0]
+    length = rows // heads
     others = exchange(key_value)
     spread_of = len(others) + 1
     small = pl.BlockSpec(memory_space=pltpu.SMEM)
     whole = pl.BlockSpec(memory_space=pltpu.VMEM)
     params = pltpu.CompilerParams(vmem_limit_bytes=40 << 20)
-    rows = length * heads
     cost = pl.CostEstimate(
         flops=4 * rows * rows * LANES, bytes_accessed=6 * rows * LANES, transcendentals=rows * rows
     )
     partial = pl.pallas_call(
         functools.partial(attend_own_kernel, heads, spread_of),
-        in_specs=[small] + [whole] * (heads + 1),
+        in_specs=[small] + [whole] * 2,
         out_specs=whole,
-        out_shape=jax.ShapeDtypeStruct((heads, length, LANES), F32),
+        out_shape=jax.ShapeDtypeStruct((rows, LANES), F32),
         compiler_params=params,
         cost_estimate=cost,
         name="attend_own",
-    )(slide_tiles, *own, key_value)
+    )(slide_tiles, queries, key_value)
+    packed = (length * 3 // 4, LANES)
     return pl.pallas_call(
         functools.partial(attend_others_kernel, heads, spread_of),
-        in_specs=[small] + [whole] * (heads + spread_of),
+        in_specs=[small] + [whole] * (1 + spread_of),
         out_specs=[whole] * heads,
-        out_shape=[jax.ShapeDtypeStruct((length * 3 // 4, LANES), BF16)] * heads,
+        out_shape=[jax.ShapeDtypeStruct(packed, BF16)] * heads,
         compiler_params=params,
         name="attend_others",
-    )(slide_tiles, *own, partial, *others)
+    )(slide_tiles, queries, partial, *others)
 
 
 def partial_out_kernel(heads, tiles_of, spread_of, *refs):
@@ -418,7 +426,7 @@
     gathered = lax.all_gather(emb, "tile", axis=0, tiled=True)
     own = over_heads(project(gathered, wq, wk, wv, heads, spread_of))
     attended = attend(
-        slide_tiles, own, unpack(own), lambda x: [along(x, "blk", blks, f) for f in range(1, spread_of)]
+        slide_tiles, own, lambda x: [along(x, "blk", blks, f) for f in range(1, spread_of)]
     )
     sums = partial_out(over_heads(attended), wo, tiles_of, spread_of)
     sums = [sums[0]] + [along(sums[d], "tile", tiles_of, d) for d in range(1, tiles_of)]

time: 81.6 us -> 80.5 us (0.987)
  Pallas kernels: 39.5 us -> 38.4 us
where the time goes in v6:
time: 80.5 us; the launch traced here: 80.3 us
  Pallas kernels  38.4 us (48%)
  waiting for transfers between devices  16.8 us (21%)
  starting transfers between devices  12.5 us (16%)
  blocking collectives  12.4 us (15%)
    pallas_call x1, Pallas kernels, encode(): pl.pallas_call(encode_kernel, grid=(2 * count // GROUP,), in_specs=[pl.Bl...  30.4 us
    ppermute x10, waiting for transfers between devices, along(): return lax.ppermute(x, axis, [(i, i ^ step) for i in range(size)])  16.8 us
    ppermute x10, starting transfers between devices, along(): return lax.ppermute(x, axis, [(i, i ^ step) for i in range(size)])  12.5 us
    all_gather x1, blocking collectives, shards(): gathered = lax.all_gather(emb, 'tile', axis=0, tiled=True)  12.4 us
    pallas_call x1, Pallas kernels, attend(): pl.pallas_call(functools.partial(attend_others_kernel, heads, spread_of),...  2.64 us
    pallas_call x1, Pallas kernels, attend(): pl.pallas_call(functools.partial(attend_own_kernel, heads, spread_of), in...  2.17 us
  transfers between devices with their start and end apart: 10, of which 6 were waited for; matrix products, arithmetic and copies ran while one was open for 0% of the time, Pallas kernels for 3%

profile of v6, /device:TPU:0, one launch (start us, length us, event | category | flops | bytes accessed | tf_op | source)
XLA Modules:
  0.0 80.3 jit_solution(6271832840269617810)
XLA Ops:
  0.0 30.4 %encode.1.emb = bf16[48,1536]{1,0:T(8,128)(2,1)} custom-call(bf16[3072,2048]{1,0:T(8,128)(2,1)} %bitcast.2, bf16[2048,512]{1,0:T(8,128)(2,1)} %wr_hbm.1, bf16[3,1536,512]{2,1,0:T(8,128)(2,1)} %bitcast.3, bf16[512,2048]{1,0:T(8,128)(2,1)} %we_hbm.1, bf16[2048,1536]{1,0:T(8,128)(2,1)} %wm_hbm.1), custom_call_target="tpu_custom_call" | custom-call | flops 27380416512 | bytes 27787264 | tf_op jit(solution)/shard_map/encode/pallas_call | solution.py:170
  30.4 12.4 %all_gather.3.emb = bf16[192,1536]{1,0:T(8,128)(2,1)S(1)} all-gather(bf16[48,1536]{1,0:T(8,128)(2,1)} %encode.1.emb), channel_id=1, replica_groups=mesh['tile'=4,'blk'=8] {'tile'}, dimensions={0}, use_global_device_ids=true | all-gather | bytes 737280 | tf_op jit(solution)/shard_map/all_gather | solution.py:426
  42.9 1.5 %project.1 = (bf16[432,128]{1,0:T(8,128)(2,1)S(1)}, bf16[432,128]{1,0:T(8,128)(2,1)S(1)}, bf16[432,128]{1,0:T(8,128)(2,1)S(1)}, bf16[432,128]{1,0:T(8,128)(2,1)S(1)}) custom-call(bf16[192,1536]{1,0:T(8,128)(2,1)S(1)} %all_gather.3.emb, bf16[1536,384]{1,0:T(8,128)(2,1)S(1)} %copy-done.1, bf16[1536,384]{1,0:T(8,128)(2,1)S(1)} %copy-done.2, ...), custom_call_target="tpu_custom_call" | custom-call | tf_op jit(solution)/shard_map/project/pallas_call | solution.py:223
  44.4 1.7 %collective-permute-start = (bf16[432,128]{1,0:T(8,128)(2,1)S(1)}, bf16[432,128]{1,0:T(8,128)(2,1)S(1)}, u32[]{:S(2)}, u32[]{:S(2)}) collective-permute-start(bf16[432,128]{1,0:T(8,128)(2,1)S(1)} %get-tuple-element.20), channel_id=1, source_target_pairs={{0,2},{1,3},{2,0},{3,1},{4,6},{5,7},{6,4},{7,5},{8,10},{9,11},{10,... | collective-permute-start | bytes 331784 | tf_op jit(solution)/shard_map/ppermute | solution.py:420
  46.1 2.6 %collective-permute-start.1 = (bf16[432,128]{1,0:T(8,128)(2,1)S(1)}, bf16[432,128]{1,0:T(8,128)(2,1)S(1)}, u32[]{:S(2)}, u32[]{:S(2)}) collective-permute-start(bf16[432,128]{1,0:T(8,128)(2,1)S(1)} %get-tuple-element.21), channel_id=1, source_target_pairs={{0,4},{1,5},{2,6},{3,7},{4,0},{5,1},{6,2},{7,3},{8,12},{9,13},{10,... | collective-permute-start | bytes 331784 | tf_op jit(solution)/shard_map/ppermute | solution.py:420
  48.7 0.2 collective-permute-start.2
  48.9 1.3 %collective-permute-done.refs_1_ = bf16[432,128]{1,0:T(8,128)(2,1)S(1)} collective-permute-done((bf16[432,128]{1,0:T(8,128)(2,1)S(1)}, bf16[432,128]{1,0:T(8,128)(2,1)S(1)}, u32[]{:S(2)}, u32[]{:S(2)}) %collective-permute-start) | collective-permute-done | bytes 110624 | tf_op jit(solution)/shard_map/ppermute | solution.py:420
  50.2 6.0 %collective-permute-done.1.refs_2_ = bf16[432,128]{1,0:T(8,128)(2,1)S(1)} collective-permute-done((bf16[432,128]{1,0:T(8,128)(2,1)S(1)}, bf16[432,128]{1,0:T(8,128)(2,1)S(1)}, u32[]{:S(2)}, u32[]{:S(2)}) %collective-permute-start.1) | collective-permute-done | bytes 110624 | tf_op jit(solution)/shard_map/ppermute | solution.py:420
  56.2 0.2 unpack.1
  56.5 0.1 collective-permute-start.3
  56.6 2.2 %attend_own.1.before = f32[768,128]{1,0:T(8,128)S(1)} custom-call(s32[4]{0:T(128)S(1)} %copy-done.5, bf16[768,128]{1,0:T(8,128)(2,1)S(1)} %get-tuple-element.23.queries, bf16[768,256]{1,0:T(8,128)(2,1)S(1)} %get-tuple-element.24.key_value), custom_call_target="tpu_custom_call" | custom-call | flops 301989888 | bytes 589824 | tf_op jit(solution)/shard_map/attend_own/pallas_call | solution.py:341
  58.7 2.6 %attend_others.1 = (bf16[144,128]{1,0:T(8,128)(2,1)S(1)}, bf16[144,128]{1,0:T(8,128)(2,1)S(1)}, bf16[144,128]{1,0:T(8,128)(2,1)S(1)}, bf16[144,128]{1,0:T(8,128)(2,1)S(1)}) custom-call(s32[4]{0:T(128)S(1)} %copy-done.5, bf16[768,128]{1,0:T(8,128)(2,1)S(1)} %get-tuple-element.23.queries, f32[768,128]{1,0:T(8,128)S(1)} %attend_own.1.before, ...), custom_call_target="tpu_custom_call" | custom-call | tf_op jit(solution)/shard_map/attend_others/pallas_call | solution.py:351
  61.4 1.8 %collective-permute-start.4 = (bf16[144,128]{1,0:T(8,128)(2,1)S(1)}, bf16[144,128]{1,0:T(8,128)(2,1)S(1)}, u32[]{:S(2)}, u32[]{:S(2)}) collective-permute-start(bf16[144,128]{1,0:T(8,128)(2,1)S(1)} %get-tuple-element.26), channel_id=1, source_target_pairs={{0,2},{1,3},{2,0},{3,1},{4,6},{5,7},{6,4},{7,5},{8,10},{9,11},{10,... | collective-permute-start | bytes 110600 | tf_op jit(solution)/shard_map/ppermute | solution.py:420
  63.2 1.3 %collective-permute-start.5 = (bf16[144,128]{1,0:T(8,128)(2,1)S(1)}, bf16[144,128]{1,0:T(8,128)(2,1)S(1)}, u32[]{:S(2)}, u32[]{:S(2)}) collective-permute-start(bf16[144,128]{1,0:T(8,128)(2,1)S(1)} %get-tuple-element.27), channel_id=1, source_target_pairs={{0,4},{1,5},{2,6},{3,7},{4,0},{5,1},{6,2},{7,3},{8,12},{9,13},{10,... | collective-permute-start | bytes 110600 | tf_op jit(solution)/shard_map/ppermute | solution.py:420
  64.5 1.3 %collective-permute-start.6 = (bf16[144,128]{1,0:T(8,128)(2,1)S(1)}, bf16[144,128]{1,0:T(8,128)(2,1)S(1)}, u32[]{:S(2)}, u32[]{:S(2)}) collective-permute-start(bf16[144,128]{1,0:T(8,128)(2,1)S(1)} %get-tuple-element.28), channel_id=1, source_target_pairs={{0,6},{1,7},{2,4},{3,5},{4,2},{5,3},{6,0},{7,1},{8,14},{9,15},{10,... | collective-permute-start | bytes 110600 | tf_op jit(solution)/shard_map/ppermute | solution.py:420
  65.9 3.0 %collective-permute-done.5.refs_2_ = bf16[144,128]{1,0:T(8,128)(2,1)S(1)} collective-permute-done((bf16[144,128]{1,0:T(8,128)(2,1)S(1)}, bf16[144,128]{1,0:T(8,128)(2,1)S(1)}, u32[]{:S(2)}, u32[]{:S(2)}) %collective-permute-start.5) | collective-permute-done | bytes 36896 | tf_op jit(solution)/shard_map/ppermute | solution.py:420
  68.8 1.5 %collective-permute-done.6.refs_3_ = bf16[144,128]{1,0:T(8,128)(2,1)S(1)} collective-permute-done((bf16[144,128]{1,0:T(8,128)(2,1)S(1)}, bf16[144,128]{1,0:T(8,128)(2,1)S(1)}, u32[]{:S(2)}, u32[]{:S(2)}) %collective-permute-start.6) | collective-permute-done | bytes 36896 | tf_op jit(solution)/shard_map/ppermute | solution.py:420
  70.3 0.7 partial_out.1
  71.0 0.2 collective-permute-start.7
  71.3 1.9 %collective-permute-start.8 = (bf16[48,1536]{1,0:T(8,128)(2,1)S(1)}, bf16[48,1536]{1,0:T(8,128)(2,1)S(1)}, u32[]{:S(2)}, u32[]{:S(2)}) collective-permute-start(bf16[48,1536]{1,0:T(8,128)(2,1)S(1)} %get-tuple-element.31), channel_id=1, source_target_pairs={{0,16},{8,24},{16,0},{24,8},{1,17},{9,25},{17,1},{25,9},{2,18},{10... | collective-permute-start | bytes 442376 | tf_op jit(solution)/shard_map/ppermute | solution.py:420
  73.1 1.5 %collective-permute-start.9 = (bf16[48,1536]{1,0:T(8,128)(2,1)S(1)}, bf16[48,1536]{1,0:T(8,128)(2,1)S(1)}, u32[]{:S(2)}, u32[]{:S(2)}) collective-permute-start(bf16[48,1536]{1,0:T(8,128)(2,1)S(1)} %get-tuple-element.32), channel_id=1, source_target_pairs={{0,24},{8,16},{16,8},{24,0},{1,25},{9,17},{17,9},{25,1},{2,26},{10... | collective-permute-start | bytes 442376 | tf_op jit(solution)/shard_map/ppermute | solution.py:420
  74.6 2.8 %collective-permute-done.7.refs_1_ = bf16[48,1536]{1,0:T(8,128)(2,1)S(1)} collective-permute-done((bf16[48,1536]{1,0:T(8,128)(2,1)S(1)}, bf16[48,1536]{1,0:T(8,128)(2,1)S(1)}, u32[]{:S(2)}, u32[]{:S(2)}) %collective-permute-start.7) | collective-permute-done | bytes 147488 | tf_op jit(solution)/shard_map/ppermute | solution.py:420
  77.3 2.2 %collective-permute-done.8.refs_2_ = bf16[48,1536]{1,0:T(8,128)(2,1)S(1)} collective-permute-done((bf16[48,1536]{1,0:T(8,128)(2,1)S(1)}, bf16[48,1536]{1,0:T(8,128)(2,1)S(1)}, u32[]{:S(2)}, u32[]{:S(2)}) %collective-permute-start.8) | collective-permute-done | bytes 147488 | tf_op jit(solution)/shard_map/ppermute | solution.py:420
  79.6 0.7 finish.1
  (16 shorter events, 0.0 us)
Async XLA Ops:
  0.0 42.9 %copy-start.1 = (bf16[1536,384]{1,0:T(8,128)(2,1)S(1)}, bf16[1536,384]{1,0:T(8,128)(2,1)}, u32[]{:S(2)}) copy-start(bf16[1536,384]{1,0:T(8,128)(2,1)} %wq.1) | copy-start | bytes 3538948
  0.0 42.9 %copy-start.2 = (bf16[1536,384]{1,0:T(8,128)(2,1)S(1)}, bf16[1536,384]{1,0:T(8,128)(2,1)}, u32[]{:S(2)}) copy-start(bf16[1536,384]{1,0:T(8,128)(2,1)} %wk.1) | copy-start | bytes 3538948
  0.0 42.9 %copy-start.3 = (bf16[1536,384]{1,0:T(8,128)(2,1)S(1)}, bf16[1536,384]{1,0:T(8,128)(2,1)}, u32[]{:S(2)}) copy-start(bf16[1536,384]{1,0:T(8,128)(2,1)} %wv.1) | copy-start | bytes 3538948
  42.9 13.7 %copy-start.5 = (s32[4]{0:T(128)S(1)}, s32[4]{0:T(128)}, u32[]{:S(2)}) copy-start(s32[4]{0:T(128)} %slide_tiles.3) | copy-start | bytes 52
  44.4 25.9 %copy-start = (bf16[384,1536]{1,0:T(8,128)(2,1)S(1)}, bf16[384,1536]{1,0:T(8,128)(2,1)}, u32[]{:S(2)}) copy-start(bf16[384,1536]{1,0:T(8,128)(2,1)} %refs_4_.1) | copy-start | bytes 3538948
  44.4 35.1 %copy-start.4 = (bf16[48,1536]{1,0:T(8,128)(2,1)S(1)}, bf16[48,1536]{1,0:T(8,128)(2,1)}, u32[]{:S(2)}) copy-start(bf16[48,1536]{1,0:T(8,128)(2,1)} %encode.1.emb) | copy-start | bytes 442372
  44.4 5.8 %collective-permute-start = (bf16[432,128]{1,0:T(8,128)(2,1)S(1)}, bf16[432,128]{1,0:T(8,128)(2,1)S(1)}, u32[]{:S(2)}, u32[]{:S(2)}) collective-permute-start(bf16[432,128]{1,0:T(8,128)(2,1)S(1)} %get-tuple-element.20), channel_id=1, source_target_pairs={{0,2},{1,3},{2,0},{3,1},{4,6},{5,7},{6,4},{7,5},{8,10},{9,11},{10,... | collective-permute-start | bytes 331784 | tf_op jit(solution)/shard_map/ppermute | solution.py:420
  46.1 10.1 %collective-permute-start.1 = (bf16[432,128]{1,0:T(8,128)(2,1)S(1)}, bf16[432,128]{1,0:T(8,128)(2,1)S(1)}, u32[]{:S(2)}, u32[]{:S(2)}) collective-permute-start(bf16[432,128]{1,0:T(8,128)(2,1)S(1)} %get-tuple-element.21), channel_id=1, source_target_pairs={{0,4},{1,5},{2,6},{3,7},{4,0},{5,1},{6,2},{7,3},{8,12},{9,13},{10,... | collective-permute-start | bytes 331784 | tf_op jit(solution)/shard_map/ppermute | solution.py:420
  48.7 7.5 %collective-permute-start.2 = (bf16[432,128]{1,0:T(8,128)(2,1)S(1)}, bf16[432,128]{1,0:T(8,128)(2,1)S(1)}, u32[]{:S(2)}, u32[]{:S(2)}) collective-permute-start(bf16[432,128]{1,0:T(8,128)(2,1)S(1)} %get-tuple-element.22), channel_id=1, source_target_pairs={{0,6},{1,7},{2,4},{3,5},{4,2},{5,3},{6,0},{7,1},{8,14},{9,15},{10,... | collective-permute-start | bytes 331784 | tf_op jit(solution)/shard_map/ppermute | solution.py:420
  56.5 2.3 %collective-permute-start.3 = (bf16[768,256]{1,0:T(8,128)(2,1)S(1)}, bf16[768,256]{1,0:T(8,128)(2,1)S(1)}, u32[]{:S(2)}, u32[]{:S(2)}) collective-permute-start(bf16[768,256]{1,0:T(8,128)(2,1)S(1)} %get-tuple-element.24.key_value), channel_id=1, source_target_pairs={{0,1},{1,0},{2,3},{3,2},{4,5},{5,4},{6,7},{7,6},{8,9},{9,8},{10,11... | collective-permute-start | bytes 1179656 | tf_op jit(solution)/shard_map/ppermute | solution.py:420
  61.4 4.5 %collective-permute-start.4 = (bf16[144,128]{1,0:T(8,128)(2,1)S(1)}, bf16[144,128]{1,0:T(8,128)(2,1)S(1)}, u32[]{:S(2)}, u32[]{:S(2)}) collective-permute-start(bf16[144,128]{1,0:T(8,128)(2,1)S(1)} %get-tuple-element.26), channel_id=1, source_target_pairs={{0,2},{1,3},{2,0},{3,1},{4,6},{5,7},{6,4},{7,5},{8,10},{9,11},{10,... | collective-permute-start | bytes 110600 | tf_op jit(solution)/shard_map/ppermute | solution.py:420
  63.2 5.6 %collective-permute-start.5 = (bf16[144,128]{1,0:T(8,128)(2,1)S(1)}, bf16[144,128]{1,0:T(8,128)(2,1)S(1)}, u32[]{:S(2)}, u32[]{:S(2)}) collective-permute-start(bf16[144,128]{1,0:T(8,128)(2,1)S(1)} %get-tuple-element.27), channel_id=1, source_target_pairs={{0,4},{1,5},{2,6},{3,7},{4,0},{5,1},{6,2},{7,3},{8,12},{9,13},{10,... | collective-permute-start | bytes 110600 | tf_op jit(solution)/shard_map/ppermute | solution.py:420
  64.5 5.8 %collective-permute-start.6 = (bf16[144,128]{1,0:T(8,128)(2,1)S(1)}, bf16[144,128]{1,0:T(8,128)(2,1)S(1)}, u32[]{:S(2)}, u32[]{:S(2)}) collective-permute-start(bf16[144,128]{1,0:T(8,128)(2,1)S(1)} %get-tuple-element.28), channel_id=1, source_target_pairs={{0,6},{1,7},{2,4},{3,5},{4,2},{5,3},{6,0},{7,1},{8,14},{9,15},{10,... | collective-permute-start | bytes 110600 | tf_op jit(solution)/shard_map/ppermute | solution.py:420
  71.0 6.3 %collective-permute-start.7 = (bf16[48,1536]{1,0:T(8,128)(2,1)S(1)}, bf16[48,1536]{1,0:T(8,128)(2,1)S(1)}, u32[]{:S(2)}, u32[]{:S(2)}) collective-permute-start(bf16[48,1536]{1,0:T(8,128)(2,1)S(1)} %get-tuple-element.30), channel_id=1, source_target_pairs={{0,8},{8,0},{16,24},{24,16},{1,9},{9,1},{17,25},{25,17},{2,10},{10... | collective-permute-start | bytes 442376 | tf_op jit(solution)/shard_map/ppermute | solution.py:420
  71.3 8.3 %collective-permute-start.8 = (bf16[48,1536]{1,0:T(8,128)(2,1)S(1)}, bf16[48,1536]{1,0:T(8,128)(2,1)S(1)}, u32[]{:S(2)}, u32[]{:S(2)}) collective-permute-start(bf16[48,1536]{1,0:T(8,128)(2,1)S(1)} %get-tuple-element.31), channel_id=1, source_target_pairs={{0,16},{8,24},{16,0},{24,8},{1,17},{9,25},{17,1},{25,9},{2,18},{10... | collective-permute-start | bytes 442376 | tf_op jit(solution)/shard_map/ppermute | solution.py:420
  73.1 6.4 %collective-permute-start.9 = (bf16[48,1536]{1,0:T(8,128)(2,1)S(1)}, bf16[48,1536]{1,0:T(8,128)(2,1)S(1)}, u32[]{:S(2)}, u32[]{:S(2)}) collective-permute-start(bf16[48,1536]{1,0:T(8,128)(2,1)S(1)} %get-tuple-element.32), channel_id=1, source_target_pairs={{0,24},{8,16},{16,8},{24,0},{1,25},{9,17},{17,9},{25,1},{2,26},{10... | collective-permute-start | bytes 442376 | tf_op jit(solution)/shard_map/ppermute | solution.py:420

commit v7 on v6

--- a/solution.py
+++ b/solution.py
@@ -186,7 +186,7 @@
             pltpu.SemaphoreType.DMA((2 * GROUP // PART,)),
             pltpu.SemaphoreType.DMA((3,)),
         ],
-        compiler_params=pltpu.CompilerParams(vmem_limit_bytes=54 << 20),
+        compiler_params=pltpu.CompilerParams(vmem_limit_bytes=52 << 20),
         cost_estimate=pl.CostEstimate(
             flops=2 * total * (2 * c * mid + 9 * mid**2),
             bytes_accessed=2 * (total * c + wr.size + ws.size + we.size + wm.size),
@@ -196,11 +196,12 @@
     )(flat, wr, ws, we, wm)
 
 
-def project_kernel(heads, spread_of, emb, wq, wk, wv, *outs):
+def project_kernel(heads, spread_of, blocks, *refs):
+    embs, (wq, wk, wv) = refs[:blocks], refs[blocks : blocks + 3]
+    outs, scratch = refs[blocks + 3 : -1], refs[-1]
     a = lax.axis_index("blk") // spread_of
-    scratch = outs[-1]
-    rows = emb.shape[0]
-    values = emb[...].astype(F32)
+    values = jnp.concatenate([emb[...].astype(F32) for emb in embs], axis=0)
+    rows = values.shape[0]
     center = jnp.mean(values, axis=1, keepdims=True)
     values = values - center
     spread = jnp.mean(values * values, axis=1, keepdims=True)
@@ -217,26 +218,33 @@
         outs[e][...] = scratch[a ^ e]
 
 
-def project(emb, wq, wk, wv, heads, spread_of):
-    rows = emb.shape[0]
+def project(embs, wq, wk, wv, heads, spread_of):
+    rows = embs[0].shape[0] * len(embs)
     packed = 2 * rows + rows // 4
-    return pl.pallas_call(
-        functools.partial(project_kernel, heads, spread_of),
+    whole = pl.BlockSpec(memory_space=pltpu.VMEM)
+    return pl.pallas_call(
+        functools.partial(project_kernel, heads, spread_of, len(embs)),
+        in_specs=[whole] * (len(embs) + 3),
+        out_specs=[whole] * heads,
         out_shape=[jax.ShapeDtypeStruct((packed, LANES), BF16)] * heads,
         scratch_shapes=[pltpu.VMEM((heads, packed, LANES), BF16)],
         compiler_params=pltpu.CompilerParams(vmem_limit_bytes=24 << 20),
+        cost_estimate=pl.CostEstimate(
+            flops=6 * rows * wq.size, bytes_accessed=6 * wq.size, transcendentals=0
+        ),
         name="project",
-    )(emb, wq, wk, wv)
-
-
-def unpack_kernel(heads, *refs):
-    own, query, key_value = refs[:heads], refs[heads], refs[heads + 1]
-    rows = own[0].shape[0] * 4 // 9
-    lane = lax.broadcasted_iota(jnp.int32, (rows, LANES), 1)
-    for e in range(heads):
-        first = own[e][:rows].astype(F32)
-        second = own[e][rows : 2 * rows].astype(F32)
-        third = own[e][2 * rows :].astype(F32)
+    )(*embs, wq, wk, wv)
+
+
+def unpack_kernel(packs, *refs):
+    query, key_value = refs[packs:]
+    at = 0
+    for pack in refs[:packs]:
+        rows = pack.shape[0] * 4 // 9
+        lane = lax.broadcasted_iota(jnp.int32, (rows, LANES), 1)
+        first = pack[:rows].astype(F32)
+        second = pack[rows : 2 * rows].astype(F32)
+        third = pack[2 * rows :].astype(F32)
         low = jnp.concatenate(
             [third] + [pltpu.roll(third, LANES - i * THIRD, axis=1) for i in range(1, 4)], axis=0
         )
@@ -245,44 +253,58 @@
         value = jnp.where(lane < THIRD, low, jnp.where(lane < 2 * THIRD, middle, high))
         value = jnp.where(lane < HD, value, jnp.where(lane == HD, 1.0, 0.0))
         key = jnp.where(lane < HD, second, 0.0)
-        query[e * rows : (e + 1) * rows] = own[e][:rows]
-        key_value[e * rows : (e + 1) * rows, :LANES] = key.astype(BF16)
-        key_value[e * rows : (e + 1) * rows, LANES:] = value.astype(BF16)
-
-
-def unpack(own):
-    heads, rows = len(own), own[0].shape[0] * 4 // 9
-    return pl.pallas_call(
-        functools.partial(unpack_kernel, heads),
+        query[at : at + rows] = pack[:rows]
+        key_value[at : at + rows, :LANES] = key.astype(BF16)
+        key_value[at : at + rows, LANES:] = value.astype(BF16)
+        at += rows
+
+
+def unpack(packs):
+    rows = sum(pack.shape[0] * 4 // 9 for pack in packs)
+    whole = pl.BlockSpec(memory_space=pltpu.VMEM)
+    return pl.pallas_call(
+        functools.partial(unpack_kernel, len(packs)),
+        in_specs=[whole] * len(packs),
+        out_specs=[whole] * 2,
         out_shape=[
-            jax.ShapeDtypeStruct((heads * rows, LANES), BF16),
-            jax.ShapeDtypeStruct((heads * rows, 2 * LANES), BF16),
+            jax.ShapeDtypeStruct((rows, LANES), BF16),
+            jax.ShapeDtypeStruct((rows, 2 * LANES), BF16),
         ],
         compiler_params=pltpu.CompilerParams(vmem_limit_bytes=24 << 20),
         name="unpack",
-    )(*own)
-
-
-class Slides:
-    def __init__(self, slide_tiles, heads, spread_of, length):
+    )(*packs)
+
+
+class Layout:
+    def __init__(self, slide_tiles, heads, spread_of, sets, count):
         blk = lax.axis_index("blk")
-        self.a, self.c = blk // spread_of, lax.rem(blk, spread_of)
-        self.heads, self.spread_of, self.length = heads, spread_of, length
+        self.t, self.a, self.c = lax.axis_index("tile"), blk // spread_of, lax.rem(blk, spread_of)
+        self.spread_of, self.count = spread_of, count
+        self.tiles_of = sum(len(members) for members in sets)
+        self.blocks = [(e, d) for members in sets for e in range(heads) for d in members]
         first = slide_tiles[0]
         second = first + slide_tiles[1]
         self.ends = (first, second, second + slide_tiles[2])
 
-    def of(self, e, f, dim):
-        shape = (self.length, 1) if dim == 0 else (1, self.length)
-        start = ((self.a ^ e) * self.spread_of + (self.c ^ f)) * self.length
-        pos = lax.broadcasted_iota(jnp.int32, shape, dim) + start
-        return sum((pos >= end).astype(jnp.int32) for end in self.ends)
+    def starts(self, f):
+        shards = [((self.a ^ e) * self.spread_of + (self.c ^ f), self.t ^ d) for e, d in self.blocks]
+        return [(shard * self.tiles_of + tile) * self.count for shard, tile in shards]
+
+    def slide_of(self, positions):
+        return sum((positions >= end).astype(jnp.int32) for end in self.ends)
 
     def of_rows(self):
-        return jnp.concatenate([self.of(e, 0, 0) for e in range(self.heads)], axis=0)
+        row = lax.broadcasted_iota(jnp.int32, (self.count, 1), 0)
+        return jnp.concatenate([self.slide_of(row + start) for start in self.starts(0)], axis=0)
 
     def of_keys(self, f):
-        return jnp.concatenate([self.of(e, f, 1) for e in range(self.heads)], axis=1)
+        lane = lax.broadcasted_iota(jnp.int32, (1, len(self.blocks) * self.count), 1)
+        starts = self.starts(f)
+        positions = lane + starts[0]
+        for i in range(1, len(starts)):
+            step = starts[i] - starts[i - 1] - self.count
+            positions = positions + jnp.where(lane >= i * self.count, step, 0)
+        return self.slide_of(positions)
 
 
 SCALE = math.log2(math.e) / math.sqrt(HD)
@@ -293,24 +315,21 @@
     return jnp.where(query_slide == key_slide, scores, -1e30)
 
 
-def attend_own_kernel(heads, spread_of, slide_tiles, queries, key_value, out):
-    rows = queries.shape[0]
-    slides = Slides(slide_tiles, heads, spread_of, rows // heads)
-    lane = lax.broadcasted_iota(jnp.int32, (rows, LANES), 1)
-    scores = masked_scores(queries[...], key_value[:, :LANES], slides.of_rows(), slides.of_keys(0))
+def attend_own_kernel(layout, slide_tiles, queries, key_value, out):
+    rows = layout(slide_tiles)
+    lane = lax.broadcasted_iota(jnp.int32, out.shape, 1)
+    scores = masked_scores(queries[...], key_value[:, :LANES], rows.of_rows(), rows.of_keys(0))
     top = jnp.max(scores, axis=1, keepdims=True)
     product = dot(jnp.exp2((scores - top) * SCALE).astype(BF16), key_value[:, LANES:])
     out[...] = jnp.where(lane == HD + 1, top, product)
 
 
-def attend_others_kernel(heads, spread_of, slide_tiles, queries, before, *refs):
-    others, outs = refs[: spread_of - 1], refs[spread_of - 1 :]
-    length = queries.shape[0] // heads
-    slides = Slides(slide_tiles, heads, spread_of, length)
-    query_slide = slides.of_rows()
-    quarter = length // 4
+def attend_others_kernel(layout, others_count, slide_tiles, queries, before, *refs):
+    others, outs = refs[:others_count], refs[others_count:]
+    rows = layout(slide_tiles)
+    query_slide = rows.of_rows()
     scores = [
-        masked_scores(queries[...], other[:, :LANES], query_slide, slides.of_keys(f))
+        masked_scores(queries[...], other[:, :LANES], query_slide, rows.of_keys(f))
         for f, other in enumerate(others, start=1)
     ]
     top_before = before[:, HD + 1 : HD + 2]
@@ -319,19 +338,25 @@
     for other, s in zip(others, scores):
         product = product + dot(jnp.exp2((s - top) * SCALE).astype(BF16), other[:, LANES:])
     result = product[:, :HD] / product[:, HD : HD + 1]
-    for e in range(heads):
-        head = result[e * length : e * length + 3 * quarter]
-        rest = result[e * length + 3 * quarter : (e + 1) * length]
+    count = rows.count
+    quarter = rows.tiles_of * count // 4
+    for e in range(len(outs)):
+        places = [rows.blocks.index((e, d)) * count for d in range(rows.tiles_of)]
+        here = jnp.concatenate([result[at : at + count] for at in places], axis=0)
+        rest = here[3 * quarter :]
         rest = jnp.concatenate([rest[:, i * THIRD : (i + 1) * THIRD] for i in range(3)], axis=0)
-        outs[e][...] = jnp.concatenate([head, rest], axis=1).astype(BF16)
-
-
-def attend(slide_tiles, own, exchange):
-    queries, key_value = unpack(own)
-    heads, rows = len(own), queries.shape[0]
-    length = rows // heads
+        outs[e][...] = jnp.concatenate([here[: 3 * quarter], rest], axis=1).astype(BF16)
+
+
+def attend(slide_tiles, packs, heads, sets, count, exchange):
+    queries, key_value = unpack(packs)
+    rows = queries.shape[0]
     others = exchange(key_value)
     spread_of = len(others) + 1
+
+    def layout(slide_tiles):
+        return Layout(slide_tiles, heads, spread_of, sets, count)
+
     small = pl.BlockSpec(memory_space=pltpu.SMEM)
     whole = pl.BlockSpec(memory_space=pltpu.VMEM)
     params = pltpu.CompilerParams(vmem_limit_bytes=40 << 20)
@@ -339,7 +364,7 @@
         flops=4 * rows * rows * LANES, bytes_accessed=6 * rows * LANES, transcendentals=rows * rows
     )
     partial = pl.pallas_call(
-        functools.partial(attend_own_kernel, heads, spread_of),
+        functools.partial(attend_own_kernel, layout),
         in_specs=[small] + [whole] * 2,
         out_specs=whole,
         out_shape=jax.ShapeDtypeStruct((rows, LANES), F32),
@@ -347,9 +372,9 @@
         cost_estimate=cost,
         name="attend_own",
     )(slide_tiles, queries, key_value)
-    packed = (length * 3 // 4, LANES)
-    return pl.pallas_call(
-        functools.partial(attend_others_kernel, heads, spread_of),
+    packed = (rows // heads * 3 // 4, LANES)
+    return pl.pallas_call(
+        functools.partial(attend_others_kernel, layout, len(others)),
         in_specs=[small] + [whole] * (1 + spread_of),
         out_specs=[whole] * heads,
         out_shape=[jax.ShapeDtypeStruct(packed, BF16)] * heads,
@@ -360,8 +385,8 @@
 
 def partial_out_kernel(heads, tiles_of, spread_of, *refs):
     parts, w_out, outs = refs[:heads], refs[heads], refs[heads + 1 : heads + 1 + tiles_of]
-    sorted_heads, sums = refs[heads + 1 + tiles_of :]
-    a, t = lax.axis_index("blk") // spread_of, lax.axis_index("tile")
+    sorted_heads = refs[-1]
+    a = lax.axis_index("blk") // spread_of
     quarter = parts[0].shape[0] // 3
     for e in range(heads):
         packed = parts[e][...].astype(F32)
@@ -371,10 +396,8 @@
     attended = jnp.concatenate([sorted_heads[h] for h in range(heads)], axis=1).astype(BF16)
     product = dot(attended, w_out[...])
     count = product.shape[0] // tiles_of
-    for block in range(tiles_of):
-        sums[block] = product[block * count : (block + 1) * count]
     for d in range(tiles_of):
-        outs[d][...] = sums[t ^ d].astype(outs[d].dtype)
+        outs[d][...] = product[d * count : (d + 1) * count].astype(outs[d].dtype)
 
 
 def partial_out(parts, w_out, tiles_of, spread_of):
@@ -387,7 +410,7 @@
         in_specs=[whole] * (heads + 1),
         out_specs=[whole] * tiles_of,
         out_shape=[jax.ShapeDtypeStruct((count, width), F32 if d == 0 else BF16) for d in range(tiles_of)],
-        scratch_shapes=[pltpu.VMEM((heads, length, HD), F32), pltpu.VMEM((tiles_of, count, width), F32)],
+        scratch_shapes=[pltpu.VMEM((heads, length, HD), F32)],
         compiler_params=pltpu.CompilerParams(vmem_limit_bytes=24 << 20),
         name="partial_out",
     )(*parts, w_out)
@@ -423,10 +446,17 @@
         return [blocks[0]] + [along(blocks[e], "blk", blks, e * spread_of) for e in range(1, heads)]
 
     emb = encode(flat, wr, ws.reshape(3, 3 * mid, mid), we, wm)
-    gathered = lax.all_gather(emb, "tile", axis=0, tiled=True)
-    own = over_heads(project(gathered, wq, wk, wv, heads, spread_of))
+    embs = [emb] + [along(emb, "tile", tiles_of, d) for d in range(1, tiles_of)]
+    sets = [range(tiles_of // 2), range(tiles_of // 2, tiles_of)]
+    packs = []
+    for members in sets:
+        blocks = [embs[d] for d in members]
+        if packs:
+            *blocks, _ = lax.optimization_barrier((*blocks, packs[1]))
+        packs += over_heads(project(blocks, wq, wk, wv, heads, spread_of))
     attended = attend(
-        slide_tiles, own, lambda x: [along(x, "blk", blks, f) for f in range(1, spread_of)]
+        slide_tiles, packs, heads, sets, count,
+        lambda x: [along(x, "blk", blks, f) for f in range(1, spread_of)],
     )
     sums = partial_out(over_heads(attended), wo, tiles_of, spread_of)
     sums = [sums[0]] + [along(sums[d], "tile", tiles_of, d) for d in range(1, tiles_of)]

time: 80.5 us -> 78.4 us (0.974)
  blocking collectives: 12.4 us -> 0 us
  starting transfers between devices: 12.5 us -> 21.9 us
  waiting for transfers between devices: 16.8 us -> 17.9 us
    all_gather x1 -> x0, blocking collectives: 12.4 us -> none  [shards(): gathered = lax.all_gather(emb, 'tile', axis=0, tiled=True)]
    ppermute x10 -> x16, starting transfers between devices: 12.5 us -> 21.9 us  [along(): return lax.ppermute(x, axis, [(i, i ^ step) for i in range(size)])]
    ppermute x10 -> x16, waiting for transfers between devices: 16.8 us -> 17.9 us  [along(): return lax.ppermute(x, axis, [(i, i ^ step) for i in range(size)])]
    pallas_call x4 -> x5, Pallas kernels: 6.55 us -> 7.06 us  [the longest x1 2.65 us: attend(): pl.pallas_call(functools.partial(attend_others_kernel, layout, len(others...]
  transfers between devices with their start and end apart: 10 -> 16, of which waited for: 6 -> 9; matrix products, arithmetic and copies ran while one was open for 0% -> 0% of each run, Pallas kernels for 3% -> 5%
where the time goes in v7:
time: 78.4 us; the launch traced here: 78.2 us
  Pallas kernels  38.3 us (49%)
  starting transfers between devices  21.9 us (28%)
  waiting for transfers between devices  17.9 us (23%)
    pallas_call x1, Pallas kernels, encode(): pl.pallas_call(encode_kernel, grid=(2 * count // GROUP,), in_specs=[pl.Bl...  29.9 us
    ppermute x16, starting transfers between devices, along(): return lax.ppermute(x, axis, [(i, i ^ step) for i in range(size)])  21.9 us
    ppermute x16, waiting for transfers between devices, along(): return lax.ppermute(x, axis, [(i, i ^ step) for i in range(size)])  17.9 us
    pallas_call x1, Pallas kernels, attend(): pl.pallas_call(functools.partial(attend_others_kernel, layout, len(others...  2.65 us
    pallas_call x1, Pallas kernels, attend(): pl.pallas_call(functools.partial(attend_own_kernel, layout), in_specs=[sm...  2.13 us
    pallas_call x2, Pallas kernels, project(): pl.pallas_call(functools.partial(project_kernel, heads, spread_of, len(em...  2.06 us
  transfers between devices with their start and end apart: 16, of which 9 were waited for; matrix products, arithmetic and copies ran while one was open for 0% of the time, Pallas kernels for 5%

profile of v7, /device:TPU:0, one launch (start us, length us, event | category | flops | bytes accessed | tf_op | source)
XLA Modules:
  0.0 78.2 jit_solution(51898753382433199)
XLA Ops:
  0.0 29.9 %encode.1.refs_0_.emb = bf16[48,1536]{1,0:T(8,128)(2,1)S(1)} custom-call(bf16[3072,2048]{1,0:T(8,128)(2,1)} %bitcast.2, bf16[2048,512]{1,0:T(8,128)(2,1)} %wr_hbm.1, bf16[3,1536,512]{2,1,0:T(8,128)(2,1)} %bitcast.3, bf16[512,2048]{1,0:T(8,128)(2,1)} %we_hbm.1, bf16[2048,1536]{1,0:T(8,128)(2,1)} %wm_hbm.1), custom_call_target="tpu_custom_call" | custom-call | flops 27380416512 | bytes 27787264 | tf_op jit(solution)/shard_map/encode/pallas_call | solution.py:170
  29.9 3.0 %collective-permute-start = (bf16[48,1536]{1,0:T(8,128)(2,1)S(1)}, bf16[48,1536]{1,0:T(8,128)(2,1)S(1)}, u32[]{:S(2)}, u32[]{:S(2)}) collective-permute-start(bf16[48,1536]{1,0:T(8,128)(2,1)S(1)} %encode.1.refs_0_.emb), channel_id=1, source_target_pairs={{0,8},{8,0},{16,24},{24,16},{1,9},{9,1},{17,25},{25,17},{2,10},{10... | collective-permute-start | bytes 442376 | tf_op jit(solution)/shard_map/ppermute | solution.py:443
  32.9 1.5 %collective-permute-start.4 = (bf16[48,1536]{1,0:T(8,128)(2,1)S(1)}, bf16[48,1536]{1,0:T(8,128)(2,1)S(1)}, u32[]{:S(2)}, u32[]{:S(2)}) collective-permute-start(bf16[48,1536]{1,0:T(8,128)(2,1)S(1)} %encode.1.refs_0_.emb), channel_id=1, source_target_pairs={{0,16},{8,24},{16,0},{24,8},{1,17},{9,25},{17,1},{25,9},{2,18},{10... | collective-permute-start | bytes 442376 | tf_op jit(solution)/shard_map/ppermute | solution.py:443
  34.4 2.8 %collective-permute-done.refs_1_ = bf16[48,1536]{1,0:T(8,128)(2,1)S(1)} collective-permute-done((bf16[48,1536]{1,0:T(8,128)(2,1)S(1)}, bf16[48,1536]{1,0:T(8,128)(2,1)S(1)}, u32[]{:S(2)}, u32[]{:S(2)}) %collective-permute-start) | collective-permute-done | bytes 147488 | tf_op jit(solution)/shard_map/ppermute | solution.py:443
  37.2 1.0 %project.2 = (bf16[216,128]{1,0:T(8,128)(2,1)S(1)}, bf16[216,128]{1,0:T(8,128)(2,1)S(1)}, bf16[216,128]{1,0:T(8,128)(2,1)S(1)}, bf16[216,128]{1,0:T(8,128)(2,1)S(1)}) custom-call(bf16[48,1536]{1,0:T(8,128)(2,1)S(1)} %encode.1.refs_0_.emb, bf16[48,1536]{1,0:T(8,128)(2,1)S(1)} %collective-permute-done.refs_1_, bf16[1536,384]{1,0:T(8,128)(2,1)S(1)} %copy-done, ...), custom_call_target="tpu_custom_call" | custom-call | flops 339738624 | bytes 3538944 | tf_op jit(solution)/shard_map/project/pallas_call | solution.py:225
  38.2 2.2 %collective-permute-start.1 = (bf16[216,128]{1,0:T(8,128)(2,1)S(1)}, bf16[216,128]{1,0:T(8,128)(2,1)S(1)}, u32[]{:S(2)}, u32[]{:S(2)}) collective-permute-start(bf16[216,128]{1,0:T(8,128)(2,1)S(1)} %get-tuple-element.26), channel_id=1, source_target_pairs={{0,2},{1,3},{2,0},{3,1},{4,6},{5,7},{6,4},{7,5},{8,10},{9,11},{10,... | collective-permute-start | bytes 165896 | tf_op jit(solution)/shard_map/ppermute | solution.py:443
  40.4 2.6 %collective-permute-start.2 = (bf16[216,128]{1,0:T(8,128)(2,1)S(1)}, bf16[216,128]{1,0:T(8,128)(2,1)S(1)}, u32[]{:S(2)}, u32[]{:S(2)}) collective-permute-start(bf16[216,128]{1,0:T(8,128)(2,1)S(1)} %get-tuple-element.27), channel_id=1, source_target_pairs={{0,4},{1,5},{2,6},{3,7},{4,0},{5,1},{6,2},{7,3},{8,12},{9,13},{10,... | collective-permute-start | bytes 165896 | tf_op jit(solution)/shard_map/ppermute | solution.py:443
  43.0 1.0 %project.3 = (bf16[216,128]{1,0:T(8,128)(2,1)S(1)}, bf16[216,128]{1,0:T(8,128)(2,1)S(1)}, bf16[216,128]{1,0:T(8,128)(2,1)S(1)}, bf16[216,128]{1,0:T(8,128)(2,1)S(1)}) custom-call(bf16[48,1536]{1,0:T(8,128)(2,1)S(1)} %collective-permute-done.4.refs_0_, bf16[48,1536]{1,0:T(8,128)(2,1)S(1)} %collective-permute-done.5.refs_1_, bf16[1536,384]{1,0:T(8,128)(2,1)S(1)} %copy-done, ...), custom_call_target="tpu_custom_call" | custom-call | flops 339738624 | bytes 3538944 | tf_op jit(solution)/shard_map/project/pallas_call | solution.py:225
  44.1 2.1 %collective-permute-start.6 = (bf16[216,128]{1,0:T(8,128)(2,1)S(1)}, bf16[216,128]{1,0:T(8,128)(2,1)S(1)}, u32[]{:S(2)}, u32[]{:S(2)}) collective-permute-start(bf16[216,128]{1,0:T(8,128)(2,1)S(1)} %get-tuple-element.32), channel_id=1, source_target_pairs={{0,2},{1,3},{2,0},{3,1},{4,6},{5,7},{6,4},{7,5},{8,10},{9,11},{10,... | collective-permute-start | bytes 165896 | tf_op jit(solution)/shard_map/ppermute | solution.py:443
  46.2 2.4 %collective-permute-start.7 = (bf16[216,128]{1,0:T(8,128)(2,1)S(1)}, bf16[216,128]{1,0:T(8,128)(2,1)S(1)}, u32[]{:S(2)}, u32[]{:S(2)}) collective-permute-start(bf16[216,128]{1,0:T(8,128)(2,1)S(1)} %get-tuple-element.33), channel_id=1, source_target_pairs={{0,4},{1,5},{2,6},{3,7},{4,0},{5,1},{6,2},{7,3},{8,12},{9,13},{10,... | collective-permute-start | bytes 165896 | tf_op jit(solution)/shard_map/ppermute | solution.py:443
  49.2 2.8 %collective-permute-done.7.refs_6_ = bf16[216,128]{1,0:T(8,128)(2,1)S(1)} collective-permute-done((bf16[216,128]{1,0:T(8,128)(2,1)S(1)}, bf16[216,128]{1,0:T(8,128)(2,1)S(1)}, u32[]{:S(2)}, u32[]{:S(2)}) %collective-permute-start.7) | collective-permute-done | bytes 55328 | tf_op jit(solution)/shard_map/ppermute | solution.py:443
  52.0 2.6 %collective-permute-done.8.refs_7_ = bf16[216,128]{1,0:T(8,128)(2,1)S(1)} collective-permute-done((bf16[216,128]{1,0:T(8,128)(2,1)S(1)}, bf16[216,128]{1,0:T(8,128)(2,1)S(1)}, u32[]{:S(2)}, u32[]{:S(2)}) %collective-permute-start.8) | collective-permute-done | bytes 55328 | tf_op jit(solution)/shard_map/ppermute | solution.py:443
  54.9 2.1 %attend_own.1.before = f32[768,128]{1,0:T(8,128)S(1)} custom-call(s32[4]{0:T(128)S(1)} %copy-done.4, bf16[768,128]{1,0:T(8,128)(2,1)S(1)} %get-tuple-element.35.queries, bf16[768,256]{1,0:T(8,128)(2,1)S(1)} %get-tuple-element.36.key_value), custom_call_target="tpu_custom_call" | custom-call | flops 301989888 | bytes 589824 | tf_op jit(solution)/shard_map/attend_own/pallas_call | solution.py:366
  57.0 2.6 %attend_others.1 = (bf16[144,128]{1,0:T(8,128)(2,1)S(1)}, bf16[144,128]{1,0:T(8,128)(2,1)S(1)}, bf16[144,128]{1,0:T(8,128)(2,1)S(1)}, bf16[144,128]{1,0:T(8,128)(2,1)S(1)}) custom-call(s32[4]{0:T(128)S(1)} %copy-done.4, bf16[768,128]{1,0:T(8,128)(2,1)S(1)} %get-tuple-element.35.queries, f32[768,128]{1,0:T(8,128)S(1)} %attend_own.1.before, ...), custom_call_target="tpu_custom_call" | custom-call | tf_op jit(solution)/shard_map/attend_others/pallas_call | solution.py:376
  59.7 1.3 %collective-permute-start.11 = (bf16[144,128]{1,0:T(8,128)(2,1)S(1)}, bf16[144,128]{1,0:T(8,128)(2,1)S(1)}, u32[]{:S(2)}, u32[]{:S(2)}) collective-permute-start(bf16[144,128]{1,0:T(8,128)(2,1)S(1)} %get-tuple-element.39), channel_id=1, source_target_pairs={{0,4},{1,5},{2,6},{3,7},{4,0},{5,1},{6,2},{7,3},{8,12},{9,13},{10,... | collective-permute-start | bytes 110600 | tf_op jit(solution)/shard_map/ppermute | solution.py:443
  61.0 3.1 %collective-permute-start.12 = (bf16[144,128]{1,0:T(8,128)(2,1)S(1)}, bf16[144,128]{1,0:T(8,128)(2,1)S(1)}, u32[]{:S(2)}, u32[]{:S(2)}) collective-permute-start(bf16[144,128]{1,0:T(8,128)(2,1)S(1)} %get-tuple-element.40), channel_id=1, source_target_pairs={{0,6},{1,7},{2,4},{3,5},{4,2},{5,3},{6,0},{7,1},{8,14},{9,15},{10,... | collective-permute-start | bytes 110600 | tf_op jit(solution)/shard_map/ppermute | solution.py:443
  64.1 0.9 %collective-permute-done.11.refs_2_ = bf16[144,128]{1,0:T(8,128)(2,1)S(1)} collective-permute-done((bf16[144,128]{1,0:T(8,128)(2,1)S(1)}, bf16[144,128]{1,0:T(8,128)(2,1)S(1)}, u32[]{:S(2)}, u32[]{:S(2)}) %collective-permute-start.11) | collective-permute-done | bytes 36896 | tf_op jit(solution)/shard_map/ppermute | solution.py:443
  65.0 1.8 %collective-permute-done.12.refs_3_ = bf16[144,128]{1,0:T(8,128)(2,1)S(1)} collective-permute-done((bf16[144,128]{1,0:T(8,128)(2,1)S(1)}, bf16[144,128]{1,0:T(8,128)(2,1)S(1)}, u32[]{:S(2)}, u32[]{:S(2)}) %collective-permute-start.12) | collective-permute-done | bytes 36896 | tf_op jit(solution)/shard_map/ppermute | solution.py:443
  66.8 0.6 partial_out.1
  67.4 1.9 %collective-permute-start.13 = (bf16[48,1536]{1,0:T(8,128)(2,1)S(1)}, bf16[48,1536]{1,0:T(8,128)(2,1)S(1)}, u32[]{:S(2)}, u32[]{:S(2)}) collective-permute-start(bf16[48,1536]{1,0:T(8,128)(2,1)S(1)} %get-tuple-element.42), channel_id=1, source_target_pairs={{0,8},{8,0},{16,24},{24,16},{1,9},{9,1},{17,25},{25,17},{2,10},{10... | collective-permute-start | bytes 442376 | tf_op jit(solution)/shard_map/ppermute | solution.py:443
  69.3 1.5 %collective-permute-start.14 = (bf16[48,1536]{1,0:T(8,128)(2,1)S(1)}, bf16[48,1536]{1,0:T(8,128)(2,1)S(1)}, u32[]{:S(2)}, u32[]{:S(2)}) collective-permute-start(bf16[48,1536]{1,0:T(8,128)(2,1)S(1)} %get-tuple-element.43), channel_id=1, source_target_pairs={{0,16},{8,24},{16,0},{24,8},{1,17},{9,25},{17,1},{25,9},{2,18},{10... | collective-permute-start | bytes 442376 | tf_op jit(solution)/shard_map/ppermute | solution.py:443
  71.0 2.7 %collective-permute-done.13.refs_1_ = bf16[48,1536]{1,0:T(8,128)(2,1)S(1)} collective-permute-done((bf16[48,1536]{1,0:T(8,128)(2,1)S(1)}, bf16[48,1536]{1,0:T(8,128)(2,1)S(1)}, u32[]{:S(2)}, u32[]{:S(2)}) %collective-permute-start.13) | collective-permute-done | bytes 147488 | tf_op jit(solution)/shard_map/ppermute | solution.py:443
  73.6 3.8 %collective-permute-done.14.refs_2_ = bf16[48,1536]{1,0:T(8,128)(2,1)S(1)} collective-permute-done((bf16[48,1536]{1,0:T(8,128)(2,1)S(1)}, bf16[48,1536]{1,0:T(8,128)(2,1)S(1)}, u32[]{:S(2)}, u32[]{:S(2)}) %collective-permute-start.14) | collective-permute-done | bytes 147488 | tf_op jit(solution)/shard_map/ppermute | solution.py:443
  77.5 0.7 finish.1
  (26 shorter events, 1.2 us)
Async XLA Ops:
  0.0 37.2 %copy-start = (bf16[1536,384]{1,0:T(8,128)(2,1)S(1)}, bf16[1536,384]{1,0:T(8,128)(2,1)}, u32[]{:S(2)}) copy-start(bf16[1536,384]{1,0:T(8,128)(2,1)} %refs_2_.3) | copy-start | bytes 3538948
  0.0 37.2 %copy-start.1 = (bf16[1536,384]{1,0:T(8,128)(2,1)S(1)}, bf16[1536,384]{1,0:T(8,128)(2,1)}, u32[]{:S(2)}) copy-start(bf16[1536,384]{1,0:T(8,128)(2,1)} %refs_3_.3) | copy-start | bytes 3538948
  0.0 37.2 %copy-start.2 = (bf16[1536,384]{1,0:T(8,128)(2,1)S(1)}, bf16[1536,384]{1,0:T(8,128)(2,1)}, u32[]{:S(2)}) copy-start(bf16[1536,384]{1,0:T(8,128)(2,1)} %refs_4_.4) | copy-start | bytes 3538948
  29.9 7.3 %collective-permute-start = (bf16[48,1536]{1,0:T(8,128)(2,1)S(1)}, bf16[48,1536]{1,0:T(8,128)(2,1)S(1)}, u32[]{:S(2)}, u32[]{:S(2)}) collective-permute-start(bf16[48,1536]{1,0:T(8,128)(2,1)S(1)} %encode.1.refs_0_.emb), channel_id=1, source_target_pairs={{0,8},{8,0},{16,24},{24,16},{1,9},{9,1},{17,25},{25,17},{2,10},{10... | collective-permute-start | bytes 442376 | tf_op jit(solution)/shard_map/ppermute | solution.py:443
  32.9 10.1 %collective-permute-start.4 = (bf16[48,1536]{1,0:T(8,128)(2,1)S(1)}, bf16[48,1536]{1,0:T(8,128)(2,1)S(1)}, u32[]{:S(2)}, u32[]{:S(2)}) collective-permute-start(bf16[48,1536]{1,0:T(8,128)(2,1)S(1)} %encode.1.refs_0_.emb), channel_id=1, source_target_pairs={{0,16},{8,24},{16,0},{24,8},{1,17},{9,25},{17,1},{25,9},{2,18},{10... | collective-permute-start | bytes 442376 | tf_op jit(solution)/shard_map/ppermute | solution.py:443
  34.4 8.6 %collective-permute-start.5 = (bf16[48,1536]{1,0:T(8,128)(2,1)S(1)}, bf16[48,1536]{1,0:T(8,128)(2,1)S(1)}, u32[]{:S(2)}, u32[]{:S(2)}) collective-permute-start(bf16[48,1536]{1,0:T(8,128)(2,1)S(1)} %encode.1.refs_0_.emb), channel_id=1, source_target_pairs={{0,24},{8,16},{16,8},{24,0},{1,25},{9,17},{17,9},{25,1},{2,26},{10... | collective-permute-start | bytes 442376 | tf_op jit(solution)/shard_map/ppermute | solution.py:443
  38.2 4.8 %collective-permute-start.1 = (bf16[216,128]{1,0:T(8,128)(2,1)S(1)}, bf16[216,128]{1,0:T(8,128)(2,1)S(1)}, u32[]{:S(2)}, u32[]{:S(2)}) collective-permute-start(bf16[216,128]{1,0:T(8,128)(2,1)S(1)} %get-tuple-element.26), channel_id=1, source_target_pairs={{0,2},{1,3},{2,0},{3,1},{4,6},{5,7},{6,4},{7,5},{8,10},{9,11},{10,... | collective-permute-start | bytes 165896 | tf_op jit(solution)/shard_map/ppermute | solution.py:443
  40.4 8.2 %collective-permute-start.2 = (bf16[216,128]{1,0:T(8,128)(2,1)S(1)}, bf16[216,128]{1,0:T(8,128)(2,1)S(1)}, u32[]{:S(2)}, u32[]{:S(2)}) collective-permute-start(bf16[216,128]{1,0:T(8,128)(2,1)S(1)} %get-tuple-element.27), channel_id=1, source_target_pairs={{0,4},{1,5},{2,6},{3,7},{4,0},{5,1},{6,2},{7,3},{8,12},{9,13},{10,... | collective-permute-start | bytes 165896 | tf_op jit(solution)/shard_map/ppermute | solution.py:443
  43.0 11.9 %copy-start.4 = (s32[4]{0:T(128)S(1)}, s32[4]{0:T(128)}, u32[]{:S(2)}) copy-start(s32[4]{0:T(128)} %slide_tiles.3) | copy-start | bytes 52
  43.0 6.1 %collective-permute-start.3 = (bf16[216,128]{1,0:T(8,128)(2,1)S(1)}, bf16[216,128]{1,0:T(8,128)(2,1)S(1)}, u32[]{:S(2)}, u32[]{:S(2)}) collective-permute-start(bf16[216,128]{1,0:T(8,128)(2,1)S(1)} %get-tuple-element.28), channel_id=1, source_target_pairs={{0,6},{1,7},{2,4},{3,5},{4,2},{5,3},{6,0},{7,1},{8,14},{9,15},{10,... | collective-permute-start | bytes 165896 | tf_op jit(solution)/shard_map/ppermute | solution.py:443
  44.1 22.7 %copy-start.3 = (bf16[384,1536]{1,0:T(8,128)(2,1)S(1)}, bf16[384,1536]{1,0:T(8,128)(2,1)}, u32[]{:S(2)}) copy-start(bf16[384,1536]{1,0:T(8,128)(2,1)} %refs_4_.5) | copy-start | bytes 3538948
  44.1 5.1 %collective-permute-start.6 = (bf16[216,128]{1,0:T(8,128)(2,1)S(1)}, bf16[216,128]{1,0:T(8,128)(2,1)S(1)}, u32[]{:S(2)}, u32[]{:S(2)}) collective-permute-start(bf16[216,128]{1,0:T(8,128)(2,1)S(1)} %get-tuple-element.32), channel_id=1, source_target_pairs={{0,2},{1,3},{2,0},{3,1},{4,6},{5,7},{6,4},{7,5},{8,10},{9,11},{10,... | collective-permute-start | bytes 165896 | tf_op jit(solution)/shard_map/ppermute | solution.py:443
  46.2 5.8 %collective-permute-start.7 = (bf16[216,128]{1,0:T(8,128)(2,1)S(1)}, bf16[216,128]{1,0:T(8,128)(2,1)S(1)}, u32[]{:S(2)}, u32[]{:S(2)}) collective-permute-start(bf16[216,128]{1,0:T(8,128)(2,1)S(1)} %get-tuple-element.33), channel_id=1, source_target_pairs={{0,4},{1,5},{2,6},{3,7},{4,0},{5,1},{6,2},{7,3},{8,12},{9,13},{10,... | collective-permute-start | bytes 165896 | tf_op jit(solution)/shard_map/ppermute | solution.py:443
  48.6 6.0 %collective-permute-start.8 = (bf16[216,128]{1,0:T(8,128)(2,1)S(1)}, bf16[216,128]{1,0:T(8,128)(2,1)S(1)}, u32[]{:S(2)}, u32[]{:S(2)}) collective-permute-start(bf16[216,128]{1,0:T(8,128)(2,1)S(1)} %get-tuple-element.34), channel_id=1, source_target_pairs={{0,6},{1,7},{2,4},{3,5},{4,2},{5,3},{6,0},{7,1},{8,14},{9,15},{10,... | collective-permute-start | bytes 165896 | tf_op jit(solution)/shard_map/ppermute | solution.py:443
  54.8 2.2 %collective-permute-start.9 = (bf16[768,256]{1,0:T(8,128)(2,1)S(1)}, bf16[768,256]{1,0:T(8,128)(2,1)S(1)}, u32[]{:S(2)}, u32[]{:S(2)}) collective-permute-start(bf16[768,256]{1,0:T(8,128)(2,1)S(1)} %get-tuple-element.36.key_value), channel_id=1, source_target_pairs={{0,1},{1,0},{2,3},{3,2},{4,5},{5,4},{6,7},{7,6},{8,9},{9,8},{10,11... | collective-permute-start | bytes 1179656 | tf_op jit(solution)/shard_map/ppermute | solution.py:443
  59.7 4.5 %collective-permute-start.10 = (bf16[144,128]{1,0:T(8,128)(2,1)S(1)}, bf16[144,128]{1,0:T(8,128)(2,1)S(1)}, u32[]{:S(2)}, u32[]{:S(2)}) collective-permute-start(bf16[144,128]{1,0:T(8,128)(2,1)S(1)} %get-tuple-element.38), channel_id=1, source_target_pairs={{0,2},{1,3},{2,0},{3,1},{4,6},{5,7},{6,4},{7,5},{8,10},{9,11},{10,... | collective-permute-start | bytes 110600 | tf_op jit(solution)/shard_map/ppermute | solution.py:443
  59.7 5.2 %collective-permute-start.11 = (bf16[144,128]{1,0:T(8,128)(2,1)S(1)}, bf16[144,128]{1,0:T(8,128)(2,1)S(1)}, u32[]{:S(2)}, u32[]{:S(2)}) collective-permute-start(bf16[144,128]{1,0:T(8,128)(2,1)S(1)} %get-tuple-element.39), channel_id=1, source_target_pairs={{0,4},{1,5},{2,6},{3,7},{4,0},{5,1},{6,2},{7,3},{8,12},{9,13},{10,... | collective-permute-start | bytes 110600 | tf_op jit(solution)/shard_map/ppermute | solution.py:443
  61.0 5.8 %collective-permute-start.12 = (bf16[144,128]{1,0:T(8,128)(2,1)S(1)}, bf16[144,128]{1,0:T(8,128)(2,1)S(1)}, u32[]{:S(2)}, u32[]{:S(2)}) collective-permute-start(bf16[144,128]{1,0:T(8,128)(2,1)S(1)} %get-tuple-element.40), channel_id=1, source_target_pairs={{0,6},{1,7},{2,4},{3,5},{4,2},{5,3},{6,0},{7,1},{8,14},{9,15},{10,... | collective-permute-start | bytes 110600 | tf_op jit(solution)/shard_map/ppermute | solution.py:443
  67.4 6.2 %collective-permute-start.13 = (bf16[48,1536]{1,0:T(8,128)(2,1)S(1)}, bf16[48,1536]{1,0:T(8,128)(2,1)S(1)}, u32[]{:S(2)}, u32[]{:S(2)}) collective-permute-start(bf16[48,1536]{1,0:T(8,128)(2,1)S(1)} %get-tuple-element.42), channel_id=1, source_target_pairs={{0,8},{8,0},{16,24},{24,16},{1,9},{9,1},{17,25},{25,17},{2,10},{10... | collective-permute-start | bytes 442376 | tf_op jit(solution)/shard_map/ppermute | solution.py:443
  69.3 8.2 %collective-permute-start.14 = (bf16[48,1536]{1,0:T(8,128)(2,1)S(1)}, bf16[48,1536]{1,0:T(8,128)(2,1)S(1)}, u32[]{:S(2)}, u32[]{:S(2)}) collective-permute-start(bf16[48,1536]{1,0:T(8,128)(2,1)S(1)} %get-tuple-element.43), channel_id=1, source_target_pairs={{0,16},{8,24},{16,0},{24,8},{1,17},{9,25},{17,1},{25,9},{2,18},{10... | collective-permute-start | bytes 442376 | tf_op jit(solution)/shard_map/ppermute | solution.py:443
  70.8 6.6 %collective-permute-start.15 = (bf16[48,1536]{1,0:T(8,128)(2,1)S(1)}, bf16[48,1536]{1,0:T(8,128)(2,1)S(1)}, u32[]{:S(2)}, u32[]{:S(2)}) collective-permute-start(bf16[48,1536]{1,0:T(8,128)(2,1)S(1)} %get-tuple-element.44), channel_id=1, source_target_pairs={{0,24},{8,16},{16,8},{24,0},{1,25},{9,17},{17,9},{25,1},{2,26},{10... | collective-permute-start | bytes 442376 | tf_op jit(solution)/shard_map/ppermute | solution.py:443

commit v8 on v7

--- a/solution.py
+++ b/solution.py
@@ -317,27 +317,38 @@
 
 def attend_own_kernel(layout, slide_tiles, queries, key_value, out):
     rows = layout(slide_tiles)
-    lane = lax.broadcasted_iota(jnp.int32, out.shape, 1)
-    scores = masked_scores(queries[...], key_value[:, :LANES], rows.of_rows(), rows.of_keys(0))
-    top = jnp.max(scores, axis=1, keepdims=True)
-    product = dot(jnp.exp2((scores - top) * SCALE).astype(BF16), key_value[:, LANES:])
-    out[...] = jnp.where(lane == HD + 1, top, product)
+    query_slide, key_slide = rows.of_rows(), rows.of_keys(0)
+    half = out.shape[0] // 2
+    lane = lax.broadcasted_iota(jnp.int32, (half, LANES), 1)
+    for at in (0, half):
+        scores = masked_scores(
+            queries[at : at + half], key_value[:, :LANES], query_slide[at : at + half], key_slide
+        )
+        top = jnp.max(scores, axis=1, keepdims=True)
+        product = dot(jnp.exp2((scores - top) * SCALE).astype(BF16), key_value[:, LANES:])
+        out[at : at + half] = jnp.where(lane == HD + 1, top, product)
 
 
 def attend_others_kernel(layout, others_count, slide_tiles, queries, before, *refs):
     others, outs = refs[:others_count], refs[others_count:]
     rows = layout(slide_tiles)
     query_slide = rows.of_rows()
-    scores = [
-        masked_scores(queries[...], other[:, :LANES], query_slide, rows.of_keys(f))
-        for f, other in enumerate(others, start=1)
-    ]
-    top_before = before[:, HD + 1 : HD + 2]
-    top = functools.reduce(jnp.maximum, [jnp.max(s, axis=1, keepdims=True) for s in scores], top_before)
-    product = before[...] * jnp.exp2((top_before - top) * SCALE)
-    for other, s in zip(others, scores):
-        product = product + dot(jnp.exp2((s - top) * SCALE).astype(BF16), other[:, LANES:])
-    result = product[:, :HD] / product[:, HD : HD + 1]
+    key_slides = [rows.of_keys(f) for f in range(1, len(others) + 1)]
+    half = query_slide.shape[0] // 2
+    results = []
+    for at in (0, half):
+        scores = [
+            masked_scores(queries[at : at + half], other[:, :LANES], query_slide[at : at + half], key_slide)
+            for other, key_slide in zip(others, key_slides)
+        ]
+        own = before[at : at + half]
+        top_own = own[:, HD + 1 : HD + 2]
+        top = functools.reduce(jnp.maximum, [jnp.max(s, axis=1, keepdims=True) for s in scores], top_own)
+        product = own * jnp.exp2((top_own - top) * SCALE)
+        for other, s in zip(others, scores):
+            product = product + dot(jnp.exp2((s - top) * SCALE).astype(BF16), other[:, LANES:])
+        results.append(product[:, :HD] / product[:, HD : HD + 1])
+    result = jnp.concatenate(results, axis=0)
     count = rows.count
     quarter = rows.tiles_of * count // 4
     for e in range(len(outs)):

time: 78.4 us -> 77.9 us (level)
  no operation moved by 1% of the time
where the time goes in v8:
time: 77.9 us; the launch traced here: 77.7 us
  Pallas kernels  37.8 us (49%)
  starting transfers between devices  21.9 us (28%)
  waiting for transfers between devices  17.9 us (23%)
    pallas_call x1, Pallas kernels, encode(): pl.pallas_call(encode_kernel, grid=(2 * count // GROUP,), in_specs=[pl.Bl...  29.9 us
    ppermute x16, starting transfers between devices, along(): return lax.ppermute(x, axis, [(i, i ^ step) for i in range(size)])  21.9 us
    ppermute x16, waiting for transfers between devices, along(): return lax.ppermute(x, axis, [(i, i ^ step) for i in range(size)])  17.9 us
    pallas_call x1, Pallas kernels, attend(): pl.pallas_call(functools.partial(attend_others_kernel, layout, len(others...  2.39 us
    pallas_call x2, Pallas kernels, project(): pl.pallas_call(functools.partial(project_kernel, heads, spread_of, len(em...  2.06 us
    pallas_call x1, Pallas kernels, attend(): pl.pallas_call(functools.partial(attend_own_kernel, layout), in_specs=[sm...  1.86 us
  transfers between devices with their start and end apart: 16, of which 9 were waited for; matrix products, arithmetic and copies ran while one was open for 0% of the time, Pallas kernels for 5%

profile of v8, /device:TPU:0, one launch (start us, length us, event | category | flops | bytes accessed | tf_op | source)
XLA Modules:
  0.0 77.7 jit_solution(3343634330251815900)
XLA Ops:
  0.0 29.9 %encode.1.refs_0_.emb = bf16[48,1536]{1,0:T(8,128)(2,1)S(1)} custom-call(bf16[3072,2048]{1,0:T(8,128)(2,1)} %bitcast.2, bf16[2048,512]{1,0:T(8,128)(2,1)} %wr_hbm.1, bf16[3,1536,512]{2,1,0:T(8,128)(2,1)} %bitcast.3, bf16[512,2048]{1,0:T(8,128)(2,1)} %we_hbm.1, bf16[2048,1536]{1,0:T(8,128)(2,1)} %wm_hbm.1), custom_call_target="tpu_custom_call" | custom-call | flops 27380416512 | bytes 27787264 | tf_op jit(solution)/shard_map/encode/pallas_call | solution.py:170
  29.9 3.0 %collective-permute-start = (bf16[48,1536]{1,0:T(8,128)(2,1)S(1)}, bf16[48,1536]{1,0:T(8,128)(2,1)S(1)}, u32[]{:S(2)}, u32[]{:S(2)}) collective-permute-start(bf16[48,1536]{1,0:T(8,128)(2,1)S(1)} %encode.1.refs_0_.emb), channel_id=1, source_target_pairs={{0,8},{8,0},{16,24},{24,16},{1,9},{9,1},{17,25},{25,17},{2,10},{10... | collective-permute-start | bytes 442376 | tf_op jit(solution)/shard_map/ppermute | solution.py:454
  32.9 1.5 %collective-permute-start.4 = (bf16[48,1536]{1,0:T(8,128)(2,1)S(1)}, bf16[48,1536]{1,0:T(8,128)(2,1)S(1)}, u32[]{:S(2)}, u32[]{:S(2)}) collective-permute-start(bf16[48,1536]{1,0:T(8,128)(2,1)S(1)} %encode.1.refs_0_.emb), channel_id=1, source_target_pairs={{0,16},{8,24},{16,0},{24,8},{1,17},{9,25},{17,1},{25,9},{2,18},{10... | collective-permute-start | bytes 442376 | tf_op jit(solution)/shard_map/ppermute | solution.py:454
  34.4 2.8 %collective-permute-done.refs_1_ = bf16[48,1536]{1,0:T(8,128)(2,1)S(1)} collective-permute-done((bf16[48,1536]{1,0:T(8,128)(2,1)S(1)}, bf16[48,1536]{1,0:T(8,128)(2,1)S(1)}, u32[]{:S(2)}, u32[]{:S(2)}) %collective-permute-start) | collective-permute-done | bytes 147488 | tf_op jit(solution)/shard_map/ppermute | solution.py:454
  37.2 1.0 %project.2 = (bf16[216,128]{1,0:T(8,128)(2,1)S(1)}, bf16[216,128]{1,0:T(8,128)(2,1)S(1)}, bf16[216,128]{1,0:T(8,128)(2,1)S(1)}, bf16[216,128]{1,0:T(8,128)(2,1)S(1)}) custom-call(bf16[48,1536]{1,0:T(8,128)(2,1)S(1)} %encode.1.refs_0_.emb, bf16[48,1536]{1,0:T(8,128)(2,1)S(1)} %collective-permute-done.refs_1_, bf16[1536,384]{1,0:T(8,128)(2,1)S(1)} %copy-done, ...), custom_call_target="tpu_custom_call" | custom-call | flops 339738624 | bytes 3538944 | tf_op jit(solution)/shard_map/project/pallas_call | solution.py:225
  38.2 2.2 %collective-permute-start.1 = (bf16[216,128]{1,0:T(8,128)(2,1)S(1)}, bf16[216,128]{1,0:T(8,128)(2,1)S(1)}, u32[]{:S(2)}, u32[]{:S(2)}) collective-permute-start(bf16[216,128]{1,0:T(8,128)(2,1)S(1)} %get-tuple-element.26), channel_id=1, source_target_pairs={{0,2},{1,3},{2,0},{3,1},{4,6},{5,7},{6,4},{7,5},{8,10},{9,11},{10,... | collective-permute-start | bytes 165896 | tf_op jit(solution)/shard_map/ppermute | solution.py:454
  40.4 2.6 %collective-permute-start.2 = (bf16[216,128]{1,0:T(8,128)(2,1)S(1)}, bf16[216,128]{1,0:T(8,128)(2,1)S(1)}, u32[]{:S(2)}, u32[]{:S(2)}) collective-permute-start(bf16[216,128]{1,0:T(8,128)(2,1)S(1)} %get-tuple-element.27), channel_id=1, source_target_pairs={{0,4},{1,5},{2,6},{3,7},{4,0},{5,1},{6,2},{7,3},{8,12},{9,13},{10,... | collective-permute-start | bytes 165896 | tf_op jit(solution)/shard_map/ppermute | solution.py:454
  43.0 1.0 %project.3 = (bf16[216,128]{1,0:T(8,128)(2,1)S(1)}, bf16[216,128]{1,0:T(8,128)(2,1)S(1)}, bf16[216,128]{1,0:T(8,128)(2,1)S(1)}, bf16[216,128]{1,0:T(8,128)(2,1)S(1)}) custom-call(bf16[48,1536]{1,0:T(8,128)(2,1)S(1)} %collective-permute-done.4.refs_0_, bf16[48,1536]{1,0:T(8,128)(2,1)S(1)} %collective-permute-done.5.refs_1_, bf16[1536,384]{1,0:T(8,128)(2,1)S(1)} %copy-done, ...), custom_call_target="tpu_custom_call" | custom-call | flops 339738624 | bytes 3538944 | tf_op jit(solution)/shard_map/project/pallas_call | solution.py:225
  44.1 2.1 %collective-permute-start.6 = (bf16[216,128]{1,0:T(8,128)(2,1)S(1)}, bf16[216,128]{1,0:T(8,128)(2,1)S(1)}, u32[]{:S(2)}, u32[]{:S(2)}) collective-permute-start(bf16[216,128]{1,0:T(8,128)(2,1)S(1)} %get-tuple-element.32), channel_id=1, source_target_pairs={{0,2},{1,3},{2,0},{3,1},{4,6},{5,7},{6,4},{7,5},{8,10},{9,11},{10,... | collective-permute-start | bytes 165896 | tf_op jit(solution)/shard_map/ppermute | solution.py:454
  46.2 2.4 %collective-permute-start.7 = (bf16[216,128]{1,0:T(8,128)(2,1)S(1)}, bf16[216,128]{1,0:T(8,128)(2,1)S(1)}, u32[]{:S(2)}, u32[]{:S(2)}) collective-permute-start(bf16[216,128]{1,0:T(8,128)(2,1)S(1)} %get-tuple-element.33), channel_id=1, source_target_pairs={{0,4},{1,5},{2,6},{3,7},{4,0},{5,1},{6,2},{7,3},{8,12},{9,13},{10,... | collective-permute-start | bytes 165896 | tf_op jit(solution)/shard_map/ppermute | solution.py:454
  49.2 2.8 %collective-permute-done.7.refs_6_ = bf16[216,128]{1,0:T(8,128)(2,1)S(1)} collective-permute-done((bf16[216,128]{1,0:T(8,128)(2,1)S(1)}, bf16[216,128]{1,0:T(8,128)(2,1)S(1)}, u32[]{:S(2)}, u32[]{:S(2)}) %collective-permute-start.7) | collective-permute-done | bytes 55328 | tf_op jit(solution)/shard_map/ppermute | solution.py:454
  52.0 2.6 %collective-permute-done.8.refs_7_ = bf16[216,128]{1,0:T(8,128)(2,1)S(1)} collective-permute-done((bf16[216,128]{1,0:T(8,128)(2,1)S(1)}, bf16[216,128]{1,0:T(8,128)(2,1)S(1)}, u32[]{:S(2)}, u32[]{:S(2)}) %collective-permute-start.8) | collective-permute-done | bytes 55328 | tf_op jit(solution)/shard_map/ppermute | solution.py:454
  54.9 1.9 %attend_own.1.before = f32[768,128]{1,0:T(8,128)S(1)} custom-call(s32[4]{0:T(128)S(1)} %copy-done.4, bf16[768,128]{1,0:T(8,128)(2,1)S(1)} %get-tuple-element.35.queries, bf16[768,256]{1,0:T(8,128)(2,1)S(1)} %get-tuple-element.36.key_value), custom_call_target="tpu_custom_call" | custom-call | flops 301989888 | bytes 589824 | tf_op jit(solution)/shard_map/attend_own/pallas_call | solution.py:377
  56.8 2.4 %attend_others.1 = (bf16[144,128]{1,0:T(8,128)(2,1)S(1)}, bf16[144,128]{1,0:T(8,128)(2,1)S(1)}, bf16[144,128]{1,0:T(8,128)(2,1)S(1)}, bf16[144,128]{1,0:T(8,128)(2,1)S(1)}) custom-call(s32[4]{0:T(128)S(1)} %copy-done.4, bf16[768,128]{1,0:T(8,128)(2,1)S(1)} %get-tuple-element.35.queries, f32[768,128]{1,0:T(8,128)S(1)} %attend_own.1.before, ...), custom_call_target="tpu_custom_call" | custom-call | tf_op jit(solution)/shard_map/attend_others/pallas_call | solution.py:387
  59.2 1.2 %collective-permute-start.11 = (bf16[144,128]{1,0:T(8,128)(2,1)S(1)}, bf16[144,128]{1,0:T(8,128)(2,1)S(1)}, u32[]{:S(2)}, u32[]{:S(2)}) collective-permute-start(bf16[144,128]{1,0:T(8,128)(2,1)S(1)} %get-tuple-element.39), channel_id=1, source_target_pairs={{0,4},{1,5},{2,6},{3,7},{4,0},{5,1},{6,2},{7,3},{8,12},{9,13},{10,... | collective-permute-start | bytes 110600 | tf_op jit(solution)/shard_map/ppermute | solution.py:454
  60.5 3.1 %collective-permute-start.12 = (bf16[144,128]{1,0:T(8,128)(2,1)S(1)}, bf16[144,128]{1,0:T(8,128)(2,1)S(1)}, u32[]{:S(2)}, u32[]{:S(2)}) collective-permute-start(bf16[144,128]{1,0:T(8,128)(2,1)S(1)} %get-tuple-element.40), channel_id=1, source_target_pairs={{0,6},{1,7},{2,4},{3,5},{4,2},{5,3},{6,0},{7,1},{8,14},{9,15},{10,... | collective-permute-start | bytes 110600 | tf_op jit(solution)/shard_map/ppermute | solution.py:454
  63.6 0.9 %collective-permute-done.11.refs_2_ = bf16[144,128]{1,0:T(8,128)(2,1)S(1)} collective-permute-done((bf16[144,128]{1,0:T(8,128)(2,1)S(1)}, bf16[144,128]{1,0:T(8,128)(2,1)S(1)}, u32[]{:S(2)}, u32[]{:S(2)}) %collective-permute-start.11) | collective-permute-done | bytes 36896 | tf_op jit(solution)/shard_map/ppermute | solution.py:454
  64.5 1.8 %collective-permute-done.12.refs_3_ = bf16[144,128]{1,0:T(8,128)(2,1)S(1)} collective-permute-done((bf16[144,128]{1,0:T(8,128)(2,1)S(1)}, bf16[144,128]{1,0:T(8,128)(2,1)S(1)}, u32[]{:S(2)}, u32[]{:S(2)}) %collective-permute-start.12) | collective-permute-done | bytes 36896 | tf_op jit(solution)/shard_map/ppermute | solution.py:454
  66.3 0.6 partial_out.1
  66.9 1.9 %collective-permute-start.13 = (bf16[48,1536]{1,0:T(8,128)(2,1)S(1)}, bf16[48,1536]{1,0:T(8,128)(2,1)S(1)}, u32[]{:S(2)}, u32[]{:S(2)}) collective-permute-start(bf16[48,1536]{1,0:T(8,128)(2,1)S(1)} %get-tuple-element.42), channel_id=1, source_target_pairs={{0,8},{8,0},{16,24},{24,16},{1,9},{9,1},{17,25},{25,17},{2,10},{10... | collective-permute-start | bytes 442376 | tf_op jit(solution)/shard_map/ppermute | solution.py:454
  68.8 1.5 %collective-permute-start.14 = (bf16[48,1536]{1,0:T(8,128)(2,1)S(1)}, bf16[48,1536]{1,0:T(8,128)(2,1)S(1)}, u32[]{:S(2)}, u32[]{:S(2)}) collective-permute-start(bf16[48,1536]{1,0:T(8,128)(2,1)S(1)} %get-tuple-element.43), channel_id=1, source_target_pairs={{0,16},{8,24},{16,0},{24,8},{1,17},{9,25},{17,1},{25,9},{2,18},{10... | collective-permute-start | bytes 442376 | tf_op jit(solution)/shard_map/ppermute | solution.py:454
  70.5 2.7 %collective-permute-done.13.refs_1_ = bf16[48,1536]{1,0:T(8,128)(2,1)S(1)} collective-permute-done((bf16[48,1536]{1,0:T(8,128)(2,1)S(1)}, bf16[48,1536]{1,0:T(8,128)(2,1)S(1)}, u32[]{:S(2)}, u32[]{:S(2)}) %collective-permute-start.13) | collective-permute-done | bytes 147488 | tf_op jit(solution)/shard_map/ppermute | solution.py:454
  73.1 3.8 %collective-permute-done.14.refs_2_ = bf16[48,1536]{1,0:T(8,128)(2,1)S(1)} collective-permute-done((bf16[48,1536]{1,0:T(8,128)(2,1)S(1)}, bf16[48,1536]{1,0:T(8,128)(2,1)S(1)}, u32[]{:S(2)}, u32[]{:S(2)}) %collective-permute-start.14) | collective-permute-done | bytes 147488 | tf_op jit(solution)/shard_map/ppermute | solution.py:454
  77.0 0.7 finish.1
  (26 shorter events, 1.2 us)
Async XLA Ops:
  0.0 37.2 %copy-start = (bf16[1536,384]{1,0:T(8,128)(2,1)S(1)}, bf16[1536,384]{1,0:T(8,128)(2,1)}, u32[]{:S(2)}) copy-start(bf16[1536,384]{1,0:T(8,128)(2,1)} %refs_2_.3) | copy-start | bytes 3538948
  0.0 37.2 %copy-start.1 = (bf16[1536,384]{1,0:T(8,128)(2,1)S(1)}, bf16[1536,384]{1,0:T(8,128)(2,1)}, u32[]{:S(2)}) copy-start(bf16[1536,384]{1,0:T(8,128)(2,1)} %refs_3_.3) | copy-start | bytes 3538948
  0.0 37.2 %copy-start.2 = (bf16[1536,384]{1,0:T(8,128)(2,1)S(1)}, bf16[1536,384]{1,0:T(8,128)(2,1)}, u32[]{:S(2)}) copy-start(bf16[1536,384]{1,0:T(8,128)(2,1)} %refs_4_.4) | copy-start | bytes 3538948
  29.9 7.3 %collective-permute-start = (bf16[48,1536]{1,0:T(8,128)(2,1)S(1)}, bf16[48,1536]{1,0:T(8,128)(2,1)S(1)}, u32[]{:S(2)}, u32[]{:S(2)}) collective-permute-start(bf16[48,1536]{1,0:T(8,128)(2,1)S(1)} %encode.1.refs_0_.emb), channel_id=1, source_target_pairs={{0,8},{8,0},{16,24},{24,16},{1,9},{9,1},{17,25},{25,17},{2,10},{10... | collective-permute-start | bytes 442376 | tf_op jit(solution)/shard_map/ppermute | solution.py:454
  32.9 10.1 %collective-permute-start.4 = (bf16[48,1536]{1,0:T(8,128)(2,1)S(1)}, bf16[48,1536]{1,0:T(8,128)(2,1)S(1)}, u32[]{:S(2)}, u32[]{:S(2)}) collective-permute-start(bf16[48,1536]{1,0:T(8,128)(2,1)S(1)} %encode.1.refs_0_.emb), channel_id=1, source_target_pairs={{0,16},{8,24},{16,0},{24,8},{1,17},{9,25},{17,1},{25,9},{2,18},{10... | collective-permute-start | bytes 442376 | tf_op jit(solution)/shard_map/ppermute | solution.py:454
  34.4 8.6 %collective-permute-start.5 = (bf16[48,1536]{1,0:T(8,128)(2,1)S(1)}, bf16[48,1536]{1,0:T(8,128)(2,1)S(1)}, u32[]{:S(2)}, u32[]{:S(2)}) collective-permute-start(bf16[48,1536]{1,0:T(8,128)(2,1)S(1)} %encode.1.refs_0_.emb), channel_id=1, source_target_pairs={{0,24},{8,16},{16,8},{24,0},{1,25},{9,17},{17,9},{25,1},{2,26},{10... | collective-permute-start | bytes 442376 | tf_op jit(solution)/shard_map/ppermute | solution.py:454
  38.2 4.8 %collective-permute-start.1 = (bf16[216,128]{1,0:T(8,128)(2,1)S(1)}, bf16[216,128]{1,0:T(8,128)(2,1)S(1)}, u32[]{:S(2)}, u32[]{:S(2)}) collective-permute-start(bf16[216,128]{1,0:T(8,128)(2,1)S(1)} %get-tuple-element.26), channel_id=1, source_target_pairs={{0,2},{1,3},{2,0},{3,1},{4,6},{5,7},{6,4},{7,5},{8,10},{9,11},{10,... | collective-permute-start | bytes 165896 | tf_op jit(solution)/shard_map/ppermute | solution.py:454
  40.4 8.2 %collective-permute-start.2 = (bf16[216,128]{1,0:T(8,128)(2,1)S(1)}, bf16[216,128]{1,0:T(8,128)(2,1)S(1)}, u32[]{:S(2)}, u32[]{:S(2)}) collective-permute-start(bf16[216,128]{1,0:T(8,128)(2,1)S(1)} %get-tuple-element.27), channel_id=1, source_target_pairs={{0,4},{1,5},{2,6},{3,7},{4,0},{5,1},{6,2},{7,3},{8,12},{9,13},{10,... | collective-permute-start | bytes 165896 | tf_op jit(solution)/shard_map/ppermute | solution.py:454
  43.0 11.9 %copy-start.4 = (s32[4]{0:T(128)S(1)}, s32[4]{0:T(128)}, u32[]{:S(2)}) copy-start(s32[4]{0:T(128)} %slide_tiles.3) | copy-start | bytes 52
  43.0 6.1 %collective-permute-start.3 = (bf16[216,128]{1,0:T(8,128)(2,1)S(1)}, bf16[216,128]{1,0:T(8,128)(2,1)S(1)}, u32[]{:S(2)}, u32[]{:S(2)}) collective-permute-start(bf16[216,128]{1,0:T(8,128)(2,1)S(1)} %get-tuple-element.28), channel_id=1, source_target_pairs={{0,6},{1,7},{2,4},{3,5},{4,2},{5,3},{6,0},{7,1},{8,14},{9,15},{10,... | collective-permute-start | bytes 165896 | tf_op jit(solution)/shard_map/ppermute | solution.py:454
  44.1 22.2 %copy-start.3 = (bf16[384,1536]{1,0:T(8,128)(2,1)S(1)}, bf16[384,1536]{1,0:T(8,128)(2,1)}, u32[]{:S(2)}) copy-start(bf16[384,1536]{1,0:T(8,128)(2,1)} %refs_4_.5) | copy-start | bytes 3538948
  44.1 5.1 %collective-permute-start.6 = (bf16[216,128]{1,0:T(8,128)(2,1)S(1)}, bf16[216,128]{1,0:T(8,128)(2,1)S(1)}, u32[]{:S(2)}, u32[]{:S(2)}) collective-permute-start(bf16[216,128]{1,0:T(8,128)(2,1)S(1)} %get-tuple-element.32), channel_id=1, source_target_pairs={{0,2},{1,3},{2,0},{3,1},{4,6},{5,7},{6,4},{7,5},{8,10},{9,11},{10,... | collective-permute-start | bytes 165896 | tf_op jit(solution)/shard_map/ppermute | solution.py:454
  46.2 5.8 %collective-permute-start.7 = (bf16[216,128]{1,0:T(8,128)(2,1)S(1)}, bf16[216,128]{1,0:T(8,128)(2,1)S(1)}, u32[]{:S(2)}, u32[]{:S(2)}) collective-permute-start(bf16[216,128]{1,0:T(8,128)(2,1)S(1)} %get-tuple-element.33), channel_id=1, source_target_pairs={{0,4},{1,5},{2,6},{3,7},{4,0},{5,1},{6,2},{7,3},{8,12},{9,13},{10,... | collective-permute-start | bytes 165896 | tf_op jit(solution)/shard_map/ppermute | solution.py:454
  48.6 6.0 %collective-permute-start.8 = (bf16[216,128]{1,0:T(8,128)(2,1)S(1)}, bf16[216,128]{1,0:T(8,128)(2,1)S(1)}, u32[]{:S(2)}, u32[]{:S(2)}) collective-permute-start(bf16[216,128]{1,0:T(8,128)(2,1)S(1)} %get-tuple-element.34), channel_id=1, source_target_pairs={{0,6},{1,7},{2,4},{3,5},{4,2},{5,3},{6,0},{7,1},{8,14},{9,15},{10,... | collective-permute-start | bytes 165896 | tf_op jit(solution)/shard_map/ppermute | solution.py:454
  54.8 2.0 %collective-permute-start.9 = (bf16[768,256]{1,0:T(8,128)(2,1)S(1)}, bf16[768,256]{1,0:T(8,128)(2,1)S(1)}, u32[]{:S(2)}, u32[]{:S(2)}) collective-permute-start(bf16[768,256]{1,0:T(8,128)(2,1)S(1)} %get-tuple-element.36.key_value), channel_id=1, source_target_pairs={{0,1},{1,0},{2,3},{3,2},{4,5},{5,4},{6,7},{7,6},{8,9},{9,8},{10,11... | collective-permute-start | bytes 1179656 | tf_op jit(solution)/shard_map/ppermute | solution.py:454
  59.2 4.5 %collective-permute-start.10 = (bf16[144,128]{1,0:T(8,128)(2,1)S(1)}, bf16[144,128]{1,0:T(8,128)(2,1)S(1)}, u32[]{:S(2)}, u32[]{:S(2)}) collective-permute-start(bf16[144,128]{1,0:T(8,128)(2,1)S(1)} %get-tuple-element.38), channel_id=1, source_target_pairs={{0,2},{1,3},{2,0},{3,1},{4,6},{5,7},{6,4},{7,5},{8,10},{9,11},{10,... | collective-permute-start | bytes 110600 | tf_op jit(solution)/shard_map/ppermute | solution.py:454
  59.2 5.2 %collective-permute-start.11 = (bf16[144,128]{1,0:T(8,128)(2,1)S(1)}, bf16[144,128]{1,0:T(8,128)(2,1)S(1)}, u32[]{:S(2)}, u32[]{:S(2)}) collective-permute-start(bf16[144,128]{1,0:T(8,128)(2,1)S(1)} %get-tuple-element.39), channel_id=1, source_target_pairs={{0,4},{1,5},{2,6},{3,7},{4,0},{5,1},{6,2},{7,3},{8,12},{9,13},{10,... | collective-permute-start | bytes 110600 | tf_op jit(solution)/shard_map/ppermute | solution.py:454
  60.5 5.8 %collective-permute-start.12 = (bf16[144,128]{1,0:T(8,128)(2,1)S(1)}, bf16[144,128]{1,0:T(8,128)(2,1)S(1)}, u32[]{:S(2)}, u32[]{:S(2)}) collective-permute-start(bf16[144,128]{1,0:T(8,128)(2,1)S(1)} %get-tuple-element.40), channel_id=1, source_target_pairs={{0,6},{1,7},{2,4},{3,5},{4,2},{5,3},{6,0},{7,1},{8,14},{9,15},{10,... | collective-permute-start | bytes 110600 | tf_op jit(solution)/shard_map/ppermute | solution.py:454
  66.9 6.2 %collective-permute-start.13 = (bf16[48,1536]{1,0:T(8,128)(2,1)S(1)}, bf16[48,1536]{1,0:T(8,128)(2,1)S(1)}, u32[]{:S(2)}, u32[]{:S(2)}) collective-permute-start(bf16[48,1536]{1,0:T(8,128)(2,1)S(1)} %get-tuple-element.42), channel_id=1, source_target_pairs={{0,8},{8,0},{16,24},{24,16},{1,9},{9,1},{17,25},{25,17},{2,10},{10... | collective-permute-start | bytes 442376 | tf_op jit(solution)/shard_map/ppermute | solution.py:454
  68.8 8.2 %collective-permute-start.14 = (bf16[48,1536]{1,0:T(8,128)(2,1)S(1)}, bf16[48,1536]{1,0:T(8,128)(2,1)S(1)}, u32[]{:S(2)}, u32[]{:S(2)}) collective-permute-start(bf16[48,1536]{1,0:T(8,128)(2,1)S(1)} %get-tuple-element.43), channel_id=1, source_target_pairs={{0,16},{8,24},{16,0},{24,8},{1,17},{9,25},{17,1},{25,9},{2,18},{10... | collective-permute-start | bytes 442376 | tf_op jit(solution)/shard_map/ppermute | solution.py:454
  70.3 6.6 %collective-permute-start.15 = (bf16[48,1536]{1,0:T(8,128)(2,1)S(1)}, bf16[48,1536]{1,0:T(8,128)(2,1)S(1)}, u32[]{:S(2)}, u32[]{:S(2)}) collective-permute-start(bf16[48,1536]{1,0:T(8,128)(2,1)S(1)} %get-tuple-element.44), channel_id=1, source_target_pairs={{0,24},{8,16},{16,8},{24,0},{1,25},{9,17},{17,9},{25,1},{2,26},{10... | collective-permute-start | bytes 442376 | tf_op jit(solution)/shard_map/ppermute | solution.py:454

commit v9 on v8

--- a/solution.py
+++ b/solution.py
@@ -15,7 +15,7 @@
 F32 = jnp.float32
 BF16 = jnp.bfloat16
 GROUP = 16
-PART = 8
+PART = 16
 
 
 def dot(a, b):

time: 77.9 us -> 76.7 us (0.985)
  Pallas kernels: 37.8 us -> 36.6 us
    pallas_call x1, Pallas kernels: 29.9 us -> 28.7 us  [encode(): pl.pallas_call(encode_kernel, grid=(2 * count // GROUP,), in_specs=[pl.Bl...]
where the time goes in v9:
time: 76.7 us; the launch traced here: 76.6 us
  Pallas kernels  36.6 us (48%)
  starting transfers between devices  21.9 us (29%)
  waiting for transfers between devices  17.9 us (23%)
    pallas_call x1, Pallas kernels, encode(): pl.pallas_call(encode_kernel, grid=(2 * count // GROUP,), in_specs=[pl.Bl...  28.7 us
    ppermute x16, starting transfers between devices, along(): return lax.ppermute(x, axis, [(i, i ^ step) for i in range(size)])  21.9 us
    ppermute x16, waiting for transfers between devices, along(): return lax.ppermute(x, axis, [(i, i ^ step) for i in range(size)])  17.9 us
    pallas_call x1, Pallas kernels, attend(): pl.pallas_call(functools.partial(attend_others_kernel, layout, len(others...  2.39 us
    pallas_call x2, Pallas kernels, project(): pl.pallas_call(functools.partial(project_kernel, heads, spread_of, len(em...  2.06 us
    pallas_call x1, Pallas kernels, attend(): pl.pallas_call(functools.partial(attend_own_kernel, layout), in_specs=[sm...  1.86 us
  transfers between devices with their start and end apart: 16, of which 9 were waited for; matrix products, arithmetic and copies ran while one was open for 0% of the time, Pallas kernels for 5%

profile of v9, /device:TPU:0, one launch (start us, length us, event | category | flops | bytes accessed | tf_op | source)
XLA Modules:
  0.0 76.6 jit_solution(12610743060874997369)
XLA Ops:
  0.0 28.7 %encode.1.refs_0_.emb = bf16[48,1536]{1,0:T(8,128)(2,1)S(1)} custom-call(bf16[3072,2048]{1,0:T(8,128)(2,1)} %bitcast.2, bf16[2048,512]{1,0:T(8,128)(2,1)} %wr_hbm.1, bf16[3,1536,512]{2,1,0:T(8,128)(2,1)} %bitcast.3, bf16[512,2048]{1,0:T(8,128)(2,1)} %we_hbm.1, bf16[2048,1536]{1,0:T(8,128)(2,1)} %wm_hbm.1), custom_call_target="tpu_custom_call" | custom-call | flops 27380416512 | bytes 27787264 | tf_op jit(solution)/shard_map/encode/pallas_call | solution.py:170
  28.7 3.0 %collective-permute-start = (bf16[48,1536]{1,0:T(8,128)(2,1)S(1)}, bf16[48,1536]{1,0:T(8,128)(2,1)S(1)}, u32[]{:S(2)}, u32[]{:S(2)}) collective-permute-start(bf16[48,1536]{1,0:T(8,128)(2,1)S(1)} %encode.1.refs_0_.emb), channel_id=1, source_target_pairs={{0,8},{8,0},{16,24},{24,16},{1,9},{9,1},{17,25},{25,17},{2,10},{10... | collective-permute-start | bytes 442376 | tf_op jit(solution)/shard_map/ppermute | solution.py:454
  31.8 1.5 %collective-permute-start.4 = (bf16[48,1536]{1,0:T(8,128)(2,1)S(1)}, bf16[48,1536]{1,0:T(8,128)(2,1)S(1)}, u32[]{:S(2)}, u32[]{:S(2)}) collective-permute-start(bf16[48,1536]{1,0:T(8,128)(2,1)S(1)} %encode.1.refs_0_.emb), channel_id=1, source_target_pairs={{0,16},{8,24},{16,0},{24,8},{1,17},{9,25},{17,1},{25,9},{2,18},{10... | collective-permute-start | bytes 442376 | tf_op jit(solution)/shard_map/ppermute | solution.py:454
  33.3 2.8 %collective-permute-done.refs_1_ = bf16[48,1536]{1,0:T(8,128)(2,1)S(1)} collective-permute-done((bf16[48,1536]{1,0:T(8,128)(2,1)S(1)}, bf16[48,1536]{1,0:T(8,128)(2,1)S(1)}, u32[]{:S(2)}, u32[]{:S(2)}) %collective-permute-start) | collective-permute-done | bytes 147488 | tf_op jit(solution)/shard_map/ppermute | solution.py:454
  36.1 1.0 %project.2 = (bf16[216,128]{1,0:T(8,128)(2,1)S(1)}, bf16[216,128]{1,0:T(8,128)(2,1)S(1)}, bf16[216,128]{1,0:T(8,128)(2,1)S(1)}, bf16[216,128]{1,0:T(8,128)(2,1)S(1)}) custom-call(bf16[48,1536]{1,0:T(8,128)(2,1)S(1)} %encode.1.refs_0_.emb, bf16[48,1536]{1,0:T(8,128)(2,1)S(1)} %collective-permute-done.refs_1_, bf16[1536,384]{1,0:T(8,128)(2,1)S(1)} %copy-done, ...), custom_call_target="tpu_custom_call" | custom-call | flops 339738624 | bytes 3538944 | tf_op jit(solution)/shard_map/project/pallas_call | solution.py:225
  37.1 2.2 %collective-permute-start.1 = (bf16[216,128]{1,0:T(8,128)(2,1)S(1)}, bf16[216,128]{1,0:T(8,128)(2,1)S(1)}, u32[]{:S(2)}, u32[]{:S(2)}) collective-permute-start(bf16[216,128]{1,0:T(8,128)(2,1)S(1)} %get-tuple-element.26), channel_id=1, source_target_pairs={{0,2},{1,3},{2,0},{3,1},{4,6},{5,7},{6,4},{7,5},{8,10},{9,11},{10,... | collective-permute-start | bytes 165896 | tf_op jit(solution)/shard_map/ppermute | solution.py:454
  39.3 2.6 %collective-permute-start.2 = (bf16[216,128]{1,0:T(8,128)(2,1)S(1)}, bf16[216,128]{1,0:T(8,128)(2,1)S(1)}, u32[]{:S(2)}, u32[]{:S(2)}) collective-permute-start(bf16[216,128]{1,0:T(8,128)(2,1)S(1)} %get-tuple-element.27), channel_id=1, source_target_pairs={{0,4},{1,5},{2,6},{3,7},{4,0},{5,1},{6,2},{7,3},{8,12},{9,13},{10,... | collective-permute-start | bytes 165896 | tf_op jit(solution)/shard_map/ppermute | solution.py:454
  41.9 1.0 %project.3 = (bf16[216,128]{1,0:T(8,128)(2,1)S(1)}, bf16[216,128]{1,0:T(8,128)(2,1)S(1)}, bf16[216,128]{1,0:T(8,128)(2,1)S(1)}, bf16[216,128]{1,0:T(8,128)(2,1)S(1)}) custom-call(bf16[48,1536]{1,0:T(8,128)(2,1)S(1)} %collective-permute-done.4.refs_0_, bf16[48,1536]{1,0:T(8,128)(2,1)S(1)} %collective-permute-done.5.refs_1_, bf16[1536,384]{1,0:T(8,128)(2,1)S(1)} %copy-done, ...), custom_call_target="tpu_custom_call" | custom-call | flops 339738624 | bytes 3538944 | tf_op jit(solution)/shard_map/project/pallas_call | solution.py:225
  42.9 2.1 %collective-permute-start.6 = (bf16[216,128]{1,0:T(8,128)(2,1)S(1)}, bf16[216,128]{1,0:T(8,128)(2,1)S(1)}, u32[]{:S(2)}, u32[]{:S(2)}) collective-permute-start(bf16[216,128]{1,0:T(8,128)(2,1)S(1)} %get-tuple-element.32), channel_id=1, source_target_pairs={{0,2},{1,3},{2,0},{3,1},{4,6},{5,7},{6,4},{7,5},{8,10},{9,11},{10,... | collective-permute-start | bytes 165896 | tf_op jit(solution)/shard_map/ppermute | solution.py:454
  45.0 2.4 %collective-permute-start.7 = (bf16[216,128]{1,0:T(8,128)(2,1)S(1)}, bf16[216,128]{1,0:T(8,128)(2,1)S(1)}, u32[]{:S(2)}, u32[]{:S(2)}) collective-permute-start(bf16[216,128]{1,0:T(8,128)(2,1)S(1)} %get-tuple-element.33), channel_id=1, source_target_pairs={{0,4},{1,5},{2,6},{3,7},{4,0},{5,1},{6,2},{7,3},{8,12},{9,13},{10,... | collective-permute-start | bytes 165896 | tf_op jit(solution)/shard_map/ppermute | solution.py:454
  48.1 2.8 %collective-permute-done.7.refs_6_ = bf16[216,128]{1,0:T(8,128)(2,1)S(1)} collective-permute-done((bf16[216,128]{1,0:T(8,128)(2,1)S(1)}, bf16[216,128]{1,0:T(8,128)(2,1)S(1)}, u32[]{:S(2)}, u32[]{:S(2)}) %collective-permute-start.7) | collective-permute-done | bytes 55328 | tf_op jit(solution)/shard_map/ppermute | solution.py:454
  50.8 2.6 %collective-permute-done.8.refs_7_ = bf16[216,128]{1,0:T(8,128)(2,1)S(1)} collective-permute-done((bf16[216,128]{1,0:T(8,128)(2,1)S(1)}, bf16[216,128]{1,0:T(8,128)(2,1)S(1)}, u32[]{:S(2)}, u32[]{:S(2)}) %collective-permute-start.8) | collective-permute-done | bytes 55328 | tf_op jit(solution)/shard_map/ppermute | solution.py:454
  53.8 1.9 %attend_own.1.before = f32[768,128]{1,0:T(8,128)S(1)} custom-call(s32[4]{0:T(128)S(1)} %copy-done.4, bf16[768,128]{1,0:T(8,128)(2,1)S(1)} %get-tuple-element.35.queries, bf16[768,256]{1,0:T(8,128)(2,1)S(1)} %get-tuple-element.36.key_value), custom_call_target="tpu_custom_call" | custom-call | flops 301989888 | bytes 589824 | tf_op jit(solution)/shard_map/attend_own/pallas_call | solution.py:377
  55.6 2.4 %attend_others.1 = (bf16[144,128]{1,0:T(8,128)(2,1)S(1)}, bf16[144,128]{1,0:T(8,128)(2,1)S(1)}, bf16[144,128]{1,0:T(8,128)(2,1)S(1)}, bf16[144,128]{1,0:T(8,128)(2,1)S(1)}) custom-call(s32[4]{0:T(128)S(1)} %copy-done.4, bf16[768,128]{1,0:T(8,128)(2,1)S(1)} %get-tuple-element.35.queries, f32[768,128]{1,0:T(8,128)S(1)} %attend_own.1.before, ...), custom_call_target="tpu_custom_call" | custom-call | tf_op jit(solution)/shard_map/attend_others/pallas_call | solution.py:387
  58.1 1.2 %collective-permute-start.11 = (bf16[144,128]{1,0:T(8,128)(2,1)S(1)}, bf16[144,128]{1,0:T(8,128)(2,1)S(1)}, u32[]{:S(2)}, u32[]{:S(2)}) collective-permute-start(bf16[144,128]{1,0:T(8,128)(2,1)S(1)} %get-tuple-element.39), channel_id=1, source_target_pairs={{0,4},{1,5},{2,6},{3,7},{4,0},{5,1},{6,2},{7,3},{8,12},{9,13},{10,... | collective-permute-start | bytes 110600 | tf_op jit(solution)/shard_map/ppermute | solution.py:454
  59.4 3.1 %collective-permute-start.12 = (bf16[144,128]{1,0:T(8,128)(2,1)S(1)}, bf16[144,128]{1,0:T(8,128)(2,1)S(1)}, u32[]{:S(2)}, u32[]{:S(2)}) collective-permute-start(bf16[144,128]{1,0:T(8,128)(2,1)S(1)} %get-tuple-element.40), channel_id=1, source_target_pairs={{0,6},{1,7},{2,4},{3,5},{4,2},{5,3},{6,0},{7,1},{8,14},{9,15},{10,... | collective-permute-start | bytes 110600 | tf_op jit(solution)/shard_map/ppermute | solution.py:454
  62.5 0.9 %collective-permute-done.11.refs_2_ = bf16[144,128]{1,0:T(8,128)(2,1)S(1)} collective-permute-done((bf16[144,128]{1,0:T(8,128)(2,1)S(1)}, bf16[144,128]{1,0:T(8,128)(2,1)S(1)}, u32[]{:S(2)}, u32[]{:S(2)}) %collective-permute-start.11) | collective-permute-done | bytes 36896 | tf_op jit(solution)/shard_map/ppermute | solution.py:454
  63.4 1.8 %collective-permute-done.12.refs_3_ = bf16[144,128]{1,0:T(8,128)(2,1)S(1)} collective-permute-done((bf16[144,128]{1,0:T(8,128)(2,1)S(1)}, bf16[144,128]{1,0:T(8,128)(2,1)S(1)}, u32[]{:S(2)}, u32[]{:S(2)}) %collective-permute-start.12) | collective-permute-done | bytes 36896 | tf_op jit(solution)/shard_map/ppermute | solution.py:454
  65.2 0.6 partial_out.1
  65.8 1.9 %collective-permute-start.13 = (bf16[48,1536]{1,0:T(8,128)(2,1)S(1)}, bf16[48,1536]{1,0:T(8,128)(2,1)S(1)}, u32[]{:S(2)}, u32[]{:S(2)}) collective-permute-start(bf16[48,1536]{1,0:T(8,128)(2,1)S(1)} %get-tuple-element.42), channel_id=1, source_target_pairs={{0,8},{8,0},{16,24},{24,16},{1,9},{9,1},{17,25},{25,17},{2,10},{10... | collective-permute-start | bytes 442376 | tf_op jit(solution)/shard_map/ppermute | solution.py:454
  67.7 1.5 %collective-permute-start.14 = (bf16[48,1536]{1,0:T(8,128)(2,1)S(1)}, bf16[48,1536]{1,0:T(8,128)(2,1)S(1)}, u32[]{:S(2)}, u32[]{:S(2)}) collective-permute-start(bf16[48,1536]{1,0:T(8,128)(2,1)S(1)} %get-tuple-element.43), channel_id=1, source_target_pairs={{0,16},{8,24},{16,0},{24,8},{1,17},{9,25},{17,1},{25,9},{2,18},{10... | collective-permute-start | bytes 442376 | tf_op jit(solution)/shard_map/ppermute | solution.py:454
  69.4 2.7 %collective-permute-done.13.refs_1_ = bf16[48,1536]{1,0:T(8,128)(2,1)S(1)} collective-permute-done((bf16[48,1536]{1,0:T(8,128)(2,1)S(1)}, bf16[48,1536]{1,0:T(8,128)(2,1)S(1)}, u32[]{:S(2)}, u32[]{:S(2)}) %collective-permute-start.13) | collective-permute-done | bytes 147488 | tf_op jit(solution)/shard_map/ppermute | solution.py:454
  72.0 3.8 %collective-permute-done.14.refs_2_ = bf16[48,1536]{1,0:T(8,128)(2,1)S(1)} collective-permute-done((bf16[48,1536]{1,0:T(8,128)(2,1)S(1)}, bf16[48,1536]{1,0:T(8,128)(2,1)S(1)}, u32[]{:S(2)}, u32[]{:S(2)}) %collective-permute-start.14) | collective-permute-done | bytes 147488 | tf_op jit(solution)/shard_map/ppermute | solution.py:454
  75.8 0.7 finish.1
  (26 shorter events, 1.2 us)
Async XLA Ops:
  0.0 36.1 %copy-start = (bf16[1536,384]{1,0:T(8,128)(2,1)S(1)}, bf16[1536,384]{1,0:T(8,128)(2,1)}, u32[]{:S(2)}) copy-start(bf16[1536,384]{1,0:T(8,128)(2,1)} %refs_2_.3) | copy-start | bytes 3538948
  0.0 36.1 %copy-start.1 = (bf16[1536,384]{1,0:T(8,128)(2,1)S(1)}, bf16[1536,384]{1,0:T(8,128)(2,1)}, u32[]{:S(2)}) copy-start(bf16[1536,384]{1,0:T(8,128)(2,1)} %refs_3_.3) | copy-start | bytes 3538948
  0.0 36.1 %copy-start.2 = (bf16[1536,384]{1,0:T(8,128)(2,1)S(1)}, bf16[1536,384]{1,0:T(8,128)(2,1)}, u32[]{:S(2)}) copy-start(bf16[1536,384]{1,0:T(8,128)(2,1)} %refs_4_.4) | copy-start | bytes 3538948
  28.7 7.3 %collective-permute-start = (bf16[48,1536]{1,0:T(8,128)(2,1)S(1)}, bf16[48,1536]{1,0:T(8,128)(2,1)S(1)}, u32[]{:S(2)}, u32[]{:S(2)}) collective-permute-start(bf16[48,1536]{1,0:T(8,128)(2,1)S(1)} %encode.1.refs_0_.emb), channel_id=1, source_target_pairs={{0,8},{8,0},{16,24},{24,16},{1,9},{9,1},{17,25},{25,17},{2,10},{10... | collective-permute-start | bytes 442376 | tf_op jit(solution)/shard_map/ppermute | solution.py:454
  31.8 10.1 %collective-permute-start.4 = (bf16[48,1536]{1,0:T(8,128)(2,1)S(1)}, bf16[48,1536]{1,0:T(8,128)(2,1)S(1)}, u32[]{:S(2)}, u32[]{:S(2)}) collective-permute-start(bf16[48,1536]{1,0:T(8,128)(2,1)S(1)} %encode.1.refs_0_.emb), channel_id=1, source_target_pairs={{0,16},{8,24},{16,0},{24,8},{1,17},{9,25},{17,1},{25,9},{2,18},{10... | collective-permute-start | bytes 442376 | tf_op jit(solution)/shard_map/ppermute | solution.py:454
  33.3 8.6 %collective-permute-start.5 = (bf16[48,1536]{1,0:T(8,128)(2,1)S(1)}, bf16[48,1536]{1,0:T(8,128)(2,1)S(1)}, u32[]{:S(2)}, u32[]{:S(2)}) collective-permute-start(bf16[48,1536]{1,0:T(8,128)(2,1)S(1)} %encode.1.refs_0_.emb), channel_id=1, source_target_pairs={{0,24},{8,16},{16,8},{24,0},{1,25},{9,17},{17,9},{25,1},{2,26},{10... | collective-permute-start | bytes 442376 | tf_op jit(solution)/shard_map/ppermute | solution.py:454
  37.1 4.8 %collective-permute-start.1 = (bf16[216,128]{1,0:T(8,128)(2,1)S(1)}, bf16[216,128]{1,0:T(8,128)(2,1)S(1)}, u32[]{:S(2)}, u32[]{:S(2)}) collective-permute-start(bf16[216,128]{1,0:T(8,128)(2,1)S(1)} %get-tuple-element.26), channel_id=1, source_target_pairs={{0,2},{1,3},{2,0},{3,1},{4,6},{5,7},{6,4},{7,5},{8,10},{9,11},{10,... | collective-permute-start | bytes 165896 | tf_op jit(solution)/shard_map/ppermute | solution.py:454
  39.3 8.2 %collective-permute-start.2 = (bf16[216,128]{1,0:T(8,128)(2,1)S(1)}, bf16[216,128]{1,0:T(8,128)(2,1)S(1)}, u32[]{:S(2)}, u32[]{:S(2)}) collective-permute-start(bf16[216,128]{1,0:T(8,128)(2,1)S(1)} %get-tuple-element.27), channel_id=1, source_target_pairs={{0,4},{1,5},{2,6},{3,7},{4,0},{5,1},{6,2},{7,3},{8,12},{9,13},{10,... | collective-permute-start | bytes 165896 | tf_op jit(solution)/shard_map/ppermute | solution.py:454
  41.9 11.9 %copy-start.4 = (s32[4]{0:T(128)S(1)}, s32[4]{0:T(128)}, u32[]{:S(2)}) copy-start(s32[4]{0:T(128)} %slide_tiles.3) | copy-start | bytes 52
  41.9 6.1 %collective-permute-start.3 = (bf16[216,128]{1,0:T(8,128)(2,1)S(1)}, bf16[216,128]{1,0:T(8,128)(2,1)S(1)}, u32[]{:S(2)}, u32[]{:S(2)}) collective-permute-start(bf16[216,128]{1,0:T(8,128)(2,1)S(1)} %get-tuple-element.28), channel_id=1, source_target_pairs={{0,6},{1,7},{2,4},{3,5},{4,2},{5,3},{6,0},{7,1},{8,14},{9,15},{10,... | collective-permute-start | bytes 165896 | tf_op jit(solution)/shard_map/ppermute | solution.py:454
  42.9 22.2 %copy-start.3 = (bf16[384,1536]{1,0:T(8,128)(2,1)S(1)}, bf16[384,1536]{1,0:T(8,128)(2,1)}, u32[]{:S(2)}) copy-start(bf16[384,1536]{1,0:T(8,128)(2,1)} %refs_4_.5) | copy-start | bytes 3538948
  42.9 5.1 %collective-permute-start.6 = (bf16[216,128]{1,0:T(8,128)(2,1)S(1)}, bf16[216,128]{1,0:T(8,128)(2,1)S(1)}, u32[]{:S(2)}, u32[]{:S(2)}) collective-permute-start(bf16[216,128]{1,0:T(8,128)(2,1)S(1)} %get-tuple-element.32), channel_id=1, source_target_pairs={{0,2},{1,3},{2,0},{3,1},{4,6},{5,7},{6,4},{7,5},{8,10},{9,11},{10,... | collective-permute-start | bytes 165896 | tf_op jit(solution)/shard_map/ppermute | solution.py:454
  45.0 5.8 %collective-permute-start.7 = (bf16[216,128]{1,0:T(8,128)(2,1)S(1)}, bf16[216,128]{1,0:T(8,128)(2,1)S(1)}, u32[]{:S(2)}, u32[]{:S(2)}) collective-permute-start(bf16[216,128]{1,0:T(8,128)(2,1)S(1)} %get-tuple-element.33), channel_id=1, source_target_pairs={{0,4},{1,5},{2,6},{3,7},{4,0},{5,1},{6,2},{7,3},{8,12},{9,13},{10,... | collective-permute-start | bytes 165896 | tf_op jit(solution)/shard_map/ppermute | solution.py:454
  47.5 6.0 %collective-permute-start.8 = (bf16[216,128]{1,0:T(8,128)(2,1)S(1)}, bf16[216,128]{1,0:T(8,128)(2,1)S(1)}, u32[]{:S(2)}, u32[]{:S(2)}) collective-permute-start(bf16[216,128]{1,0:T(8,128)(2,1)S(1)} %get-tuple-element.34), channel_id=1, source_target_pairs={{0,6},{1,7},{2,4},{3,5},{4,2},{5,3},{6,0},{7,1},{8,14},{9,15},{10,... | collective-permute-start | bytes 165896 | tf_op jit(solution)/shard_map/ppermute | solution.py:454
  53.7 2.0 %collective-permute-start.9 = (bf16[768,256]{1,0:T(8,128)(2,1)S(1)}, bf16[768,256]{1,0:T(8,128)(2,1)S(1)}, u32[]{:S(2)}, u32[]{:S(2)}) collective-permute-start(bf16[768,256]{1,0:T(8,128)(2,1)S(1)} %get-tuple-element.36.key_value), channel_id=1, source_target_pairs={{0,1},{1,0},{2,3},{3,2},{4,5},{5,4},{6,7},{7,6},{8,9},{9,8},{10,11... | collective-permute-start | bytes 1179656 | tf_op jit(solution)/shard_map/ppermute | solution.py:454
  58.0 4.5 %collective-permute-start.10 = (bf16[144,128]{1,0:T(8,128)(2,1)S(1)}, bf16[144,128]{1,0:T(8,128)(2,1)S(1)}, u32[]{:S(2)}, u32[]{:S(2)}) collective-permute-start(bf16[144,128]{1,0:T(8,128)(2,1)S(1)} %get-tuple-element.38), channel_id=1, source_target_pairs={{0,2},{1,3},{2,0},{3,1},{4,6},{5,7},{6,4},{7,5},{8,10},{9,11},{10,... | collective-permute-start | bytes 110600 | tf_op jit(solution)/shard_map/ppermute | solution.py:454
  58.1 5.2 %collective-permute-start.11 = (bf16[144,128]{1,0:T(8,128)(2,1)S(1)}, bf16[144,128]{1,0:T(8,128)(2,1)S(1)}, u32[]{:S(2)}, u32[]{:S(2)}) collective-permute-start(bf16[144,128]{1,0:T(8,128)(2,1)S(1)} %get-tuple-element.39), channel_id=1, source_target_pairs={{0,4},{1,5},{2,6},{3,7},{4,0},{5,1},{6,2},{7,3},{8,12},{9,13},{10,... | collective-permute-start | bytes 110600 | tf_op jit(solution)/shard_map/ppermute | solution.py:454
  59.4 5.8 %collective-permute-start.12 = (bf16[144,128]{1,0:T(8,128)(2,1)S(1)}, bf16[144,128]{1,0:T(8,128)(2,1)S(1)}, u32[]{:S(2)}, u32[]{:S(2)}) collective-permute-start(bf16[144,128]{1,0:T(8,128)(2,1)S(1)} %get-tuple-element.40), channel_id=1, source_target_pairs={{0,6},{1,7},{2,4},{3,5},{4,2},{5,3},{6,0},{7,1},{8,14},{9,15},{10,... | collective-permute-start | bytes 110600 | tf_op jit(solution)/shard_map/ppermute | solution.py:454
  65.8 6.2 %collective-permute-start.13 = (bf16[48,1536]{1,0:T(8,128)(2,1)S(1)}, bf16[48,1536]{1,0:T(8,128)(2,1)S(1)}, u32[]{:S(2)}, u32[]{:S(2)}) collective-permute-start(bf16[48,1536]{1,0:T(8,128)(2,1)S(1)} %get-tuple-element.42), channel_id=1, source_target_pairs={{0,8},{8,0},{16,24},{24,16},{1,9},{9,1},{17,25},{25,17},{2,10},{10... | collective-permute-start | bytes 442376 | tf_op jit(solution)/shard_map/ppermute | solution.py:454
  67.7 8.2 %collective-permute-start.14 = (bf16[48,1536]{1,0:T(8,128)(2,1)S(1)}, bf16[48,1536]{1,0:T(8,128)(2,1)S(1)}, u32[]{:S(2)}, u32[]{:S(2)}) collective-permute-start(bf16[48,1536]{1,0:T(8,128)(2,1)S(1)} %get-tuple-element.43), channel_id=1, source_target_pairs={{0,16},{8,24},{16,0},{24,8},{1,17},{9,25},{17,1},{25,9},{2,18},{10... | collective-permute-start | bytes 442376 | tf_op jit(solution)/shard_map/ppermute | solution.py:454
  69.2 6.6 %collective-permute-start.15 = (bf16[48,1536]{1,0:T(8,128)(2,1)S(1)}, bf16[48,1536]{1,0:T(8,128)(2,1)S(1)}, u32[]{:S(2)}, u32[]{:S(2)}) collective-permute-start(bf16[48,1536]{1,0:T(8,128)(2,1)S(1)} %get-tuple-element.44), channel_id=1, source_target_pairs={{0,24},{8,16},{16,8},{24,0},{1,25},{9,17},{17,9},{25,1},{2,26},{10... | collective-permute-start | bytes 442376 | tf_op jit(solution)/shard_map/ppermute | solution.py:454

commit v10 on v9

--- a/solution.py
+++ b/solution.py
@@ -103,9 +103,9 @@
             g = (step + 1) // 2 * per + i
             x_copy(g).wait()
 
-            @pl.when(g + 2 < parts)
+            @pl.when((g >= 1) & (g + 1 < parts))
             def _():
-                x_copy(g + 2).start()
+                x_copy(g + 1).start()
 
             @pl.when(g + 1 < early)
             def _():

time: 76.7 us -> 76.8 us (level)
  no operation moved by 1% of the time
where the time goes in v10:
time: 76.8 us; the launch traced here: 76.7 us
  Pallas kernels  36.7 us (48%)
  starting transfers between devices  21.9 us (29%)
  waiting for transfers between devices  17.9 us (23%)
    pallas_call x1, Pallas kernels, encode(): pl.pallas_call(encode_kernel, grid=(2 * count // GROUP,), in_specs=[pl.Bl...  28.8 us
    ppermute x16, starting transfers between devices, along(): return lax.ppermute(x, axis, [(i, i ^ step) for i in range(size)])  21.9 us
    ppermute x16, waiting for transfers between devices, along(): return lax.ppermute(x, axis, [(i, i ^ step) for i in range(size)])  17.9 us
    pallas_call x1, Pallas kernels, attend(): pl.pallas_call(functools.partial(attend_others_kernel, layout, len(others...  2.39 us
    pallas_call x2, Pallas kernels, project(): pl.pallas_call(functools.partial(project_kernel, heads, spread_of, len(em...  2.06 us
    pallas_call x1, Pallas kernels, attend(): pl.pallas_call(functools.partial(attend_own_kernel, layout), in_specs=[sm...  1.86 us
  transfers between devices with their start and end apart: 16, of which 9 were waited for; matrix products, arithmetic and copies ran while one was open for 0% of the time, Pallas kernels for 5%

profile of v10, /device:TPU:0, one launch (start us, length us, event | category | flops | bytes accessed | tf_op | source)
XLA Modules:
  0.0 76.7 jit_solution(3296031831704642570)
XLA Ops:
  0.0 28.8 %encode.1.refs_0_.emb = bf16[48,1536]{1,0:T(8,128)(2,1)S(1)} custom-call(bf16[3072,2048]{1,0:T(8,128)(2,1)} %bitcast.2, bf16[2048,512]{1,0:T(8,128)(2,1)} %wr_hbm.1, bf16[3,1536,512]{2,1,0:T(8,128)(2,1)} %bitcast.3, bf16[512,2048]{1,0:T(8,128)(2,1)} %we_hbm.1, bf16[2048,1536]{1,0:T(8,128)(2,1)} %wm_hbm.1), custom_call_target="tpu_custom_call" | custom-call | flops 27380416512 | bytes 27787264 | tf_op jit(solution)/shard_map/encode/pallas_call | solution.py:170
  28.8 3.0 %collective-permute-start = (bf16[48,1536]{1,0:T(8,128)(2,1)S(1)}, bf16[48,1536]{1,0:T(8,128)(2,1)S(1)}, u32[]{:S(2)}, u32[]{:S(2)}) collective-permute-start(bf16[48,1536]{1,0:T(8,128)(2,1)S(1)} %encode.1.refs_0_.emb), channel_id=1, source_target_pairs={{0,8},{8,0},{16,24},{24,16},{1,9},{9,1},{17,25},{25,17},{2,10},{10... | collective-permute-start | bytes 442376 | tf_op jit(solution)/shard_map/ppermute | solution.py:454
  31.8 1.5 %collective-permute-start.4 = (bf16[48,1536]{1,0:T(8,128)(2,1)S(1)}, bf16[48,1536]{1,0:T(8,128)(2,1)S(1)}, u32[]{:S(2)}, u32[]{:S(2)}) collective-permute-start(bf16[48,1536]{1,0:T(8,128)(2,1)S(1)} %encode.1.refs_0_.emb), channel_id=1, source_target_pairs={{0,16},{8,24},{16,0},{24,8},{1,17},{9,25},{17,1},{25,9},{2,18},{10... | collective-permute-start | bytes 442376 | tf_op jit(solution)/shard_map/ppermute | solution.py:454
  33.4 2.8 %collective-permute-done.refs_1_ = bf16[48,1536]{1,0:T(8,128)(2,1)S(1)} collective-permute-done((bf16[48,1536]{1,0:T(8,128)(2,1)S(1)}, bf16[48,1536]{1,0:T(8,128)(2,1)S(1)}, u32[]{:S(2)}, u32[]{:S(2)}) %collective-permute-start) | collective-permute-done | bytes 147488 | tf_op jit(solution)/shard_map/ppermute | solution.py:454
  36.1 1.0 %project.2 = (bf16[216,128]{1,0:T(8,128)(2,1)S(1)}, bf16[216,128]{1,0:T(8,128)(2,1)S(1)}, bf16[216,128]{1,0:T(8,128)(2,1)S(1)}, bf16[216,128]{1,0:T(8,128)(2,1)S(1)}) custom-call(bf16[48,1536]{1,0:T(8,128)(2,1)S(1)} %encode.1.refs_0_.emb, bf16[48,1536]{1,0:T(8,128)(2,1)S(1)} %collective-permute-done.refs_1_, bf16[1536,384]{1,0:T(8,128)(2,1)S(1)} %copy-done, ...), custom_call_target="tpu_custom_call" | custom-call | flops 339738624 | bytes 3538944 | tf_op jit(solution)/shard_map/project/pallas_call | solution.py:225
  37.2 2.2 %collective-permute-start.1 = (bf16[216,128]{1,0:T(8,128)(2,1)S(1)}, bf16[216,128]{1,0:T(8,128)(2,1)S(1)}, u32[]{:S(2)}, u32[]{:S(2)}) collective-permute-start(bf16[216,128]{1,0:T(8,128)(2,1)S(1)} %get-tuple-element.26), channel_id=1, source_target_pairs={{0,2},{1,3},{2,0},{3,1},{4,6},{5,7},{6,4},{7,5},{8,10},{9,11},{10,... | collective-permute-start | bytes 165896 | tf_op jit(solution)/shard_map/ppermute | solution.py:454
  39.3 2.6 %collective-permute-start.2 = (bf16[216,128]{1,0:T(8,128)(2,1)S(1)}, bf16[216,128]{1,0:T(8,128)(2,1)S(1)}, u32[]{:S(2)}, u32[]{:S(2)}) collective-permute-start(bf16[216,128]{1,0:T(8,128)(2,1)S(1)} %get-tuple-element.27), channel_id=1, source_target_pairs={{0,4},{1,5},{2,6},{3,7},{4,0},{5,1},{6,2},{7,3},{8,12},{9,13},{10,... | collective-permute-start | bytes 165896 | tf_op jit(solution)/shard_map/ppermute | solution.py:454
  42.0 1.0 %project.3 = (bf16[216,128]{1,0:T(8,128)(2,1)S(1)}, bf16[216,128]{1,0:T(8,128)(2,1)S(1)}, bf16[216,128]{1,0:T(8,128)(2,1)S(1)}, bf16[216,128]{1,0:T(8,128)(2,1)S(1)}) custom-call(bf16[48,1536]{1,0:T(8,128)(2,1)S(1)} %collective-permute-done.4.refs_0_, bf16[48,1536]{1,0:T(8,128)(2,1)S(1)} %collective-permute-done.5.refs_1_, bf16[1536,384]{1,0:T(8,128)(2,1)S(1)} %copy-done, ...), custom_call_target="tpu_custom_call" | custom-call | flops 339738624 | bytes 3538944 | tf_op jit(solution)/shard_map/project/pallas_call | solution.py:225
  43.0 2.1 %collective-permute-start.6 = (bf16[216,128]{1,0:T(8,128)(2,1)S(1)}, bf16[216,128]{1,0:T(8,128)(2,1)S(1)}, u32[]{:S(2)}, u32[]{:S(2)}) collective-permute-start(bf16[216,128]{1,0:T(8,128)(2,1)S(1)} %get-tuple-element.32), channel_id=1, source_target_pairs={{0,2},{1,3},{2,0},{3,1},{4,6},{5,7},{6,4},{7,5},{8,10},{9,11},{10,... | collective-permute-start | bytes 165896 | tf_op jit(solution)/shard_map/ppermute | solution.py:454
  45.1 2.4 %collective-permute-start.7 = (bf16[216,128]{1,0:T(8,128)(2,1)S(1)}, bf16[216,128]{1,0:T(8,128)(2,1)S(1)}, u32[]{:S(2)}, u32[]{:S(2)}) collective-permute-start(bf16[216,128]{1,0:T(8,128)(2,1)S(1)} %get-tuple-element.33), channel_id=1, source_target_pairs={{0,4},{1,5},{2,6},{3,7},{4,0},{5,1},{6,2},{7,3},{8,12},{9,13},{10,... | collective-permute-start | bytes 165896 | tf_op jit(solution)/shard_map/ppermute | solution.py:454
  48.1 2.8 %collective-permute-done.7.refs_6_ = bf16[216,128]{1,0:T(8,128)(2,1)S(1)} collective-permute-done((bf16[216,128]{1,0:T(8,128)(2,1)S(1)}, bf16[216,128]{1,0:T(8,128)(2,1)S(1)}, u32[]{:S(2)}, u32[]{:S(2)}) %collective-permute-start.7) | collective-permute-done | bytes 55328 | tf_op jit(solution)/shard_map/ppermute | solution.py:454
  50.9 2.6 %collective-permute-done.8.refs_7_ = bf16[216,128]{1,0:T(8,128)(2,1)S(1)} collective-permute-done((bf16[216,128]{1,0:T(8,128)(2,1)S(1)}, bf16[216,128]{1,0:T(8,128)(2,1)S(1)}, u32[]{:S(2)}, u32[]{:S(2)}) %collective-permute-start.8) | collective-permute-done | bytes 55328 | tf_op jit(solution)/shard_map/ppermute | solution.py:454
  53.8 1.9 %attend_own.1.before = f32[768,128]{1,0:T(8,128)S(1)} custom-call(s32[4]{0:T(128)S(1)} %copy-done.4, bf16[768,128]{1,0:T(8,128)(2,1)S(1)} %get-tuple-element.35.queries, bf16[768,256]{1,0:T(8,128)(2,1)S(1)} %get-tuple-element.36.key_value), custom_call_target="tpu_custom_call" | custom-call | flops 301989888 | bytes 589824 | tf_op jit(solution)/shard_map/attend_own/pallas_call | solution.py:377
  55.7 2.4 %attend_others.1 = (bf16[144,128]{1,0:T(8,128)(2,1)S(1)}, bf16[144,128]{1,0:T(8,128)(2,1)S(1)}, bf16[144,128]{1,0:T(8,128)(2,1)S(1)}, bf16[144,128]{1,0:T(8,128)(2,1)S(1)}) custom-call(s32[4]{0:T(128)S(1)} %copy-done.4, bf16[768,128]{1,0:T(8,128)(2,1)S(1)} %get-tuple-element.35.queries, f32[768,128]{1,0:T(8,128)S(1)} %attend_own.1.before, ...), custom_call_target="tpu_custom_call" | custom-call | tf_op jit(solution)/shard_map/attend_others/pallas_call | solution.py:387
  58.2 1.2 %collective-permute-start.11 = (bf16[144,128]{1,0:T(8,128)(2,1)S(1)}, bf16[144,128]{1,0:T(8,128)(2,1)S(1)}, u32[]{:S(2)}, u32[]{:S(2)}) collective-permute-start(bf16[144,128]{1,0:T(8,128)(2,1)S(1)} %get-tuple-element.39), channel_id=1, source_target_pairs={{0,4},{1,5},{2,6},{3,7},{4,0},{5,1},{6,2},{7,3},{8,12},{9,13},{10,... | collective-permute-start | bytes 110600 | tf_op jit(solution)/shard_map/ppermute | solution.py:454
  59.4 3.1 %collective-permute-start.12 = (bf16[144,128]{1,0:T(8,128)(2,1)S(1)}, bf16[144,128]{1,0:T(8,128)(2,1)S(1)}, u32[]{:S(2)}, u32[]{:S(2)}) collective-permute-start(bf16[144,128]{1,0:T(8,128)(2,1)S(1)} %get-tuple-element.40), channel_id=1, source_target_pairs={{0,6},{1,7},{2,4},{3,5},{4,2},{5,3},{6,0},{7,1},{8,14},{9,15},{10,... | collective-permute-start | bytes 110600 | tf_op jit(solution)/shard_map/ppermute | solution.py:454
  62.6 0.9 %collective-permute-done.11.refs_2_ = bf16[144,128]{1,0:T(8,128)(2,1)S(1)} collective-permute-done((bf16[144,128]{1,0:T(8,128)(2,1)S(1)}, bf16[144,128]{1,0:T(8,128)(2,1)S(1)}, u32[]{:S(2)}, u32[]{:S(2)}) %collective-permute-start.11) | collective-permute-done | bytes 36896 | tf_op jit(solution)/shard_map/ppermute | solution.py:454
  63.4 1.8 %collective-permute-done.12.refs_3_ = bf16[144,128]{1,0:T(8,128)(2,1)S(1)} collective-permute-done((bf16[144,128]{1,0:T(8,128)(2,1)S(1)}, bf16[144,128]{1,0:T(8,128)(2,1)S(1)}, u32[]{:S(2)}, u32[]{:S(2)}) %collective-permute-start.12) | collective-permute-done | bytes 36896 | tf_op jit(solution)/shard_map/ppermute | solution.py:454
  65.2 0.6 partial_out.1
  65.9 1.9 %collective-permute-start.13 = (bf16[48,1536]{1,0:T(8,128)(2,1)S(1)}, bf16[48,1536]{1,0:T(8,128)(2,1)S(1)}, u32[]{:S(2)}, u32[]{:S(2)}) collective-permute-start(bf16[48,1536]{1,0:T(8,128)(2,1)S(1)} %get-tuple-element.42), channel_id=1, source_target_pairs={{0,8},{8,0},{16,24},{24,16},{1,9},{9,1},{17,25},{25,17},{2,10},{10... | collective-permute-start | bytes 442376 | tf_op jit(solution)/shard_map/ppermute | solution.py:454
  67.7 1.5 %collective-permute-start.14 = (bf16[48,1536]{1,0:T(8,128)(2,1)S(1)}, bf16[48,1536]{1,0:T(8,128)(2,1)S(1)}, u32[]{:S(2)}, u32[]{:S(2)}) collective-permute-start(bf16[48,1536]{1,0:T(8,128)(2,1)S(1)} %get-tuple-element.43), channel_id=1, source_target_pairs={{0,16},{8,24},{16,0},{24,8},{1,17},{9,25},{17,1},{25,9},{2,18},{10... | collective-permute-start | bytes 442376 | tf_op jit(solution)/shard_map/ppermute | solution.py:454
  69.4 2.7 %collective-permute-done.13.refs_1_ = bf16[48,1536]{1,0:T(8,128)(2,1)S(1)} collective-permute-done((bf16[48,1536]{1,0:T(8,128)(2,1)S(1)}, bf16[48,1536]{1,0:T(8,128)(2,1)S(1)}, u32[]{:S(2)}, u32[]{:S(2)}) %collective-permute-start.13) | collective-permute-done | bytes 147488 | tf_op jit(solution)/shard_map/ppermute | solution.py:454
  72.1 3.8 %collective-permute-done.14.refs_2_ = bf16[48,1536]{1,0:T(8,128)(2,1)S(1)} collective-permute-done((bf16[48,1536]{1,0:T(8,128)(2,1)S(1)}, bf16[48,1536]{1,0:T(8,128)(2,1)S(1)}, u32[]{:S(2)}, u32[]{:S(2)}) %collective-permute-start.14) | collective-permute-done | bytes 147488 | tf_op jit(solution)/shard_map/ppermute | solution.py:454
  75.9 0.7 finish.1
  (26 shorter events, 1.2 us)
Async XLA Ops:
  0.0 36.1 %copy-start = (bf16[1536,384]{1,0:T(8,128)(2,1)S(1)}, bf16[1536,384]{1,0:T(8,128)(2,1)}, u32[]{:S(2)}) copy-start(bf16[1536,384]{1,0:T(8,128)(2,1)} %refs_2_.3) | copy-start | bytes 3538948
  0.0 36.1 %copy-start.1 = (bf16[1536,384]{1,0:T(8,128)(2,1)S(1)}, bf16[1536,384]{1,0:T(8,128)(2,1)}, u32[]{:S(2)}) copy-start(bf16[1536,384]{1,0:T(8,128)(2,1)} %refs_3_.3) | copy-start | bytes 3538948
  0.0 36.1 %copy-start.2 = (bf16[1536,384]{1,0:T(8,128)(2,1)S(1)}, bf16[1536,384]{1,0:T(8,128)(2,1)}, u32[]{:S(2)}) copy-start(bf16[1536,384]{1,0:T(8,128)(2,1)} %refs_4_.4) | copy-start | bytes 3538948
  28.8 7.3 %collective-permute-start = (bf16[48,1536]{1,0:T(8,128)(2,1)S(1)}, bf16[48,1536]{1,0:T(8,128)(2,1)S(1)}, u32[]{:S(2)}, u32[]{:S(2)}) collective-permute-start(bf16[48,1536]{1,0:T(8,128)(2,1)S(1)} %encode.1.refs_0_.emb), channel_id=1, source_target_pairs={{0,8},{8,0},{16,24},{24,16},{1,9},{9,1},{17,25},{25,17},{2,10},{10... | collective-permute-start | bytes 442376 | tf_op jit(solution)/shard_map/ppermute | solution.py:454
  31.8 10.1 %collective-permute-start.4 = (bf16[48,1536]{1,0:T(8,128)(2,1)S(1)}, bf16[48,1536]{1,0:T(8,128)(2,1)S(1)}, u32[]{:S(2)}, u32[]{:S(2)}) collective-permute-start(bf16[48,1536]{1,0:T(8,128)(2,1)S(1)} %encode.1.refs_0_.emb), channel_id=1, source_target_pairs={{0,16},{8,24},{16,0},{24,8},{1,17},{9,25},{17,1},{25,9},{2,18},{10... | collective-permute-start | bytes 442376 | tf_op jit(solution)/shard_map/ppermute | solution.py:454
  33.4 8.6 %collective-permute-start.5 = (bf16[48,1536]{1,0:T(8,128)(2,1)S(1)}, bf16[48,1536]{1,0:T(8,128)(2,1)S(1)}, u32[]{:S(2)}, u32[]{:S(2)}) collective-permute-start(bf16[48,1536]{1,0:T(8,128)(2,1)S(1)} %encode.1.refs_0_.emb), channel_id=1, source_target_pairs={{0,24},{8,16},{16,8},{24,0},{1,25},{9,17},{17,9},{25,1},{2,26},{10... | collective-permute-start | bytes 442376 | tf_op jit(solution)/shard_map/ppermute | solution.py:454
  37.2 4.8 %collective-permute-start.1 = (bf16[216,128]{1,0:T(8,128)(2,1)S(1)}, bf16[216,128]{1,0:T(8,128)(2,1)S(1)}, u32[]{:S(2)}, u32[]{:S(2)}) collective-permute-start(bf16[216,128]{1,0:T(8,128)(2,1)S(1)} %get-tuple-element.26), channel_id=1, source_target_pairs={{0,2},{1,3},{2,0},{3,1},{4,6},{5,7},{6,4},{7,5},{8,10},{9,11},{10,... | collective-permute-start | bytes 165896 | tf_op jit(solution)/shard_map/ppermute | solution.py:454
  39.3 8.2 %collective-permute-start.2 = (bf16[216,128]{1,0:T(8,128)(2,1)S(1)}, bf16[216,128]{1,0:T(8,128)(2,1)S(1)}, u32[]{:S(2)}, u32[]{:S(2)}) collective-permute-start(bf16[216,128]{1,0:T(8,128)(2,1)S(1)} %get-tuple-element.27), channel_id=1, source_target_pairs={{0,4},{1,5},{2,6},{3,7},{4,0},{5,1},{6,2},{7,3},{8,12},{9,13},{10,... | collective-permute-start | bytes 165896 | tf_op jit(solution)/shard_map/ppermute | solution.py:454
  41.9 11.9 %copy-start.4 = (s32[4]{0:T(128)S(1)}, s32[4]{0:T(128)}, u32[]{:S(2)}) copy-start(s32[4]{0:T(128)} %slide_tiles.3) | copy-start | bytes 52
  41.9 6.1 %collective-permute-start.3 = (bf16[216,128]{1,0:T(8,128)(2,1)S(1)}, bf16[216,128]{1,0:T(8,128)(2,1)S(1)}, u32[]{:S(2)}, u32[]{:S(2)}) collective-permute-start(bf16[216,128]{1,0:T(8,128)(2,1)S(1)} %get-tuple-element.28), channel_id=1, source_target_pairs={{0,6},{1,7},{2,4},{3,5},{4,2},{5,3},{6,0},{7,1},{8,14},{9,15},{10,... | collective-permute-start | bytes 165896 | tf_op jit(solution)/shard_map/ppermute | solution.py:454
  43.0 22.2 %copy-start.3 = (bf16[384,1536]{1,0:T(8,128)(2,1)S(1)}, bf16[384,1536]{1,0:T(8,128)(2,1)}, u32[]{:S(2)}) copy-start(bf16[384,1536]{1,0:T(8,128)(2,1)} %refs_4_.5) | copy-start | bytes 3538948
  43.0 5.1 %collective-permute-start.6 = (bf16[216,128]{1,0:T(8,128)(2,1)S(1)}, bf16[216,128]{1,0:T(8,128)(2,1)S(1)}, u32[]{:S(2)}, u32[]{:S(2)}) collective-permute-start(bf16[216,128]{1,0:T(8,128)(2,1)S(1)} %get-tuple-element.32), channel_id=1, source_target_pairs={{0,2},{1,3},{2,0},{3,1},{4,6},{5,7},{6,4},{7,5},{8,10},{9,11},{10,... | collective-permute-start | bytes 165896 | tf_op jit(solution)/shard_map/ppermute | solution.py:454
  45.1 5.8 %collective-permute-start.7 = (bf16[216,128]{1,0:T(8,128)(2,1)S(1)}, bf16[216,128]{1,0:T(8,128)(2,1)S(1)}, u32[]{:S(2)}, u32[]{:S(2)}) collective-permute-start(bf16[216,128]{1,0:T(8,128)(2,1)S(1)} %get-tuple-element.33), channel_id=1, source_target_pairs={{0,4},{1,5},{2,6},{3,7},{4,0},{5,1},{6,2},{7,3},{8,12},{9,13},{10,... | collective-permute-start | bytes 165896 | tf_op jit(solution)/shard_map/ppermute | solution.py:454
  47.6 6.0 %collective-permute-start.8 = (bf16[216,128]{1,0:T(8,128)(2,1)S(1)}, bf16[216,128]{1,0:T(8,128)(2,1)S(1)}, u32[]{:S(2)}, u32[]{:S(2)}) collective-permute-start(bf16[216,128]{1,0:T(8,128)(2,1)S(1)} %get-tuple-element.34), channel_id=1, source_target_pairs={{0,6},{1,7},{2,4},{3,5},{4,2},{5,3},{6,0},{7,1},{8,14},{9,15},{10,... | collective-permute-start | bytes 165896 | tf_op jit(solution)/shard_map/ppermute | solution.py:454
  53.7 2.0 %collective-permute-start.9 = (bf16[768,256]{1,0:T(8,128)(2,1)S(1)}, bf16[768,256]{1,0:T(8,128)(2,1)S(1)}, u32[]{:S(2)}, u32[]{:S(2)}) collective-permute-start(bf16[768,256]{1,0:T(8,128)(2,1)S(1)} %get-tuple-element.36.key_value), channel_id=1, source_target_pairs={{0,1},{1,0},{2,3},{3,2},{4,5},{5,4},{6,7},{7,6},{8,9},{9,8},{10,11... | collective-permute-start | bytes 1179656 | tf_op jit(solution)/shard_map/ppermute | solution.py:454
  58.1 4.5 %collective-permute-start.10 = (bf16[144,128]{1,0:T(8,128)(2,1)S(1)}, bf16[144,128]{1,0:T(8,128)(2,1)S(1)}, u32[]{:S(2)}, u32[]{:S(2)}) collective-permute-start(bf16[144,128]{1,0:T(8,128)(2,1)S(1)} %get-tuple-element.38), channel_id=1, source_target_pairs={{0,2},{1,3},{2,0},{3,1},{4,6},{5,7},{6,4},{7,5},{8,10},{9,11},{10,... | collective-permute-start | bytes 110600 | tf_op jit(solution)/shard_map/ppermute | solution.py:454
  58.2 5.2 %collective-permute-start.11 = (bf16[144,128]{1,0:T(8,128)(2,1)S(1)}, bf16[144,128]{1,0:T(8,128)(2,1)S(1)}, u32[]{:S(2)}, u32[]{:S(2)}) collective-permute-start(bf16[144,128]{1,0:T(8,128)(2,1)S(1)} %get-tuple-element.39), channel_id=1, source_target_pairs={{0,4},{1,5},{2,6},{3,7},{4,0},{5,1},{6,2},{7,3},{8,12},{9,13},{10,... | collective-permute-start | bytes 110600 | tf_op jit(solution)/shard_map/ppermute | solution.py:454
  59.4 5.8 %collective-permute-start.12 = (bf16[144,128]{1,0:T(8,128)(2,1)S(1)}, bf16[144,128]{1,0:T(8,128)(2,1)S(1)}, u32[]{:S(2)}, u32[]{:S(2)}) collective-permute-start(bf16[144,128]{1,0:T(8,128)(2,1)S(1)} %get-tuple-element.40), channel_id=1, source_target_pairs={{0,6},{1,7},{2,4},{3,5},{4,2},{5,3},{6,0},{7,1},{8,14},{9,15},{10,... | collective-permute-start | bytes 110600 | tf_op jit(solution)/shard_map/ppermute | solution.py:454
  65.9 6.2 %collective-permute-start.13 = (bf16[48,1536]{1,0:T(8,128)(2,1)S(1)}, bf16[48,1536]{1,0:T(8,128)(2,1)S(1)}, u32[]{:S(2)}, u32[]{:S(2)}) collective-permute-start(bf16[48,1536]{1,0:T(8,128)(2,1)S(1)} %get-tuple-element.42), channel_id=1, source_target_pairs={{0,8},{8,0},{16,24},{24,16},{1,9},{9,1},{17,25},{25,17},{2,10},{10... | collective-permute-start | bytes 442376 | tf_op jit(solution)/shard_map/ppermute | solution.py:454
  67.7 8.2 %collective-permute-start.14 = (bf16[48,1536]{1,0:T(8,128)(2,1)S(1)}, bf16[48,1536]{1,0:T(8,128)(2,1)S(1)}, u32[]{:S(2)}, u32[]{:S(2)}) collective-permute-start(bf16[48,1536]{1,0:T(8,128)(2,1)S(1)} %get-tuple-element.43), channel_id=1, source_target_pairs={{0,16},{8,24},{16,0},{24,8},{1,17},{9,25},{17,1},{25,9},{2,18},{10... | collective-permute-start | bytes 442376 | tf_op jit(solution)/shard_map/ppermute | solution.py:454
  69.3 6.6 %collective-permute-start.15 = (bf16[48,1536]{1,0:T(8,128)(2,1)S(1)}, bf16[48,1536]{1,0:T(8,128)(2,1)S(1)}, u32[]{:S(2)}, u32[]{:S(2)}) collective-permute-start(bf16[48,1536]{1,0:T(8,128)(2,1)S(1)} %get-tuple-element.44), channel_id=1, source_target_pairs={{0,24},{8,16},{16,8},{24,0},{1,25},{9,17},{17,9},{25,1},{2,26},{10... | collective-permute-start | bytes 442376 | tf_op jit(solution)/shard_map/ppermute | solution.py:454
